TPU v7x, 32 devices: a whole 2x2x4 slice. The times are simulated.
32 devices in a mesh: dp: 16 (over z, y, core), shard: 2 (over x).
Axes of the slice: x: 2, y: 2, z: 4, core: 2. Of those that a mesh axis runs over, the one named last changes fastest.
Arguments:
- hidden: bfloat16 [32, 4096, 256], P('shard', 'dp'), may hold values from -6 to 6
- cotangent: bfloat16 [32, 4096, 256], P('shard', 'dp'), may hold values from -6 to 6
- assign: int32 [32], replicated, may hold values from 0 to 15, as said below
- live_blocks: int32 [32], replicated, may hold values from 16 to 64, as said below
- tail_live: int32 [32, 64], replicated, may hold values from 0 to 1, as said below
- random_blocks: int32 [32, 4, 64, 3], P(('dp', 'shard')), may hold values from 2 to 63, as said below
- w_qkv: bfloat16 [256, 768], P('shard'), may hold values from -0.375 to 0.375
- w_out: bfloat16 [256, 256], P('shard'), may hold values from -3 to 3
- w_up: bfloat16 [256, 1024], P('shard'), may hold values from -0.375 to 0.375
- w_down: bfloat16 [1024, 256], P('shard'), may hold values from -0.1875 to 0.1875
- up_bias: bfloat16 [1024], P('shard'), may hold values from -2 to 2
- vectors: bfloat16 [8, 256], P('shard')
- state_qkv: float32 [3, 256, 768], P(None, 'shard')
- state_out: float32 [3, 256, 256], P(None, 'shard')
- state_up: float32 [3, 256, 1024], P(None, 'shard')
- state_down: float32 [3, 1024, 256], P(None, 'shard')
- state_ubias: float32 [3, 1024], P(None, 'shard')
- state_vec: float32 [3, 8, 256], P(None, 'shard')
Outputs:
- layer_out: bfloat16 [32, 4096, 256], P('shard', 'dp')
- input_grad: bfloat16 [32, 4096, 256], P('shard', 'dp')
- grad_qkv: float32 [256, 768], P('shard')
- grad_out: float32 [256, 256], P('shard')
- grad_up: float32 [256, 1024], P('shard')
- grad_down: float32 [1024, 256], P('shard')
- grad_ubias: float32 [1024], P('shard')
- grad_vec: float32 [8, 256], P('shard')
- new_masters: float32 [2, 394752], P('shard')
- new_firsts: float32 [2, 394752], P('shard')
- new_seconds: float32 [2, 394752], P('shard')
Inputs may be any that keep to these rules, and one draw needn't show every extreme that they name: `assign`: among the slots g with (g) % 2 equal to one value, every number 0 to 15 appears once. `live_blocks`: among each shard row's 16 sequences one has 64 live blocks. `tail_live`: position 0 of each row is 1. `random_blocks`: for query block i the 3 entries of one slot and head are distinct, and none is 0, 1, i - 1, i or i + 1.
All inputs are finite; a program needn't handle non-finite values.
Results may differ from a plain program's by a relative error of at most 0.014.
Values may be sent and summed in bfloat16 or wider, within the bound.
No kernel may reach another device: no remote copies, remote signals or barrier semaphores. Data moves between devices by JAX's collectives and lax.ppermute only.
A program may use at most 256 MiB of HBM per device.

v0:
```python
import jax
import jax.numpy as jnp
from jax import lax
from jax.sharding import PartitionSpec as P

STEP = 1


QUERY_SCALE = 0.125
NORM_EPSILON = 1e-12
LEARNING_RATE = 0.02
WEIGHT_DECAY = 0.01
ADAM_EPSILON = 1e-08
FIRST_BETA = 0.5
SECOND_BETA = 0.5
MASK_VALUE = -1e30
ROOT_HALF = 0.7071067811865476
NORMAL_PEAK = 0.3989422804014327


def for_sending(shard):
    return jax.tree.map(lambda a: a.astype(jnp.bfloat16) if a.dtype == jnp.float32 else a, shard)


def gelu_exact(values):
    return 0.5 * values * (1.0 + jax.scipy.special.erf(values * ROOT_HALF))


def gelu_slope(values):
    cumulative = 0.5 * (1.0 + jax.scipy.special.erf(values * ROOT_HALF))
    return cumulative + values * NORMAL_PEAK * jnp.exp(-0.5 * values * values)


def normalize(summed):
    center = summed - jnp.mean(summed, axis=-1, keepdims=True)
    factor = lax.rsqrt(jnp.mean(center * center, axis=-1, keepdims=True) + NORM_EPSILON)
    return (center * factor, factor)


def normalize_back(grad_normed, normed, factor):
    return factor * (
        grad_normed
        - jnp.mean(grad_normed, axis=-1, keepdims=True)
        - normed * jnp.mean(grad_normed * normed, axis=-1, keepdims=True)
    )


def token_mask(live_count, tail_flags, blocks):
    block_ids = jnp.arange(blocks, dtype=jnp.int32)[:, None]
    tail_open = (tail_flags == 1)[None, :]
    return (block_ids < live_count - 1) | (block_ids == live_count - 1) & tail_open


def tile_tables(first_block, tile_span, random_row, live_grid):
    blocks = live_grid.shape[0]
    head_count = random_row.shape[0]
    block_ids = first_block + jnp.arange(tile_span, dtype=jnp.int32)
    nearby = jnp.stack(
        [
            jnp.maximum(block_ids - 1, 0),
            block_ids,
            jnp.minimum(block_ids + 1, blocks - 1),
            jnp.zeros_like(block_ids),
            jnp.ones_like(block_ids),
        ],
        axis=1,
    )
    drawn_ids = jnp.transpose(
        lax.dynamic_slice_in_dim(random_row, first_block, tile_span, 1), (1, 0, 2)
    )
    key_index = jnp.concatenate(
        [jnp.broadcast_to(nearby[:, None, :], (tile_span, head_count, 5)), drawn_ids], axis=2
    )
    always = jnp.ones_like(block_ids) > 0
    allowed = jnp.stack(
        [
            block_ids >= 3,
            block_ids >= 2,
            (block_ids >= 1) & (block_ids + 1 < blocks),
            always,
            always,
        ],
        axis=1,
    )
    allowed = jnp.concatenate(
        [allowed, jnp.broadcast_to(always[:, None], (tile_span, drawn_ids.shape[2]))], axis=1
    )
    choose = (
        key_index[..., None] == jnp.arange(blocks, dtype=jnp.int32)[None, None, None, :]
    ).astype(jnp.float32)
    key_live = jnp.einsum("thsn,nk->thsk", choose, live_grid.astype(jnp.float32)) > 0.5
    key_mask = allowed[:, None, None, :, None] & key_live[:, :, None, :, :]
    return (choose, key_mask)


def pick_blocks(choose, heads):
    return jnp.einsum(
        "thsn,hnkd->thskd", choose.astype(jnp.bfloat16), heads, preferred_element_type=jnp.float32
    ).astype(jnp.bfloat16)


def place_blocks(choose, terms):
    upper = terms.astype(jnp.bfloat16)
    lower = (terms - upper.astype(jnp.float32)).astype(jnp.bfloat16)
    choose_low = choose.astype(jnp.bfloat16)
    return jnp.einsum(
        "thsn,thskd->hnkd", choose_low, upper, preferred_element_type=jnp.float32
    ) + jnp.einsum("thsn,thskd->hnkd", choose_low, lower, preferred_element_type=jnp.float32)


def split_heads(query_rows, key_rows, value_rows, head_count, blocks):
    length, model_width = query_rows.shape
    head_depth = model_width // head_count
    block_rows = length // blocks
    query_blocks = query_rows.reshape(blocks, block_rows, head_count, head_depth)
    key_heads = jnp.transpose(
        key_rows.reshape(blocks, block_rows, head_count, head_depth), (2, 0, 1, 3)
    )
    value_heads = jnp.transpose(
        value_rows.reshape(blocks, block_rows, head_count, head_depth), (2, 0, 1, 3)
    )
    return (query_blocks, key_heads, value_heads)


def attend_forward(query_rows, key_rows, value_rows, live_grid, live_count, random_row):
    length, model_width = query_rows.shape
    head_count = random_row.shape[0]
    head_depth = model_width // head_count
    blocks = live_grid.shape[0]
    block_rows = length // blocks
    tile_span = 8
    query_blocks, key_heads, value_heads = split_heads(
        query_rows, key_rows, value_rows, head_count, blocks
    )
    tile_count = (live_count + tile_span - 1) // tile_span

    def one_tile(tile_index, state_pair):
        context_rows, logsum_rows = state_pair
        first_block = tile_index * tile_span
        choose, key_mask = tile_tables(first_block, tile_span, random_row, live_grid)
        query_tile = lax.dynamic_slice_in_dim(query_blocks, first_block, tile_span, 0)
        scores = (
            jnp.einsum(
                "tqhd,thskd->thqsk",
                query_tile,
                pick_blocks(choose, key_heads),
                preferred_element_type=jnp.float32,
            )
            * QUERY_SCALE
        )
        scores = jnp.where(key_mask, scores, MASK_VALUE)
        row_peak = jnp.max(scores, axis=(3, 4), keepdims=True)
        raised = jnp.exp(scores - row_peak)
        totals = jnp.sum(raised, axis=(3, 4), keepdims=True)
        prob_low = (raised / totals).astype(jnp.bfloat16)
        context = jnp.einsum(
            "thqsk,thskd->tqhd",
            prob_low,
            pick_blocks(choose, value_heads),
            preferred_element_type=jnp.float32,
        )
        context_rows = lax.dynamic_update_slice_in_dim(
            context_rows,
            context.reshape(tile_span * block_rows, model_width),
            first_block * block_rows,
            0,
        )
        logsum = (row_peak + jnp.log(totals))[:, :, :, 0, 0]
        logsum_rows = lax.dynamic_update_slice_in_dim(logsum_rows, logsum, first_block, 0)
        return (context_rows, logsum_rows)

    context_rows, logsum_rows = lax.fori_loop(
        0,
        tile_count,
        one_tile,
        (
            jnp.zeros((length, model_width), jnp.float32),
            jnp.zeros((blocks, head_count, block_rows), jnp.float32),
        ),
    )
    glob_rows = 2 * block_rows
    glob_query = query_rows[:glob_rows].reshape(glob_rows, head_count, head_depth)
    scores = (
        jnp.einsum(
            "qhd,khd->hqk",
            glob_query,
            key_rows.reshape(length, head_count, head_depth),
            preferred_element_type=jnp.float32,
        )
        * QUERY_SCALE
    )
    key_open = live_grid.reshape(length)[None, None, :]
    scores = jnp.where(key_open, scores, MASK_VALUE)
    row_peak = jnp.max(scores, axis=2, keepdims=True)
    raised = jnp.exp(scores - row_peak)
    totals = jnp.sum(raised, axis=2, keepdims=True)
    prob_low = (raised / totals).astype(jnp.bfloat16)
    glob_context = jnp.einsum(
        "hqk,khd->qhd",
        prob_low,
        value_rows.reshape(length, head_count, head_depth),
        preferred_element_type=jnp.float32,
    ).reshape(glob_rows, model_width)
    context_rows = lax.dynamic_update_slice_in_dim(context_rows, glob_context, 0, 0)
    glob_logsum = (row_peak + jnp.log(totals))[:, :, 0]
    return (context_rows, logsum_rows, glob_logsum)


def attend_backward(
    query_rows,
    key_rows,
    value_rows,
    grad_context,
    logsum_rows,
    glob_logsum,
    live_grid,
    live_count,
    random_row,
):
    length, model_width = query_rows.shape
    head_count = random_row.shape[0]
    head_depth = model_width // head_count
    blocks = live_grid.shape[0]
    block_rows = length // blocks
    tile_span = 8
    glob_rows = 2 * block_rows
    query_blocks, key_heads, value_heads = split_heads(
        query_rows, key_rows, value_rows, head_count, blocks
    )
    tile_count = (live_count + tile_span - 1) // tile_span
    row_ids = jnp.arange(length, dtype=jnp.int32)[:, None]
    grad_sparse = jnp.where(row_ids >= glob_rows, grad_context, jnp.zeros_like(grad_context))
    grad_blocks = grad_sparse.reshape(blocks, block_rows, head_count, head_depth)

    def one_tile(tile_index, grad_state):
        grad_query, grad_keys, grad_values = grad_state
        first_block = tile_index * tile_span
        choose, key_mask = tile_tables(first_block, tile_span, random_row, live_grid)
        query_tile = lax.dynamic_slice_in_dim(query_blocks, first_block, tile_span, 0)
        grad_tile = lax.dynamic_slice_in_dim(grad_blocks, first_block, tile_span, 0)
        logsum_tile = lax.dynamic_slice_in_dim(logsum_rows, first_block, tile_span, 0)
        keys_picked = pick_blocks(choose, key_heads)
        values_picked = pick_blocks(choose, value_heads)
        scores = (
            jnp.einsum(
                "tqhd,thskd->thqsk", query_tile, keys_picked, preferred_element_type=jnp.float32
            )
            * QUERY_SCALE
        )
        probs = jnp.where(key_mask, jnp.exp(scores - logsum_tile[:, :, :, None, None]), 0.0)
        prob_low = probs.astype(jnp.bfloat16)
        grad_value_tile = jnp.einsum(
            "thqsk,tqhd->thskd", prob_low, grad_tile, preferred_element_type=jnp.float32
        )
        grad_prob = jnp.einsum(
            "tqhd,thskd->thqsk", grad_tile, values_picked, preferred_element_type=jnp.float32
        )
        inner = jnp.sum(probs * grad_prob, axis=(3, 4), keepdims=True)
        grad_score = (probs * (grad_prob - inner)).astype(jnp.bfloat16)
        grad_query_tile = (
            jnp.einsum(
                "thqsk,thskd->tqhd", grad_score, keys_picked, preferred_element_type=jnp.float32
            )
            * QUERY_SCALE
        )
        grad_key_tile = (
            jnp.einsum(
                "thqsk,tqhd->thskd", grad_score, query_tile, preferred_element_type=jnp.float32
            )
            * QUERY_SCALE
        )
        grad_query = lax.dynamic_update_slice_in_dim(grad_query, grad_query_tile, first_block, 0)
        grad_keys = grad_keys + place_blocks(choose, grad_key_tile)
        grad_values = grad_values + place_blocks(choose, grad_value_tile)
        return (grad_query, grad_keys, grad_values)

    grad_query, grad_keys, grad_values = lax.fori_loop(
        0,
        tile_count,
        one_tile,
        (
            jnp.zeros(query_blocks.shape, jnp.float32),
            jnp.zeros(key_heads.shape, jnp.float32),
            jnp.zeros(value_heads.shape, jnp.float32),
        ),
    )
    glob_query = query_rows[:glob_rows].reshape(glob_rows, head_count, head_depth)
    glob_grad = grad_context[:glob_rows].reshape(glob_rows, head_count, head_depth)
    key_flat = key_rows.reshape(length, head_count, head_depth)
    value_flat = value_rows.reshape(length, head_count, head_depth)
    scores = (
        jnp.einsum("qhd,khd->hqk", glob_query, key_flat, preferred_element_type=jnp.float32)
        * QUERY_SCALE
    )
    key_open = live_grid.reshape(length)[None, None, :]
    probs = jnp.where(key_open, jnp.exp(scores - glob_logsum[:, :, None]), 0.0)
    prob_low = probs.astype(jnp.bfloat16)
    grad_value_glob = jnp.einsum(
        "hqk,qhd->khd", prob_low, glob_grad, preferred_element_type=jnp.float32
    )
    grad_prob = jnp.einsum(
        "qhd,khd->hqk", glob_grad, value_flat, preferred_element_type=jnp.float32
    )
    inner = jnp.sum(probs * grad_prob, axis=2, keepdims=True)
    grad_score = (probs * (grad_prob - inner)).astype(jnp.bfloat16)
    grad_query_glob = (
        jnp.einsum("hqk,khd->qhd", grad_score, key_flat, preferred_element_type=jnp.float32)
        * QUERY_SCALE
    )
    grad_key_glob = (
        jnp.einsum("hqk,qhd->khd", grad_score, glob_query, preferred_element_type=jnp.float32)
        * QUERY_SCALE
    )
    grad_query_rows = grad_query.reshape(length, model_width) + jnp.pad(
        grad_query_glob.reshape(glob_rows, model_width), ((0, length - glob_rows), (0, 0))
    )
    grad_key_rows = jnp.transpose(grad_keys, (1, 2, 0, 3)).reshape(
        length, model_width
    ) + grad_key_glob.reshape(length, model_width)
    grad_value_rows = jnp.transpose(grad_values, (1, 2, 0, 3)).reshape(
        length, model_width
    ) + grad_value_glob.reshape(length, model_width)
    return (grad_query_rows, grad_key_rows, grad_value_rows)


def forward_sequence(weights, tokens, live_count, tail_flags, random_row):
    qkv_weight, out_weight, up_weight, down_weight, up_shift, vector_rows = weights
    vector_f32 = vector_rows.astype(jnp.float32)
    length, model_width = tokens.shape
    blocks = random_row.shape[1]
    live_grid = token_mask(live_count, tail_flags, blocks)
    live_rows = live_grid.reshape(length, 1).astype(jnp.float32)
    shift_qkv = jnp.concatenate([vector_f32[0], jnp.zeros_like(vector_f32[0]), vector_f32[1]])
    qkv_low = (jnp.dot(tokens, qkv_weight, preferred_element_type=jnp.float32) + shift_qkv).astype(
        jnp.bfloat16
    )
    context, logsum_rows, glob_logsum = attend_forward(
        qkv_low[:, :model_width],
        qkv_low[:, model_width : 2 * model_width],
        qkv_low[:, 2 * model_width :],
        live_grid,
        live_count,
        random_row,
    )
    context_low = context.astype(jnp.bfloat16)
    attended = jnp.dot(context_low, out_weight, preferred_element_type=jnp.float32) + vector_f32[2]
    normed_one, factor_one = normalize(tokens.astype(jnp.float32) + attended)
    first_out = normed_one * vector_f32[3] + vector_f32[4]
    first_low = first_out.astype(jnp.bfloat16)
    hidden_pre = jnp.dot(
        first_low, up_weight, preferred_element_type=jnp.float32
    ) + up_shift.astype(jnp.float32)
    activated = gelu_exact(hidden_pre).astype(jnp.bfloat16)
    branch = jnp.dot(activated, down_weight, preferred_element_type=jnp.float32) + vector_f32[5]
    normed_two, factor_two = normalize(first_out + branch)
    result = ((normed_two * vector_f32[6] + vector_f32[7]) * live_rows).astype(jnp.bfloat16)
    kept = (
        qkv_low,
        logsum_rows,
        glob_logsum,
        context_low,
        normed_one,
        factor_one,
        first_low,
        hidden_pre,
        normed_two,
        factor_two,
    )
    return (result, kept)


def backward_sequence(weights, tokens, cotangent_rows, live_count, tail_flags, random_row, kept):
    qkv_weight, out_weight, up_weight, down_weight, up_shift, vector_rows = weights
    (
        qkv_low,
        logsum_rows,
        glob_logsum,
        context_low,
        normed_one,
        factor_one,
        first_low,
        hidden_pre,
        normed_two,
        factor_two,
    ) = kept
    vector_f32 = vector_rows.astype(jnp.float32)
    length, model_width = tokens.shape
    blocks = random_row.shape[1]
    live_grid = token_mask(live_count, tail_flags, blocks)
    live_rows = live_grid.reshape(length, 1).astype(jnp.float32)
    grad_y = cotangent_rows.astype(jnp.float32) * live_rows
    grad_gain_two = jnp.sum(grad_y * normed_two, axis=0)
    grad_shift_two = jnp.sum(grad_y, axis=0)
    grad_z2 = normalize_back(grad_y * vector_f32[6], normed_two, factor_two)
    grad_branch = grad_z2.astype(jnp.bfloat16)
    activated = gelu_exact(hidden_pre).astype(jnp.bfloat16)
    grad_down = jnp.einsum("nf,nd->fd", activated, grad_branch, preferred_element_type=jnp.float32)
    grad_down_shift = jnp.sum(grad_branch, axis=0, dtype=jnp.float32)
    grad_act = jnp.einsum("nd,fd->nf", grad_branch, down_weight, preferred_element_type=jnp.float32)
    grad_pre = (grad_act * gelu_slope(hidden_pre)).astype(jnp.bfloat16)
    grad_up = jnp.einsum("nd,nf->df", first_low, grad_pre, preferred_element_type=jnp.float32)
    grad_up_shift = jnp.sum(grad_pre, axis=0, dtype=jnp.float32)
    grad_first = grad_z2 + jnp.einsum(
        "nf,df->nd", grad_pre, up_weight, preferred_element_type=jnp.float32
    )
    grad_gain_one = jnp.sum(grad_first * normed_one, axis=0)
    grad_shift_one = jnp.sum(grad_first, axis=0)
    grad_z1 = normalize_back(grad_first * vector_f32[3], normed_one, factor_one)
    grad_attended = grad_z1.astype(jnp.bfloat16)
    grad_out = jnp.einsum(
        "nd,ne->de", context_low, grad_attended, preferred_element_type=jnp.float32
    )
    grad_out_shift = jnp.sum(grad_attended, axis=0, dtype=jnp.float32)
    grad_context = jnp.einsum(
        "ne,de->nd", grad_attended, out_weight, preferred_element_type=jnp.float32
    ).astype(jnp.bfloat16)
    grad_query, grad_keys, grad_values = attend_backward(
        qkv_low[:, :model_width],
        qkv_low[:, model_width : 2 * model_width],
        qkv_low[:, 2 * model_width :],
        grad_context,
        logsum_rows,
        glob_logsum,
        live_grid,
        live_count,
        random_row,
    )
    grad_qkv_low = jnp.concatenate([grad_query, grad_keys, grad_values], axis=1).astype(
        jnp.bfloat16
    )
    grad_qkv = jnp.einsum("nd,ne->de", tokens, grad_qkv_low, preferred_element_type=jnp.float32)
    grad_query_shift = jnp.sum(grad_qkv_low[:, :model_width], axis=0, dtype=jnp.float32)
    grad_value_shift = jnp.sum(grad_qkv_low[:, 2 * model_width :], axis=0, dtype=jnp.float32)
    grad_tokens = grad_z1 + jnp.einsum(
        "ne,de->nd", grad_qkv_low, qkv_weight, preferred_element_type=jnp.float32
    )
    grad_vectors = jnp.stack(
        [
            grad_query_shift,
            grad_value_shift,
            grad_out_shift,
            grad_gain_one,
            grad_shift_one,
            grad_down_shift,
            grad_gain_two,
            grad_shift_two,
        ]
    )
    return (
        grad_tokens.astype(jnp.bfloat16),
        (grad_qkv, grad_out, grad_up, grad_down, grad_up_shift, grad_vectors),
    )


def adam_update(grad, state, decay, correct_one, correct_two):
    first_new = FIRST_BETA * state[1] + (1.0 - FIRST_BETA) * grad
    second_new = SECOND_BETA * state[2] + (1.0 - SECOND_BETA) * grad * grad
    direction = first_new / correct_one / (jnp.sqrt(second_new / correct_two) + ADAM_EPSILON)
    master_new = state[0] - LEARNING_RATE * (direction + decay * state[0])
    return (master_new, first_new, second_new)


def flat_row(pieces):
    return jnp.concatenate([piece.reshape(1, -1) for piece in pieces], axis=1)


def on_device(
    hidden,
    cotangent,
    assign,
    live_blocks,
    tail_live,
    random_blocks,
    w_qkv,
    w_out,
    w_up,
    w_down,
    up_bias,
    vectors,
    state_qkv,
    state_out,
    state_up,
    state_down,
    state_ubias,
    state_vec,
):
    weights = (
        lax.all_gather(w_qkv, "shard", axis=0, tiled=True),
        lax.all_gather(w_out, "shard", axis=0, tiled=True),
        lax.all_gather(w_up, "shard", axis=0, tiled=True),
        lax.all_gather(w_down, "shard", axis=0, tiled=True),
        lax.all_gather(up_bias, "shard", axis=0, tiled=True),
        lax.all_gather(vectors, "shard", axis=0, tiled=True),
    )
    shard_count = lax.axis_size("shard")
    data_count = lax.axis_size("dp")
    shard_index = lax.axis_index("shard")
    data_index = lax.axis_index("dp")
    row_seqs = hidden.shape[0]
    per_device = random_blocks.shape[0]
    slot_table = assign.reshape(data_count, shard_count, per_device)
    row_assign = lax.dynamic_index_in_dim(slot_table, shard_index, 1, keepdims=False).reshape(
        row_seqs
    )
    send_hidden = jnp.take(hidden, row_assign, axis=0)
    send_cotangent = jnp.take(cotangent, row_assign, axis=0)
    own_hidden, own_cotangent = (
        lax.all_to_all(send_hidden, "dp", split_axis=0, concat_axis=1, tiled=True),
        lax.all_to_all(send_cotangent, "dp", split_axis=0, concat_axis=1, tiled=True),
    )
    own_local = lax.dynamic_slice_in_dim(row_assign, data_index * per_device, per_device)
    own_global = shard_index * row_seqs + own_local
    own_counts = jnp.take(live_blocks, own_global)
    own_tails = jnp.take(tail_live, own_global, axis=0)

    def forward_step(unused, inputs):
        return (unused, forward_sequence(weights, *inputs))

    unused_carry, (outputs, kept_all) = lax.scan(
        forward_step, 0, (own_hidden, own_counts, own_tails, random_blocks)
    )

    def backward_step(grad_sums, inputs):
        grad_tokens, grads = backward_sequence(weights, *inputs)
        return (tuple((summed + added for summed, added in zip(grad_sums, grads))), grad_tokens)

    empty_grads = tuple((jnp.zeros(weight.shape, jnp.float32) for weight in weights))
    grad_sums, grad_tokens = lax.scan(
        backward_step,
        empty_grads,
        (own_hidden, own_cotangent, own_counts, own_tails, random_blocks, kept_all),
    )
    back_out, back_grad = (
        lax.all_to_all(outputs, "dp", split_axis=1, concat_axis=0, tiled=True),
        lax.all_to_all(grad_tokens, "dp", split_axis=1, concat_axis=0, tiled=True),
    )
    halves = jax.tree.map(
        lambda part: part.astype(jnp.float32),
        lax.psum_scatter(for_sending(grad_sums), "shard", scatter_dimension=0, tiled=True),
    )
    grad_totals = lax.psum(halves, "dp")
    correct_one = 1.0 - FIRST_BETA**STEP
    correct_two = 1.0 - SECOND_BETA**STEP
    states = (state_qkv, state_out, state_up, state_down, state_ubias, state_vec)
    decays = (WEIGHT_DECAY, WEIGHT_DECAY, WEIGHT_DECAY, WEIGHT_DECAY, 0.0, 0.0)
    updated = [
        adam_update(grad, state, decay, correct_one, correct_two)
        for grad, state, decay in zip(grad_totals, states, decays)
    ]
    new_masters = flat_row([entry[0] for entry in updated])
    new_firsts = flat_row([entry[1] for entry in updated])
    new_seconds = flat_row([entry[2] for entry in updated])
    inverse = (
        jnp.zeros((row_seqs,), jnp.int32).at[row_assign].set(jnp.arange(row_seqs, dtype=jnp.int32))
    )
    layer_out = jnp.take(back_out, inverse, axis=0)
    input_grad = jnp.take(back_grad, inverse, axis=0)
    return (layer_out, input_grad) + tuple(grad_totals) + (new_masters, new_firsts, new_seconds)


def solution(mesh):
    placed = (
        P("shard", "dp", None),
        P("shard", "dp", None),
        P(),
        P(),
        P(),
        P(("dp", "shard"), None, None, None),
        P("shard", None),
        P("shard", None),
        P("shard", None),
        P("shard", None),
        P("shard"),
        P("shard", None),
        P(None, "shard", None),
        P(None, "shard", None),
        P(None, "shard", None),
        P(None, "shard", None),
        P(None, "shard"),
        P(None, "shard", None),
    )
    return jax.shard_map(
        on_device,
        mesh=mesh,
        in_specs=placed,
        out_specs=(
            P("shard", "dp", None),
            P("shard", "dp", None),
            P("shard", None),
            P("shard", None),
            P("shard", None),
            P("shard", None),
            P("shard"),
            P("shard", None),
            P("shard", None),
            P("shard", None),
            P("shard", None),
        ),
        check_vma=False,
    )
```

profile of v0, /device:TPU:0, one launch (start us, length us, event | category | flops | bytes accessed | tf_op | source)
XLA Modules:
  0.0 1323.0 jit_solution(3012729582737985020)
XLA Ops:
  18.6 7.5 all-to-all-start
  28.7 38.6 %all-to-all-done = bf16[16,256,256]{2,1,0:T(8,128)(2,1)S(1)} async-done(((bf16[16,256,256]{2,1,0:T(8,128)(2,1)}), bf16[16,256,256]{2,1,0:T(8,128)(2,1)S(1)}, u32[]{:S(2)}, u32[]{:S(2)}) %all-to-all-start) | async-done | bytes 2097184 | tf_op jit(solution)/shard_map/all_to_all | solution.py:508
  67.3 11.3 all-to-all-start.2
  105.7 7.8 all_gather.21
  158.5 7.6 copy.136
  180.6 92.6 %while.43 = (s32[]{:T(128)}, bf16[4096,256]{0,1:T(8,128)(2,1)}, f32[64,4,64]{2,1,0:T(4,128)S(1)}, s32[]{:T(128)}, s32[4,64,3]{1,0,2:T(4,128)S(1)}, /*index=5*/bf...) while((s32[]{:T(128)}, bf16[4096,256]{0,1:T(8,128)(2,1)}, ...), condition=%wide.region_3.5_spmd.clone, body=%wide.region_0.4_spmd.clone.sunk | while | flops 553802112 | bytes 36078092 | solution.py:172
  284.8 9.7 multiply_convert_fusion.2
  309.2 17.0 %fusion.204 = (bf16[1024]{0:T(1024)(128)(2,1)}, bf16[4096,1024]{1,0:T(8,128)(2,1)}) fusion(f32[4096,1024]{1,0:T(8,128)} %get-tuple-element.757, f32[1024]{0:T(1024)S(1)} %bitcast.565, bf16[1024,256]{1,0:T(8,128)(2,1)S(1)} %copy-done.35, f32[4096,256]{0,1:T(8,128)S(1)} %get-tuple-element.695), kind=kOutput, calls=%fused_computation.336 | convolution fusion | flops 2198862848 | bytes 29890560 | tf_op jit(solution)/shard_map/while/body/eval_jaxpr/nd,fd->nf/dot_general | solution.py:399
  326.3 15.1 %multiply_reduce_fusion.3 = (bf16[256]{0:T(256)(128)(2,1)}, f32[4096]{0:T(1024)S(1)}, f32[4096]{0:T(1024)S(1)}, bf16[256]{0:T(256)(128)(2,1)}, f32[4096,256]{0,1:T(8,128)S(1)}) fusion(f32[4096,256]{0,1:T(8,128)S(1)} %get-tuple-element.755, f32[4096]{0:T(1024)S(1)} %add_rsqrt_fusion.1, f32[4096]{0:T(1024)S(1)} %broadcast_multiply_fusion.4, ...), kind=kOutput, calls=%fused_computation.171 | convolution fusion | flops 2157960704 | bytes 21563392 | tf_op jit(solution)/shard_map/while/body/eval_jaxpr/nf,df->nd/dot_general | solution.py:403
  389.1 259.9 %while.44 = (s32[]{:T(128)}, f32[64,64,4,64]{1,0,3,2:T(8,128)}, f32[4,64,64,64]{3,1,2,0:T(8,128)}, f32[4,64,64,64]{3,1,2,0:T(8,128)}, s32[]{:T(128)}, /*index=5*...) while((s32[]{:T(128)}, f32[64,64,4,64]{1,0,3,2:T(8,128)}, ...), condition=%wide.region_17.19_spmd.clone, body=%wide.region_15.18_spmd.clone.sunk | while | flops 1510414720 | bytes 114002984 | solution.py:277
  429.4 8.7 fusion.320
  443.7 8.6 fusion.318
  494.3 8.7 fusion.320
  508.7 8.6 fusion.318
  559.3 8.7 fusion.320
  573.6 8.6 fusion.318
  624.2 8.7 fusion.320
  638.5 8.6 fusion.318
  649.0 9.1 copy.147
  658.0 7.9 reshape.555
  665.9 7.9 reshape.550
  673.8 9.0 copy.146
  682.8 8.0 reshape.553
  706.0 7.8 convolution_convert_fusion.1
  714.2 8.0 convolution_convert_fusion.2
  730.1 21.6 %reduce.20 = bf16[4096,256]{1,0:T(8,128)(2,1)S(1)} reduce(bf16[4096,1,256]{2,1,0:T(2,128)(2,1)} %bitcast.512, bf16[]{:T(256)} %broadcast.1075), dimensions={1}, to_apply=%bitcast.387.reduce_sub_computation | reduce | bytes 4194306
  753.8 357.4 %all-to-all-start.1 = ((bf16[16,2,32768]{2,1,0:T(2,128)(2,1)}), bf16[16,2,32768]{2,1,0:T(2,128)(2,1)S(1)}, u32[]{:S(2)}, u32[]{:S(2)}) async-start(bf16[16,2,32768]{2,1,0:T(2,128)(2,1)} %reshape.706), calls=%async_computation.1 | async-start | bytes 4194304 | tf_op jit(solution)/shard_map/all_to_all | solution.py:534
  1117.3 10.0 copy.149
  1127.3 22.9 %reduce.19 = bf16[4096,256]{1,0:T(8,128)(2,1)} reduce(bf16[4096,1,256]{2,1,0:T(2,128)(2,1)} %bitcast.513, bf16[]{:T(256)} %broadcast.1075), dimensions={1}, to_apply=%bitcast.389.reduce_sub_computation | reduce | bytes 4194306
  1159.4 75.2 %all-reduce.6 = (f32[128,768]{1,0:T(8,128)}, f32[128,256]{1,0:T(8,128)S(1)}, f32[128,1024]{1,0:T(8,128)}, f32[512,256]{1,0:T(8,128)}, f32[512]{0:T(512)S(1)}, /*index=5*/f32[4,256]{1,0:T(4,128)S(1)}) all-reduce(bf16[128,768]{1,0:T(8,128)(2,1)} %reduce-scatter.5.cloned.1.call-done, ...), channel_id=1, replica_groups=mesh['dp'=16,'shard'=2] {'dp'}, use_global_device_ids=true, to_apply=%region_20.22 | all-reduce | flops 394752 | bytes 2371584 | tf_op jit(solution)/shard_map/psum | solution.py:541
  1264.0 27.3 %all-to-all-done.3 = bf16[16,2,32768]{2,1,0:T(2,128)(2,1)} async-done(((bf16[16,2,32768]{2,1,0:T(2,128)(2,1)}), bf16[16,2,32768]{2,1,0:T(2,128)(2,1)}, u32[]{:S(2)}, u32[]{:S(2)}) %all-to-all-start.3) | async-done | bytes 2097184 | tf_op jit(solution)/shard_map/all_to_all | solution.py:535
  1291.3 10.5 reshape.709
  (585 shorter events, 537.4 us)
Async XLA Ops:
  18.6 60.7 %copy-start.85 = (u32[32]{0:T(128)S(1)}, u32[32]{0:T(128)}, u32[]{:S(2)}) copy-start(u32[32]{0:T(128)} %constant.483) | copy-start | bytes 388
  18.6 62.6 %copy-start.73 = (bf16[512]{0:T(512)(128)(2,1)S(1)}, bf16[512]{0:T(512)(128)(2,1)}, u32[]{:S(2)}) copy-start(bf16[512]{0:T(512)(128)(2,1)} %param.34) | copy-start | bytes 3076
  18.6 67.6 %copy-start.70 = (bf16[4,256]{1,0:T(4,128)(2,1)S(1)}, bf16[4,256]{1,0:T(4,128)(2,1)}, u32[]{:S(2)}) copy-start(bf16[4,256]{1,0:T(4,128)(2,1)} %param.35) | copy-start | bytes 6148
  18.6 72.6 %copy-start.43 = (s32[1,4,64,3]{2,1,3,0:T(4,128)S(1)}, s32[1,4,64,3]{2,1,3,0:T(4,128)}, u32[]{:S(2)}) copy-start(s32[1,4,64,3]{2,1,3,0:T(4,128)} %param.29) | copy-start | bytes 9220
  18.6 74.4 %copy-start.55 = (bf16[128,256]{1,0:T(8,128)(2,1)S(1)}, bf16[128,256]{1,0:T(8,128)(2,1)}, u32[]{:S(2)}) copy-start(bf16[128,256]{1,0:T(8,128)(2,1)} %param.31) | copy-start | bytes 196612
  18.6 79.5 %copy-start.44 = (bf16[128,768]{1,0:T(8,128)(2,1)S(1)}, bf16[128,768]{1,0:T(8,128)(2,1)}, u32[]{:S(2)}) copy-start(bf16[128,768]{1,0:T(8,128)(2,1)} %param.30) | copy-start | bytes 589828
  18.6 87.0 %copy-start.41 = (bf16[128,1024]{1,0:T(8,128)(2,1)S(1)}, bf16[128,1024]{1,0:T(8,128)(2,1)}, u32[]{:S(2)}) copy-start(bf16[128,1024]{1,0:T(8,128)(2,1)} %param.32) | copy-start | bytes 786436
  18.6 94.8 %copy-start.42 = (bf16[512,256]{1,0:T(8,128)(2,1)S(1)}, bf16[512,256]{1,0:T(8,128)(2,1)}, u32[]{:S(2)}) copy-start(bf16[512,256]{1,0:T(8,128)(2,1)} %param.33) | copy-start | bytes 786436
  18.6 48.6 %all-to-all-start = ((bf16[16,256,256]{2,1,0:T(8,128)(2,1)}), bf16[16,256,256]{2,1,0:T(8,128)(2,1)S(1)}, u32[]{:S(2)}, u32[]{:S(2)}) async-start(bf16[16,256,256]{2,1,0:T(8,128)(2,1)} %get-tuple-element.751), calls=%async_computation | async-start | bytes 4194304 | tf_op jit(solution)/shard_map/all_to_all | solution.py:508
  26.2 95.0 %copy-start.64 = (f32[3,512]{1,0:T(4,128)S(1)}, f32[3,512]{1,0:T(4,128)}, u32[]{:S(2)}) copy-start(f32[3,512]{1,0:T(4,128)} %param.40) | copy-start | bytes 18436
  67.3 57.5 %copy-start.17 = (bf16[16,256,256]{2,1,0:T(8,128)(2,1)}, bf16[16,256,256]{2,1,0:T(8,128)(2,1)S(1)}, u32[]{:S(2)}) copy-start(bf16[16,256,256]{2,1,0:T(8,128)(2,1)S(1)} %all-to-all-done) | copy-start | bytes 6291460
  67.3 62.8 %all-to-all-start.2 = ((bf16[16,256,256]{2,1,0:T(8,128)(2,1)}), bf16[16,256,256]{2,1,0:T(8,128)(2,1)}, u32[]{:S(2)}, u32[]{:S(2)}) async-start(bf16[16,256,256]{2,1,0:T(8,128)(2,1)} %get-tuple-element.750), calls=%async_computation.2 | async-start | bytes 4194304 | tf_op jit(solution)/shard_map/all_to_all | solution.py:509
  78.6 1080.8 %reduce-scatter.7.cloned.1.call-start = ((), (), s32[]{:S(2)}) async-start(), calls=%async_computation.9 | async-start | bytes 196608 | tf_op jit(solution)/shard_map/reduce_scatter | solution.py:539
  93.1 33.6 %copy-start.86 = (s32[16]{0:T(128)}, s32[16]{0:T(128)S(1)}, u32[]{:S(2)}) copy-start(s32[16]{0:T(128)S(1)} %scatter_custom_fusion) | copy-start | bytes 196
  104.5 22.2 %copy-start.36 = (bf16[256,768]{1,0:T(8,128)(2,1)}, bf16[256,768]{1,0:T(8,128)(2,1)S(1)}, u32[]{:S(2)}) copy-start(bf16[256,768]{1,0:T(8,128)(2,1)S(1)} %all_gather.18) | copy-start | bytes 1179652
  105.7 24.5 %copy-start.56 = (f32[1,256]{1,0:T(1,128)}, f32[1,256]{1,0:T(1,128)S(1)}, u32[]{:S(2)}) copy-start(f32[1,256]{1,0:T(1,128)S(1)} %get-tuple-element.740) | copy-start | bytes 3076
  130.1 22.8 %copy-start.6 = (bf16[4096,256]{0,1:T(8,128)(2,1)}, bf16[4096,256]{0,1:T(8,128)(2,1)S(1)}, u32[]{:S(2)}) copy-start(bf16[4096,256]{0,1:T(8,128)(2,1)S(1)} %get-tuple-element.718) | copy-start | bytes 6291460
  180.6 92.6 %copy-start.30 = (bf16[128,256]{0,1:T(8,128)(2,1)S(1)}, bf16[128,256]{0,1:T(8,128)(2,1)}, u32[]{:S(2)}) copy-start(bf16[128,256]{0,1:T(8,128)(2,1)} %slice.192) | copy-start | bytes 196612
  180.6 92.6 %copy-start.40 = (pred[4096]{0:T(1024)(128)(4,1)S(1)}, pred[4096]{0:T(1024)(128)(4,1)}, u32[]{:S(2)}) copy-start(pred[4096]{0:T(1024)(128)(4,1)} %copy-done.39) | copy-start | bytes 12292
  283.3 58.1 %copy-start.5 = (f32[4096,256]{0,1:T(8,128)}, f32[4096,256]{0,1:T(8,128)S(1)}, u32[]{:S(2)}) copy-start(f32[4096,256]{0,1:T(8,128)S(1)} %get-tuple-element.755) | copy-start | bytes 12582916
  283.4 58.1 %copy-start.46 = (f32[4096]{0:T(1024)}, f32[4096]{0:T(1024)S(1)}, u32[]{:S(2)}) copy-start(f32[4096]{0:T(1024)S(1)} %broadcast_multiply_fusion.4) | copy-start | bytes 49156
  283.9 57.6 %copy-start.52 = (f32[4096]{0:T(1024)}, f32[4096]{0:T(1024)S(1)}, u32[]{:S(2)}) copy-start(f32[4096]{0:T(1024)S(1)} %add_rsqrt_fusion.1) | copy-start | bytes 49156
  309.2 17.1 %copy-start.22 = (f32[4096,256]{0,1:T(8,128)}, f32[4096,256]{0,1:T(8,128)S(1)}, u32[]{:S(2)}) copy-start(f32[4096,256]{0,1:T(8,128)S(1)} %get-tuple-element.695) | copy-start | bytes 12582916
  370.0 789.3 %reduce-scatter.5.cloned.1.call-start = ((), (), s32[]{:S(2)}) async-start(), calls=%async_computation.8 | async-start | bytes 589824 | tf_op jit(solution)/shard_map/reduce_scatter | solution.py:539
  706.0 453.4 %reduce-scatter.11.cloned.1.call-start = ((), (), s32[]{:S(2)}) async-start(), calls=%async_computation.11 | async-start | bytes 786432 | tf_op jit(solution)/shard_map/reduce_scatter | solution.py:539
  713.8 445.6 %reduce-scatter.9.cloned.1.call-start = ((), (), s32[]{:S(2)}) async-start(), calls=%async_computation.10 | async-start | bytes 786432 | tf_op jit(solution)/shard_map/reduce_scatter | solution.py:539
  751.7 359.5 %copy-start.37 = (bf16[256,768]{1,0:T(8,128)(2,1)S(1)}, bf16[256,768]{1,0:T(8,128)(2,1)}, u32[]{:S(2)}) copy-start(bf16[256,768]{1,0:T(8,128)(2,1)} %copy-done.36) | copy-start | bytes 1179652
  753.8 492.0 %all-to-all-start.1 = ((bf16[16,2,32768]{2,1,0:T(2,128)(2,1)}), bf16[16,2,32768]{2,1,0:T(2,128)(2,1)S(1)}, u32[]{:S(2)}, u32[]{:S(2)}) async-start(bf16[16,2,32768]{2,1,0:T(2,128)(2,1)} %reshape.706), calls=%async_computation.1 | async-start | bytes 4194304 | tf_op jit(solution)/shard_map/all_to_all | solution.py:534
  1127.3 27.0 %copy-start.71 = (bf16[1024]{0:T(1024)(128)(2,1)S(1)}, bf16[1024]{0:T(1024)(128)(2,1)}, u32[]{:S(2)}) copy-start(bf16[1024]{0:T(1024)(128)(2,1)} %get-tuple-element.765) | copy-start | bytes 6148
  1150.2 86.1 %copy-start.29 = (f32[3,128,768]{2,1,0:T(8,128)S(1)}, f32[3,128,768]{2,1,0:T(8,128)}, u32[]{:S(2)}) copy-start(f32[3,128,768]{2,1,0:T(8,128)} %param.36) | copy-start | bytes 3538948
  1234.6 16.5 %copy-start.72 = (f32[512]{0:T(512)}, f32[512]{0:T(512)S(1)}, u32[]{:S(2)}) copy-start(f32[512]{0:T(512)S(1)} %get-tuple-element.685) | copy-start | bytes 6148
  1245.7 45.5 %all-to-all-start.3 = ((bf16[16,2,32768]{2,1,0:T(2,128)(2,1)}), bf16[16,2,32768]{2,1,0:T(2,128)(2,1)}, u32[]{:S(2)}, u32[]{:S(2)}) async-start(bf16[16,2,32768]{2,1,0:T(2,128)(2,1)} %reshape.708), calls=%async_computation.3 | async-start | bytes 4194304 | tf_op jit(solution)/shard_map/all_to_all | solution.py:535
  (72 other events, 363.6 us)
Sparse Core Ops, SparseCore 0:
  370.2 102.3 reduce-scatter.6
  706.1 364.7 reduce-scatter.4
  1073.8 14.5 reduce-scatter.10
  1091.1 14.5 reduce-scatter.8
where the time goes:
time: 1340 us; the launch traced here: 1320 us
  starting transfers between devices  381 us (28%)
  matrix products  373 us (28%)
  local copies, waits for them, and re-layouts  249 us (19%)
  other arithmetic  119 us (9%)
  blocking collectives  115 us (9%)
  waiting for transfers between devices  66 us (5%)
  between operations  18.3 us (1%)
    all_to_all x1, starting transfers between devices, on_device(): lax.all_to_all(outputs, 'dp', split_axis=1, concat_axis=0, tiled=True)  357 us
    psum x1, blocking collectives, on_device(): grad_totals = lax.psum(halves, 'dp')  75.2 us
    dot_general x8, matrix products, place_blocks(): jnp.einsum('thsn,thskd->hnkd', choose_low, upper, preferred_element_type=...  69.1 us
    unnamed x218, local copies, waits for them, and re-layouts  60.2 us
    dot_general x16, matrix products, pick_blocks(): jnp.einsum('thsn,hnkd->thskd', choose.astype(jnp.bfloat16), heads, prefer...  55.6 us
    unnamed x9, other arithmetic  48 us
    all_to_all x1, waiting for transfers between devices, on_device(): lax.all_to_all(send_hidden, 'dp', split_axis=0, concat_axis=1, tiled=True)  38.6 us
    dot_general x4, matrix products, one_tile(): jnp.einsum('tqhd,thskd->thqsk', grad_tile, values_picked, preferred_eleme...  29.5 us
  transfers between devices with their start and end apart: 8, of which 2 were waited for; matrix products, arithmetic and copies ran while one was open for 35% of the time, Pallas kernels for 0%

commit v1 on v0

v1 whole, which is shorter than its diff:
```python
import functools

import jax
import jax.numpy as jnp
from jax import lax
from jax.experimental import pallas as pl
from jax.experimental.pallas import tpu as pltpu
from jax.sharding import PartitionSpec as P

STEP = 1
QUERY_SCALE = 0.125
NORM_EPSILON = 1e-12
LEARNING_RATE = 0.02
WEIGHT_DECAY = 0.01
ADAM_EPSILON = 1e-08
FIRST_BETA = 0.5
SECOND_BETA = 0.5
MASK_VALUE = -1e30
NORMAL_PEAK = 0.3989422804014327

LOW = jnp.bfloat16
F32 = jnp.float32
VMEM_LIMIT = 60 * 1024 * 1024

BLOCK = 64
HALF = 128


def dot_nn(a, b):
    return lax.dot_general(a, b, (((1,), (0,)), ((), ())), preferred_element_type=F32)


def dot_nt(a, b):
    return lax.dot_general(a, b, (((1,), (1,)), ((), ())), preferred_element_type=F32)


def dot_tn(a, b):
    return lax.dot_general(a, b, (((0,), (0,)), ((), ())), preferred_element_type=F32)


def first_half(rows):
    return lax.broadcasted_iota(jnp.int32, (rows, HALF), 1) < BLOCK


def spread_heads(rows, picks):
    return jnp.concatenate([rows, rows, rows, rows], axis=0) * picks


def pick_heads(wide):
    low = first_half(BLOCK)
    left = jnp.where(low, wide[0:64, 0:HALF], wide[64:128, 0:HALF])
    right = jnp.where(low, wide[128:192, HALF:], wide[192:256, HALF:])
    return jnp.concatenate([left, right], axis=1)


def head_picks():
    row = lax.broadcasted_iota(jnp.int32, (256, 256), 0) // BLOCK
    col = lax.broadcasted_iota(jnp.int32, (256, 256), 1) // BLOCK
    return jnp.where(row == col, 1.0, 0.0).astype(LOW)


def gather_slot(ref, chosen, tile):
    a, b = chosen[2 * tile], chosen[2 * tile + 1]
    cols = pl.ds(tile * HALF, HALF)
    left = ref[pl.ds(pl.multiple_of(a * BLOCK, BLOCK), BLOCK), cols]
    right = ref[pl.ds(pl.multiple_of(b * BLOCK, BLOCK), BLOCK), cols]
    return jnp.where(first_half(BLOCK), left, right)


class Unit:
    def __init__(self, i, live, drawn, blocks):
        last = live - 1

        def state(b):
            return (b >= last).astype(jnp.int32) + (b > last).astype(jnp.int32)

        after = jnp.minimum(i + 1, blocks - 1)
        self.near = [i - 1, i, after]
        self.near_state = [
            jnp.where(i >= 3, state(i - 1), 2),
            state(i),
            jnp.where(i + 1 < blocks, state(after), 2),
        ]
        self.fixed_state = [state(0 * i), state(0 * i + 1)]
        self.chosen = [
            [drawn[(h * blocks + i) * 3 + s] for h in range(4)] for s in range(3)
        ]
        self.chosen_state = [[state(b) for b in row] for row in self.chosen]

    def gather(self, ref, out):
        for n, b in enumerate(self.near):
            out[pl.ds(128 + 64 * n, 64), :] = ref[pl.ds(pl.multiple_of(b * BLOCK, BLOCK), BLOCK), :]
        for s in range(3):
            for t in range(2):
                out[pl.ds(320 + 64 * s, 64), pl.ds(t * HALF, HALF)] = gather_slot(
                    ref, self.chosen[s], t
                )

    def bias(self, table, slots):
        rows = []
        for n in slots:
            if n < 5:
                one = table[(self.fixed_state + self.near_state)[n]]
                rows.append(jnp.concatenate([one, one], axis=1))
            else:
                st = self.chosen_state[n - 5]
                low = first_half(BLOCK)
                rows.append(
                    jnp.concatenate(
                        [
                            jnp.where(low, table[st[0]], table[st[1]]),
                            jnp.where(low, table[st[2]], table[st[3]]),
                        ],
                        axis=1,
                    )
                )
        return jnp.concatenate(rows, axis=0)


def chunk_bias(table, live, first, count):
    last = live - 1
    rows = []
    for n in range(count):
        b = first + n
        st = (b >= last).astype(jnp.int32) + (b > last).astype(jnp.int32)
        one = table[st]
        rows.append(jnp.concatenate([one, one], axis=1))
    return jnp.concatenate(rows, axis=0)


def forward_kernel(scal, drawn, table, x, w, shift, q_o, k_o, v_o, ctx_o, lse_o, picks, kg, vg, sg):
    length = x.shape[0]
    blocks = length // BLOCK
    live = scal[0]
    picks[...] = head_picks()

    def project(c, _):
        rows = pl.ds(pl.multiple_of(c * 512, 512), 512)
        out = (dot_nn(x[rows, :], w[...]) + shift[...]).astype(LOW)
        q_o[rows, :] = out[:, 0:256]
        k_o[rows, :] = out[:, 256:512]
        v_o[rows, :] = out[:, 512:768]
        return 0

    lax.fori_loop(0, length // 512, project, 0)
    for u in range(2):
        kg[u, 0:128, :] = k_o[0:128, :]
        vg[u, 0:128, :] = v_o[0:128, :]

    def sparse(i, u):
        unit = Unit(i, live, drawn, blocks)
        rows = pl.ds(pl.multiple_of(i * BLOCK, BLOCK), BLOCK)
        bd = spread_heads(q_o[rows, :] * jnp.asarray(QUERY_SCALE, LOW), picks[...])
        unit.gather(k_o, kg.at[u])
        unit.gather(v_o, vg.at[u])
        s = dot_nt(kg[u], bd) + unit.bias(table, range(8))
        m = jnp.max(s, axis=0, keepdims=True)
        e = jnp.exp(s - m)
        total = jnp.sum(e, axis=0, keepdims=True)
        p = (e * (1.0 / total)).astype(LOW)
        o = dot_tn(p, vg[u])
        ctx_o[rows, :] = pick_heads(o).astype(LOW)
        lse_o[pl.ds(i, 1), :] = m + jnp.log(total)

    def pair(j, _):
        sparse(2 + 2 * j, 0)
        sparse(3 + 2 * j, 1)
        return 0

    lax.fori_loop(0, blocks // 2 - 1, pair, 0)

    for g in range(2):
        bd = spread_heads(q_o[g * 64 : g * 64 + 64, :] * jnp.asarray(QUERY_SCALE, LOW), picks[...])

        def score(c, m):
            rows = pl.ds(pl.multiple_of(c * 512, 512), 512)
            s = dot_nt(k_o[rows, :], bd) + chunk_bias(table, live, c * 8, 8)
            sg[rows, :] = s
            return jnp.maximum(m, jnp.max(s, axis=0, keepdims=True))

        m = lax.fori_loop(0, length // 512, score, jnp.full((1, 256), MASK_VALUE, F32))

        def raise_(c, total):
            rows = pl.ds(pl.multiple_of(c * 512, 512), 512)
            e = jnp.exp(sg[rows, :] - m)
            sg[rows, :] = e
            return total + jnp.sum(e, axis=0, keepdims=True)

        total = lax.fori_loop(0, length // 512, raise_, jnp.zeros((1, 256), F32))
        scale = 1.0 / total

        def mix(c, o):
            rows = pl.ds(pl.multiple_of(c * 512, 512), 512)
            p = (sg[rows, :] * scale).astype(LOW)
            return o + dot_tn(p, v_o[rows, :])

        o = lax.fori_loop(0, length // 512, mix, jnp.zeros((256, 256), F32))
        ctx_o[g * 64 : g * 64 + 64, :] = pick_heads(o).astype(LOW)
        lse_o[g : g + 1, :] = m + jnp.log(total)


def vmem():
    return pl.BlockSpec(memory_space=pltpu.VMEM)


def smem():
    return pl.BlockSpec(memory_space=pltpu.SMEM)


def forward_attention(scal, drawn, table, x, w, shift):
    length = x.shape[0]
    blocks = length // BLOCK
    rows = jax.ShapeDtypeStruct((length, 256), LOW)
    return pl.pallas_call(
        forward_kernel,
        out_shape=(rows, rows, rows, rows, jax.ShapeDtypeStruct((blocks, 256), F32)),
        in_specs=[smem(), smem(), vmem(), vmem(), vmem(), vmem()],
        out_specs=[vmem()] * 5,
        scratch_shapes=[
            pltpu.VMEM((256, 256), LOW),
            pltpu.VMEM((2, 512, 256), LOW),
            pltpu.VMEM((2, 512, 256), LOW),
            pltpu.VMEM((length, 256), F32),
        ],
        compiler_params=pltpu.CompilerParams(vmem_limit_bytes=VMEM_LIMIT),
        cost_estimate=pl.CostEstimate(flops=16_000_000_000, bytes_accessed=12_000_000, transcendentals=10_000_000),
        name="attend_forward",
    )(scal, drawn, table, x, w, shift)


def normalize(summed):
    center = summed - jnp.mean(summed, axis=-1, keepdims=True)
    factor = lax.rsqrt(jnp.mean(center * center, axis=-1, keepdims=True) + NORM_EPSILON)
    return (center * factor, factor)


def normalize_back(grad_normed, normed, factor):
    return factor * (
        grad_normed
        - jnp.mean(grad_normed, axis=-1, keepdims=True)
        - normed * jnp.mean(grad_normed * normed, axis=-1, keepdims=True)
    )


ERF_P = 0.3275911 * 0.7071067811865476
ERF_A = (0.254829592, -0.284496736, 1.421413741, -1.453152027, 1.061405429)


def gelu_parts(v):
    bell = jnp.exp(-0.5 * v * v)
    t = 1.0 / (1.0 + ERF_P * jnp.abs(v))
    a1, a2, a3, a4, a5 = (0.5 * a for a in ERF_A)
    tail = ((((a5 * t + a4) * t + a3) * t + a2) * t + a1) * t * bell
    cumulative = jnp.where(v < 0.0, tail, 1.0 - tail)
    return v * cumulative, cumulative + v * (NORMAL_PEAK * bell)


def middle_kernel(
    scal, table, x, cot, ctx, w_out, w_up, w_down, up_shift, vec,
    out_o, gz1_o, gctx_o, delta_o, gdown_o, gup_o, gout_o, gub_o, gvec_o, act, slope,
):
    step = pl.program_id(0)
    rows = x.shape[0]
    last = scal[0] - 1

    @pl.when(step == 0)
    def _():
        for ref in (gdown_o, gup_o, gout_o, gub_o, gvec_o):
            ref[...] = jnp.zeros_like(ref)

    marks = []
    for n in range(rows // BLOCK):
        b = step * (rows // BLOCK) + n
        st = (b >= last).astype(jnp.int32) + (b > last).astype(jnp.int32)
        one = table[st]
        marks.append(jnp.concatenate([one, one], axis=1))
    open_ = jnp.concatenate(marks, axis=0) == 0.0

    def row(n):
        return vec[n : n + 1, :]

    ctx_v = ctx[...]
    attended = dot_nn(ctx_v, w_out[...]) + row(2)
    normed_one, factor_one = normalize(x[...].astype(F32) + attended)
    first_out = normed_one * row(3) + row(4)
    first_low = first_out.astype(LOW)
    branch = row(5)
    for c in range(0, 1024, 256):
        pre = dot_nn(first_low, w_up[:, c : c + 256]) + up_shift[:, c : c + 256]
        a, s = gelu_parts(pre)
        act[:, c : c + 256] = a.astype(LOW)
        slope[:, c : c + 256] = s
    branch = dot_nn(act[...], w_down[...]) + row(5)
    normed_two, factor_two = normalize(first_out + branch)
    out_o[...] = jnp.where(open_, normed_two * row(6) + row(7), 0.0).astype(LOW)
    grad_y = jnp.where(open_, cot[...].astype(F32), 0.0)
    grad_z2 = normalize_back(grad_y * row(6), normed_two, factor_two)
    grad_branch = grad_z2.astype(LOW)
    gdown_o[...] += dot_tn(act[...], grad_branch)
    back = jnp.zeros((rows, 256), F32)
    for c in range(0, 1024, 256):
        grad_act = dot_nt(grad_branch, w_down[c : c + 256, :])
        grad_pre = (grad_act * slope[:, c : c + 256]).astype(LOW)
        act[:, c : c + 256] = grad_pre
        gub_o[:, c : c + 256] += jnp.sum(grad_pre.astype(F32), axis=0, keepdims=True)
    gup_o[...] += dot_tn(first_low, act[...])
    grad_first = grad_z2 + dot_nt(act[...], w_up[...])
    grad_z1 = normalize_back(grad_first * row(3), normed_one, factor_one)
    gz1_o[...] = grad_z1
    grad_attended = grad_z1.astype(LOW)
    gout_o[...] += dot_tn(ctx_v, grad_attended)
    grad_context = dot_nt(grad_attended, w_out[...]).astype(LOW)
    gctx_o[...] = grad_context

    def add(n, values):
        gvec_o[n : n + 1, :] += jnp.sum(values, axis=0, keepdims=True)

    add(2, grad_attended.astype(F32))
    add(3, grad_first * normed_one)
    add(4, grad_first)
    add(5, grad_branch.astype(F32))
    add(6, grad_y * normed_two)
    add(7, grad_y)
    both = ctx_v.astype(F32) * grad_context.astype(F32)
    upper = both.astype(LOW)
    lower = (both - upper.astype(F32)).astype(LOW)
    group = lax.broadcasted_iota(jnp.int32, (8, 256), 1) // BLOCK
    ones = jnp.where(group == lax.broadcasted_iota(jnp.int32, (8, 256), 0), 1.0, 0.0).astype(LOW)
    sums = dot_nt(ones, upper) + dot_nt(ones, lower)
    for n in range(rows // BLOCK):
        part = sums[0:4, n * BLOCK : (n + 1) * BLOCK]
        delta_o[n : n + 1, :] = jnp.concatenate([part[h : h + 1, :] for h in range(4)], axis=1)


def middle(scal, table, x, cot, ctx, w_out, w_up, w_down, up_shift, vec):
    length = x.shape[0]
    rows = 512
    wide = pl.BlockSpec((rows, 256), lambda i, s: (i, 0))

    def whole(*shape):
        return pl.BlockSpec(shape, lambda i, s: (0,) * len(shape))

    shape = jax.ShapeDtypeStruct
    return pl.pallas_call(
        middle_kernel,
        grid_spec=pltpu.PrefetchScalarGridSpec(
            num_scalar_prefetch=1,
            grid=(length // rows,),
            in_specs=[
                whole(3, 64, 128), wide, wide, wide, whole(256, 256), whole(256, 1024), whole(1024, 256),
                whole(1, 1024), whole(8, 256),
            ],
            out_specs=[
                wide, wide, wide, pl.BlockSpec((rows // BLOCK, 256), lambda i, s: (i, 0)),
                whole(1024, 256), whole(256, 1024), whole(256, 256), whole(1, 1024), whole(8, 256),
            ],
            scratch_shapes=[pltpu.VMEM((rows, 1024), LOW), pltpu.VMEM((rows, 1024), F32)],
        ),
        out_shape=(
            shape((length, 256), LOW), shape((length, 256), F32), shape((length, 256), LOW),
            shape((length // BLOCK, 256), F32), shape((1024, 256), F32), shape((256, 1024), F32),
            shape((256, 256), F32), shape((1, 1024), F32), shape((8, 256), F32),
        ),
        compiler_params=pltpu.CompilerParams(vmem_limit_bytes=VMEM_LIMIT),
        cost_estimate=pl.CostEstimate(flops=16_000_000_000, bytes_accessed=20_000_000, transcendentals=10_000_000),
        name="middle",
    )(scal, table, x, cot, ctx, w_out, w_up, w_down, up_shift, vec)


def backward_kernel(
    scal, drawn, table, q, k, v, gctx, lse, delta, gz1, x, w,
    gin_o, gw_o, gs_o, picks, kg, vg, dq, dk, dv,
):
    length = x.shape[0]
    blocks = length // BLOCK
    live = scal[0]
    picks[...] = head_picks()
    dk[...] = jnp.zeros_like(dk)
    dv[...] = jnp.zeros_like(dv)
    for u in range(2):
        kg[u, 0:128, :] = k[0:128, :]
        vg[u, 0:128, :] = v[0:128, :]

    def terms(kh, vh, bias, bdq, bdo, lse_row, delta_row):
        p = jnp.exp(dot_nt(kh, bdq) + bias - lse_row)
        dvh = dot_nn(p.astype(LOW), bdo)
        ds = (p * (dot_nt(vh, bdo) - delta_row)).astype(LOW)
        return dvh, dot_nn(ds, bdq), dot_tn(ds, kh)

    def spread(i):
        rows = pl.ds(pl.multiple_of(i * BLOCK, BLOCK), BLOCK)
        bdq = spread_heads(q[rows, :] * jnp.asarray(QUERY_SCALE, LOW), picks[...])
        bdo = spread_heads(gctx[rows, :], picks[...])
        return rows, bdq, bdo

    def sparse(i, u):
        unit = Unit(i, live, drawn, blocks)
        rows, bdq, bdo = spread(i)
        unit.gather(k, kg.at[u])
        unit.gather(v, vg.at[u])
        lse_row, delta_row = lse[pl.ds(i, 1), :], delta[pl.ds(i, 1), :]
        low = first_half(BLOCK)
        grad_q = None
        for half in range(2):
            part = slice(half * 256, half * 256 + 256)
            dvh, dkh, dqh = terms(
                kg[u, part, :], vg[u, part, :], unit.bias(table, range(4 * half, 4 * half + 4)), bdq, bdo, lse_row, delta_row
            )
            grad_q = dqh if grad_q is None else grad_q + dqh
            for acc, terms_ in ((dk, dkh), (dv, dvh)):
                if half == 0:
                    acc[0:128, :] += terms_[0:128, :]
                for n in range(4):
                    slot = 4 * half + n
                    one = terms_[n * 64 : n * 64 + 64, :]
                    if slot < 2:
                        continue
                    if slot < 5:
                        at = pl.ds(pl.multiple_of(unit.near[slot - 2] * BLOCK, BLOCK), BLOCK)
                        acc[at, :] += one
                    else:
                        for h in range(4):
                            t = h // 2
                            at = pl.ds(pl.multiple_of(unit.chosen[slot - 5][h] * BLOCK, BLOCK), BLOCK)
                            cols = pl.ds(t * HALF, HALF)
                            mine = low if h % 2 == 0 else jnp.logical_not(low)
                            acc[at, cols] += jnp.where(mine, one[:, t * HALF : t * HALF + HALF], 0.0)
        dq[rows, :] = (pick_heads(grad_q) * QUERY_SCALE).astype(LOW)

    def pair(j, _):
        sparse(2 + 2 * j, 0)
        sparse(3 + 2 * j, 1)
        return 0

    lax.fori_loop(0, blocks // 2 - 1, pair, 0)

    for g in range(2):
        _, bdq, bdo = spread(g)
        lse_row, delta_row = lse[g : g + 1, :], delta[g : g + 1, :]

        def chunk(c, grad_q):
            at = pl.ds(pl.multiple_of(c * 256, 256), 256)
            dvh, dkh, dqh = terms(
                k[at, :], v[at, :], chunk_bias(table, live, c * 4, 4), bdq, bdo, lse_row, delta_row
            )
            dk[at, :] += dkh
            dv[at, :] += dvh
            return grad_q + dqh

        grad_q = lax.fori_loop(0, length // 256, chunk, jnp.zeros((256, 256), F32))
        dq[g * 64 : g * 64 + 64, :] = (pick_heads(grad_q) * QUERY_SCALE).astype(LOW)

    gw_o[...] = jnp.zeros_like(gw_o)

    def finish(c, shifts):
        rows = pl.ds(pl.multiple_of(c * 512, 512), 512)
        dqkv = jnp.concatenate([dq[rows, :], dk[rows, :].astype(LOW), dv[rows, :].astype(LOW)], axis=1)
        gin_o[rows, :] = (gz1[rows, :] + dot_nt(dqkv, w[...])).astype(LOW)
        gw_o[...] += dot_tn(x[rows, :], dqkv)
        return shifts + jnp.sum(dqkv.astype(F32), axis=0, keepdims=True)

    gs_o[...] = lax.fori_loop(0, length // 512, finish, jnp.zeros((1, 768), F32))


def backward_attention(scal, drawn, table, q, k, v, gctx, lse, delta, gz1, x, w):
    length = x.shape[0]
    shape = jax.ShapeDtypeStruct
    return pl.pallas_call(
        backward_kernel,
        out_shape=(shape((length, 256), LOW), shape((256, 768), F32), shape((1, 768), F32)),
        in_specs=[smem(), smem()] + [vmem()] * 10,
        out_specs=[vmem()] * 3,
        scratch_shapes=[
            pltpu.VMEM((256, 256), LOW),
            pltpu.VMEM((2, 512, 256), LOW),
            pltpu.VMEM((2, 512, 256), LOW),
            pltpu.VMEM((length, 256), LOW),
            pltpu.VMEM((length, 256), F32),
            pltpu.VMEM((length, 256), F32),
        ],
        compiler_params=pltpu.CompilerParams(vmem_limit_bytes=VMEM_LIMIT),
        cost_estimate=pl.CostEstimate(flops=40_000_000_000, bytes_accessed=20_000_000, transcendentals=10_000_000),
        name="attend_backward",
    )(scal, drawn, table, q, k, v, gctx, lse, delta, gz1, x, w)


def bias_table(tail):
    column = jnp.stack([jnp.zeros_like(tail, F32), jnp.where(tail == 1, 0.0, MASK_VALUE), jnp.full(tail.shape, MASK_VALUE, F32)])
    return jnp.broadcast_to(column[:, :, None], (3, BLOCK, HALF))


def reorder_kernel(scatter, order, src, dst, sems):
    count = src.shape[0]
    copies = []
    for j in range(count):
        one = order[j]
        if scatter:
            copies.append(pltpu.make_async_copy(src.at[j], dst.at[one], sems.at[j]))
        else:
            copies.append(pltpu.make_async_copy(src.at[one], dst.at[j], sems.at[j]))
        copies[-1].start()
    for copy in copies:
        copy.wait()


def reorder(order, src, scatter):
    return pl.pallas_call(
        functools.partial(reorder_kernel, scatter),
        out_shape=jax.ShapeDtypeStruct(src.shape, src.dtype),
        in_specs=[smem(), pl.BlockSpec(memory_space=pl.ANY)],
        out_specs=pl.BlockSpec(memory_space=pl.ANY),
        scratch_shapes=[pltpu.SemaphoreType.DMA((src.shape[0],))],
        cost_estimate=pl.CostEstimate(flops=0, bytes_accessed=2 * src.size * 2, transcendentals=0),
        name="reorder",
    )(order, src)


def exchange_weights(shard_index, parts):
    w_qkv, w_out, w_up, w_down, up_bias, vectors = parts
    rows = w_qkv.shape[0]
    down = w_down.reshape(4, rows, -1)
    pack = jnp.concatenate([w_qkv, w_out, w_up] + [down[n] for n in range(4)], axis=1)
    small = jnp.concatenate([up_bias.reshape(-1, 256), vectors], axis=0)
    swap = [(0, 1), (1, 0)]
    other, other_small = lax.ppermute(pack, "shard", swap), lax.ppermute(small, "shard", swap)
    first = shard_index == 0

    def join(own, got):
        return jnp.stack([jnp.where(first, own, got), jnp.where(first, got, own)])

    both, both_small = join(pack, other), join(small, other_small)

    def cols(lo, hi):
        return both[:, :, lo:hi].reshape(2 * rows, hi - lo)

    full_down = jnp.transpose(both[:, :, 2048:].reshape(2, rows, 4, 256), (0, 2, 1, 3)).reshape(-1, 256)
    full_bias = both_small[:, :2].reshape(-1)
    full_vec = both_small[:, 2:].reshape(8, 256)
    return cols(0, 768), cols(768, 1024), cols(1024, 2048), full_down, full_bias, full_vec


def sum_over_devices(pack):
    shards, rows, columns = pack.shape
    count = lax.axis_size("dp")
    pieces = jnp.transpose(pack.reshape(shards, count, rows // count, columns), (1, 0, 2, 3))
    pieces = pieces.reshape(count * shards, rows // count, columns)
    got = lax.all_to_all(pieces, ("dp", "shard"), split_axis=0, concat_axis=0, tiled=True)
    mine = jnp.sum(got.astype(F32), axis=0)
    return lax.all_gather(mine, "dp", axis=0, tiled=True)


def adam_update(grad, state, decay):
    correct_one = 1.0 - FIRST_BETA**STEP
    correct_two = 1.0 - SECOND_BETA**STEP
    first_new = FIRST_BETA * state[1] + (1.0 - FIRST_BETA) * grad
    second_new = SECOND_BETA * state[2] + (1.0 - SECOND_BETA) * grad * grad
    direction = first_new / correct_one / (jnp.sqrt(second_new / correct_two) + ADAM_EPSILON)
    master_new = state[0] - LEARNING_RATE * (direction + decay * state[0])
    return (master_new, first_new, second_new)


def on_device(
    hidden, cotangent, assign, live_blocks, tail_live, random_blocks, w_qkv, w_out, w_up, w_down, up_bias, vectors,
    state_qkv, state_out, state_up, state_down, state_ubias, state_vec,
):
    shard_count = lax.axis_size("shard")
    shard_index = lax.axis_index("shard")
    data_index = lax.axis_index("dp")
    row_seqs, rows_here, width = hidden.shape
    length = row_seqs * rows_here
    order = lax.dynamic_index_in_dim(assign.reshape(row_seqs, shard_count), shard_index, 1, keepdims=False)
    own = shard_index * row_seqs + lax.dynamic_index_in_dim(order, data_index, 0, keepdims=False)
    live = lax.dynamic_slice_in_dim(live_blocks, own, 1)
    tail = lax.dynamic_index_in_dim(tail_live, own, 0, keepdims=False)

    def to_slot(rows):
        return lax.all_to_all(rows, "dp", split_axis=0, concat_axis=0, tiled=True)

    x = to_slot(reorder(order, hidden, False)).reshape(length, width)
    cot = to_slot(reorder(order, cotangent, False)).reshape(length, width)
    w_qkv, w_out, w_up, w_down, up_bias, vectors = exchange_weights(
        shard_index, (w_qkv, w_out, w_up, w_down, up_bias, vectors)
    )
    vec = vectors.astype(F32)
    shift = jnp.concatenate([vec[0], jnp.zeros_like(vec[0]), vec[1]])[None]
    table = bias_table(tail)
    drawn = random_blocks.reshape(-1)
    q, k, v, ctx, lse = forward_attention(live, drawn, table, x, w_qkv, shift)
    out, gz1, gctx, delta, gdown, gup, gout, gub, gvec = middle(
        live, table, x, cot, ctx, w_out, w_up, w_down, up_bias.astype(F32)[None], vec
    )

    def from_slot(rows):
        back = lax.all_to_all(
            rows.reshape(row_seqs, rows_here, width), "dp", split_axis=0, concat_axis=0, tiled=True
        )
        return reorder(order, back, True)

    layer_out = from_slot(out)
    half = gup.shape[0] // 2

    def extra(*pieces):
        block = jnp.concatenate([piece.reshape(shard_count, -1, HALF) for piece in pieces], axis=1)
        return jnp.pad(block, ((0, 0), (0, half - block.shape[1]), (0, 0)))

    down = jnp.transpose(gdown.reshape(2, 4, half, 256), (0, 2, 1, 3)).reshape(2, half, 1024)
    early = jnp.concatenate(
        [gup.reshape(2, half, 1024), gout.reshape(2, half, 256), down, extra(gub, gvec)], axis=2
    ).astype(LOW)
    early = sum_over_devices(early)
    gin, gw, gs = backward_attention(live, drawn, table, q, k, v, gctx, lse, delta, gz1, x, w_qkv)
    input_grad = from_slot(gin)
    ends = jnp.concatenate([gs[:, :256], gs[:, 512:], jnp.zeros((6, 256), F32)])
    late = jnp.concatenate([gw.reshape(2, half, 768), extra(ends)], axis=2).astype(LOW)
    late = sum_over_devices(late)
    grad_qkv = late[:, :768]
    grad_up = early[:, :1024]
    grad_out = early[:, 1024:1280]
    grad_down = jnp.concatenate([early[:, 1280 + 256 * n : 1536 + 256 * n] for n in range(4)], axis=0)
    grad_ubias = early[0:4, 2304:].reshape(-1)
    grad_vec = early[4:12, 2304:].reshape(4, 256) + late[0:8, 768:].reshape(4, 256)
    grads = (grad_qkv, grad_out, grad_up, grad_down, grad_ubias, grad_vec)
    states = (state_qkv, state_out, state_up, state_down, state_ubias, state_vec)
    decays = (WEIGHT_DECAY, WEIGHT_DECAY, WEIGHT_DECAY, WEIGHT_DECAY, 0.0, 0.0)
    updated = [adam_update(*group) for group in zip(grads, states, decays)]
    rows = [jnp.concatenate([entry[n].reshape(1, -1) for entry in updated], axis=1) for n in range(3)]
    return (layer_out, input_grad) + grads + tuple(rows)


def solution(mesh):
    placed = (
        P("shard", "dp", None), P("shard", "dp", None), P(), P(), P(), P(("dp", "shard"), None, None, None),
        P("shard", None), P("shard", None), P("shard", None), P("shard", None), P("shard"), P("shard", None),
        P(None, "shard", None), P(None, "shard", None), P(None, "shard", None), P(None, "shard", None),
        P(None, "shard"), P(None, "shard", None),
    )
    return jax.shard_map(
        on_device,
        mesh=mesh,
        in_specs=placed,
        out_specs=(
            P("shard", "dp", None), P("shard", "dp", None), P("shard", None), P("shard", None), P("shard", None),
            P("shard", None), P("shard"), P("shard", None), P("shard", None), P("shard", None), P("shard", None),
        ),
        check_vma=False,
    )
```

time: 1340 us -> 652 us (0.49); the launches traced: 1320 us -> 651 us
  Pallas kernels: 0 us -> 438 us
  matrix products: 373 us -> 0 us
  starting transfers between devices: 381 us -> 46.3 us
  local copies, waits for them, and re-layouts: 249 us -> 33.8 us
  other arithmetic: 119 us -> 19.3 us
  blocking collectives: 115 us -> 37.8 us
    pallas_call x0 -> x7, Pallas kernels: none -> 438 us  [the longest x4 262 us: reorder(): pl.pallas_call(functools.partial(reorder_kernel, scatter), out_shape=jax....]
    dot_general x86 -> x0, matrix products: 373 us -> none  [the longest x8 69.1 us: place_blocks(): jnp.einsum('thsn,thskd->hnkd', choose_low, upper, preferred_element_type=...]
    all_to_all x4 -> x6, starting transfers between devices: 381 us -> 44.1 us  [the longest x2 22.3 us: from_slot(): lax.all_to_all(rows.reshape(row_seqs, rows_here, width), 'dp', split_axis...]
    psum x1 -> x0, blocking collectives: 75.2 us -> none  [on_device(): grad_totals = lax.psum(halves, 'dp')]
    reshape x14 -> x7, local copies, waits for them, and re-layouts: 64.8 us -> 2.81 us  [the longest x1 0.83 us: exchange_weights(): both[:, :, 2048:].reshape(2, rows, 4, 256)]
    unnamed x9 -> x10, other arithmetic: 48 us -> 9.64 us
    unnamed x218 -> x89, local copies, waits for them, and re-layouts: 60.2 us -> 22.9 us
    reduce_sum x12 -> x2, other arithmetic: 33.8 us -> 0.89 us  [sum_over_devices(): mine = jnp.sum(got.astype(F32), axis=0)]
  transfers between devices with their start and end apart: 8 -> 9, of which waited for: 2 -> 3; matrix products, arithmetic and copies ran while one was open for 35% -> 4% of each run, Pallas kernels for 0% -> 39%
where the time goes in v1:
time: 652 us; the launch traced here: 651 us
  Pallas kernels  438 us (67%)
  waiting for transfers between devices  59.9 us (9%)
  starting transfers between devices  46.3 us (7%)
  blocking collectives  37.8 us (6%)
  local copies, waits for them, and re-layouts  33.8 us (5%)
  other arithmetic  19.3 us (3%)
  between operations  15.4 us (2%)
    pallas_call x4, Pallas kernels, reorder(): pl.pallas_call(functools.partial(reorder_kernel, scatter), out_shape=jax....  262 us
    pallas_call x1, Pallas kernels, backward_attention(): pl.pallas_call(backward_kernel, out_shape=(shape((length, 256), LOW), sha...  76.7 us
    pallas_call x1, Pallas kernels, forward_attention(): pl.pallas_call(forward_kernel, out_shape=(rows, rows, rows, rows, jax.Sha...  58.2 us
    pallas_call x1, Pallas kernels, middle(): pl.pallas_call(middle_kernel, grid_spec=pltpu.PrefetchScalarGridSpec(num_...  41.6 us
    all_to_all x2, waiting for transfers between devices, from_slot(): lax.all_to_all(rows.reshape(row_seqs, rows_here, width), 'dp', split_axis...  38.8 us
    all_gather x1, blocking collectives, sum_over_devices(): return lax.all_gather(mine, 'dp', axis=0, tiled=True)  37.8 us
    unnamed x89, local copies, waits for them, and re-layouts  22.9 us
    all_to_all x2, starting transfers between devices, from_slot(): lax.all_to_all(rows.reshape(row_seqs, rows_here, width), 'dp', split_axis...  22.3 us
  transfers between devices with their start and end apart: 9, of which 3 were waited for; matrix products, arithmetic and copies ran while one was open for 4% of the time, Pallas kernels for 39%

profile of v1, /device:TPU:0, one launch (start us, length us, event | category | flops | bytes accessed | tf_op | source)
XLA Modules:
  0.0 651.0 jit_solution(6479458820422665880)
XLA Ops:
  8.6 65.4 %reorder.4 = bf16[16,256,256]{2,1,0:T(8,128)(2,1)} custom-call(s32[16]{0:T(128)} %dynamic-slice_reduce_fusion.order, bf16[16,256,256]{2,1,0:T(8,128)(2,1)} %src.2), custom_call_target="tpu_custom_call" | custom-call | bytes 4194304 | tf_op jit(solution)/shard_map/reorder/pallas_call | solution.py:507
  74.1 7.4 %all-to-all-start = ((bf16[16,256,256]{2,1,0:T(8,128)(2,1)}), bf16[16,256,256]{2,1,0:T(8,128)(2,1)S(1)}, u32[]{:S(2)}, u32[]{:S(2)}) async-start(bf16[16,256,256]{2,1,0:T(8,128)(2,1)} %reorder.4), calls=%async_computation | async-start | bytes 4194304 | tf_op jit(solution)/shard_map/all_to_all | solution.py:577
  81.6 1.6 collective-permute-start.1
  83.1 65.4 %reorder.5 = bf16[16,256,256]{2,1,0:T(8,128)(2,1)} custom-call(s32[16]{0:T(128)} %dynamic-slice_reduce_fusion.order, bf16[16,256,256]{2,1,0:T(8,128)(2,1)} %src.3), custom_call_target="tpu_custom_call" | custom-call | bytes 4194304 | tf_op jit(solution)/shard_map/reorder/pallas_call | solution.py:507
  149.7 1.3 copy-done.5
  151.0 6.1 all-to-all-start.1
  162.6 14.4 %collective-permute-done = bf16[128,3072]{1,0:T(8,128)(2,1)S(1)} collective-permute-done((bf16[128,3072]{1,0:T(8,128)(2,1)S(1)}, bf16[128,3072]{1,0:T(8,128)(2,1)S(1)}, u32[]{:S(2)}, u32[]{:S(2)}) %collective-permute-start) | collective-permute-done | bytes 786464 | tf_op jit(solution)/shard_map/ppermute | solution.py:525
  180.9 58.2 %attend_forward.1 = (bf16[4096,256]{1,0:T(8,128)(2,1)}, bf16[4096,256]{1,0:T(8,128)(2,1)}, bf16[4096,256]{1,0:T(8,128)(2,1)}, bf16[4096,256]{1,0:T(8,128)(2,1)}, f32[64,256]{1,0:T(8,128)}) custom-call(s32[1]{0:T(128)} %dynamic_slice.17.scal, s32[768]{0:T(1024)} %reshape.439.drawn, f32[3,64,128]{2,1,0:T(8,128)} %broadcast_in_dim.23.table, ...), custom_call_target="tpu_custom_call" | custom-call | flops 16000000000 | bytes 12000000 | tf_op jit(solution)/shard_map/attend_forward/pallas_call | solution.py:214
  239.1 41.6 %middle.1 = (bf16[4096,256]{1,0:T(8,128)(2,1)}, f32[4096,256]{1,0:T(8,128)}, bf16[4096,256]{1,0:T(8,128)(2,1)}, f32[64,256]{1,0:T(8,128)}, f32[1024,256]{1,0:T(8...) custom-call(s32[1]{0:T(128)} %dynamic_slice.17.scal, ...), custom_call_target="tpu_custom_call" | custom-call | flops 16000000000 | bytes 20000000 | tf_op jit(solution)/shard_map/middle/pallas_call | solution.py:344
  280.8 76.7 %attend_backward.1 = (bf16[4096,256]{1,0:T(8,128)(2,1)}, f32[256,768]{1,0:T(8,128)}, f32[1,768]{1,0:T(1,128)}) custom-call(s32[1]{0:T(128)} %dynamic_slice.17.scal, s32[768]{0:T(1024)} %reshape.439.drawn, f32[3,64,128]{2,1,0:T(8,128)} %broadcast_in_dim.23.table, bf16[4096,256]{1,0:T(8,128)(2,1)} %get-tuple-element.30.q, ...), custom_call_target="tpu_custom_call" | custom-call | flops 40000000000 | bytes 20000000 | tf_op jit(solution)/shard_map/attend_backward/pallas_call | solution.py:468
  358.2 1.2 convert.45
  360.3 4.9 all-to-all-start.4
  365.4 1.4 copy.47
  366.8 1.3 copy.48
  368.1 1.4 copy.50
  371.0 1.1 copy.41
  372.1 6.7 %all-to-all-done.4 = bf16[32,8,896]{2,1,0:T(8,128)(2,1)S(1)} async-done(((bf16[32,8,896]{2,1,0:T(8,128)(2,1)}), bf16[32,8,896]{2,1,0:T(8,128)(2,1)S(1)}, u32[]{:S(2)}, u32[]{:S(2)}) %all-to-all-start.4) | async-done | bytes 458784 | tf_op jit(solution)/shard_map/all_to_all | solution.py:547
  378.8 3.4 all-to-all-start.5
  382.3 37.8 %all_gather.6 = f32[128,896]{1,0:T(8,128)S(1)} all-gather(f32[8,896]{1,0:T(8,128)S(1)} %convert_reduce_fusion.1), channel_id=1, replica_groups=mesh['dp'=16,'shard'=2] {'dp'}, dimensions={0}, use_global_device_ids=true | all-gather | bytes 487424 | tf_op jit(solution)/shard_map/all_gather | solution.py:549
  423.2 1.2 copy.44
  424.4 6.9 %all-to-all-start.3 = ((bf16[16,256,256]{2,1,0:T(8,128)(2,1)}), bf16[16,256,256]{2,1,0:T(8,128)(2,1)S(1)}, u32[]{:S(2)}, u32[]{:S(2)}) async-start(bf16[16,256,256]{2,1,0:T(8,128)(2,1)} %bitcast.187), calls=%async_computation.3 | async-start | bytes 4194304 | tf_op jit(solution)/shard_map/all_to_all | solution.py:594
  431.3 1.8 constant_dynamic-update-slice_fusion.7
  433.1 2.1 copy.57
  436.0 38.8 %all-to-all-done.3.src = bf16[16,256,256]{2,1,0:T(8,128)(2,1)S(1)} async-done(((bf16[16,256,256]{2,1,0:T(8,128)(2,1)}), bf16[16,256,256]{2,1,0:T(8,128)(2,1)S(1)}, u32[]{:S(2)}, u32[]{:S(2)}) %all-to-all-start.3) | async-done | bytes 2097184 | tf_op jit(solution)/shard_map/all_to_all | solution.py:594
  474.8 1.4 copy-done
  476.2 15.4 %all-to-all-start.2 = ((bf16[16,256,256]{2,1,0:T(8,128)(2,1)}), bf16[16,256,256]{2,1,0:T(8,128)(2,1)}, u32[]{:S(2)}, u32[]{:S(2)}) async-start(bf16[16,256,256]{2,1,0:T(8,128)(2,1)} %bitcast.186), calls=%async_computation.2 | async-start | bytes 4194304 | tf_op jit(solution)/shard_map/all_to_all | solution.py:594
  492.4 65.4 %reorder.7 = bf16[16,256,256]{2,1,0:T(8,128)(2,1)} custom-call(s32[16]{0:T(128)} %dynamic-slice_reduce_fusion.order, bf16[16,256,256]{2,1,0:T(8,128)(2,1)} %copy-done), custom_call_target="tpu_custom_call" | custom-call | bytes 4194304 | tf_op jit(solution)/shard_map/reorder/pallas_call | solution.py:507
  557.9 65.6 %reorder.6 = bf16[16,256,256]{2,1,0:T(8,128)(2,1)} custom-call(s32[16]{0:T(128)} %dynamic-slice_reduce_fusion.order, bf16[16,256,256]{2,1,0:T(8,128)(2,1)} %all-to-all-done.2.src), custom_call_target="tpu_custom_call" | custom-call | bytes 4194304 | tf_op jit(solution)/shard_map/reorder/pallas_call | solution.py:507
  623.5 1.2 fusion.32
  626.4 1.1 fusion.19
  635.5 6.1 constant_dynamic-update-slice_fusion.16
  641.6 1.3 fusion.31
  (150 shorter events, 30.0 us)
Async XLA Ops:
  74.1 7.4 %copy-start.27 = (bf16[512]{0:T(512)(128)(2,1)S(1)}, bf16[512]{0:T(512)(128)(2,1)}, u32[]{:S(2)}) copy-start(bf16[512]{0:T(512)(128)(2,1)} %param.28) | copy-start | bytes 3076
  74.1 7.4 %copy-start.23 = (bf16[4,256]{1,0:T(4,128)(2,1)S(1)}, bf16[4,256]{1,0:T(4,128)(2,1)}, u32[]{:S(2)}) copy-start(bf16[4,256]{1,0:T(4,128)(2,1)} %param.29) | copy-start | bytes 6148
  74.1 75.6 %all-to-all-start = ((bf16[16,256,256]{2,1,0:T(8,128)(2,1)}), bf16[16,256,256]{2,1,0:T(8,128)(2,1)S(1)}, u32[]{:S(2)}, u32[]{:S(2)}) async-start(bf16[16,256,256]{2,1,0:T(8,128)(2,1)} %reorder.4), calls=%async_computation | async-start | bytes 4194304 | tf_op jit(solution)/shard_map/all_to_all | solution.py:577
  81.5 68.0 %copy-start.19 = (bf16[128,256]{1,0:T(8,128)(2,1)S(1)}, bf16[128,256]{1,0:T(8,128)(2,1)}, u32[]{:S(2)}) copy-start(bf16[128,256]{1,0:T(8,128)(2,1)} %param.25) | copy-start | bytes 196612
  81.6 68.0 %copy-start.17 = (bf16[128,1024]{1,0:T(8,128)(2,1)S(1)}, bf16[128,1024]{1,0:T(8,128)(2,1)}, u32[]{:S(2)}) copy-start(bf16[128,1024]{1,0:T(8,128)(2,1)} %param.26) | copy-start | bytes 786436
  81.6 68.0 %copy-start.18 = (bf16[512,256]{1,0:T(8,128)(2,1)S(1)}, bf16[512,256]{1,0:T(8,128)(2,1)}, u32[]{:S(2)}) copy-start(bf16[512,256]{1,0:T(8,128)(2,1)} %param.27) | copy-start | bytes 786436
  81.6 79.7 %collective-permute-start.1 = (bf16[6,256]{1,0:T(8,128)(2,1)S(1)}, bf16[6,256]{1,0:T(8,128)(2,1)S(1)}, u32[]{:S(2)}, u32[]{:S(2)}) collective-permute-start(bf16[6,256]{1,0:T(8,128)(2,1)S(1)} %pad_maximum_fusion.3), channel_id=1, source_target_pairs={{0,1},{1,0},{2,3},{3,2},{4,5},{5,4},{6,7},{7,6},{8,9},{9,8},{10,11... | collective-permute-start | bytes 9224 | tf_op jit(solution)/shard_map/ppermute | solution.py:525
  149.6 10.0 %copy-start.28 = (s32[32]{0:T(128)S(1)}, s32[32]{0:T(128)}, u32[]{:S(2)}) copy-start(s32[32]{0:T(128)} %param.21) | copy-start | bytes 388
  149.6 10.6 %copy-start.24 = (s32[1,4,64,3]{2,1,3,0:T(4,128)S(1)}, s32[1,4,64,3]{2,1,3,0:T(4,128)}, u32[]{:S(2)}) copy-start(s32[1,4,64,3]{2,1,3,0:T(4,128)} %param.23) | copy-start | bytes 9220
  149.7 1.3 copy-start.5
  151.0 88.1 %all-to-all-start.1 = ((bf16[16,256,256]{2,1,0:T(8,128)(2,1)}), bf16[16,256,256]{2,1,0:T(8,128)(2,1)}, u32[]{:S(2)}, u32[]{:S(2)}) async-start(bf16[16,256,256]{2,1,0:T(8,128)(2,1)} %reorder.5), calls=%async_computation.1 | async-start | bytes 4194304 | tf_op jit(solution)/shard_map/all_to_all | solution.py:577
  157.1 19.9 %collective-permute-start = (bf16[128,3072]{1,0:T(8,128)(2,1)S(1)}, bf16[128,3072]{1,0:T(8,128)(2,1)S(1)}, u32[]{:S(2)}, u32[]{:S(2)}) collective-permute-start(bf16[128,3072]{1,0:T(8,128)(2,1)S(1)} %slice_dynamic-update-slice_fusion), channel_id=1, source_target_pairs={{0,1},{1,0},{2,3},{3,2},{4,5},{5,4},{6,7},{7,6},{8,9},{9,8},{10,11... | collective-permute-start | bytes 2359304 | tf_op jit(solution)/shard_map/ppermute | solution.py:525
  161.3 15.7 %copy-start.20 = (f32[8,256]{1,0:T(8,128)}, f32[8,256]{1,0:T(8,128)S(1)}, u32[]{:S(2)}) copy-start(f32[8,256]{1,0:T(8,128)S(1)} %reshape.465.vec) | copy-start | bytes 24580
  359.4 5.8 copy-start.9
  360.3 18.5 %all-to-all-start.4 = ((bf16[32,8,896]{2,1,0:T(8,128)(2,1)}), bf16[32,8,896]{2,1,0:T(8,128)(2,1)S(1)}, u32[]{:S(2)}, u32[]{:S(2)}) async-start(bf16[32,8,896]{2,1,0:T(8,128)(2,1)} %bitcast.19), calls=%async_computation.4 | async-start | bytes 917504 | tf_op jit(solution)/shard_map/all_to_all | solution.py:547
  365.3 4.1 copy-start.21
  365.3 4.1 copy-start.22
  365.4 4.2 copy-start.13
  378.8 42.1 %copy-start.6 = (f32[3,128,768]{2,1,0:T(8,128)S(1)}, f32[3,128,768]{2,1,0:T(8,128)}, u32[]{:S(2)}) copy-start(f32[3,128,768]{2,1,0:T(8,128)} %param.30) | copy-start | bytes 3538948
  378.8 45.6 %all-to-all-start.5 = ((bf16[32,8,2432]{2,1,0:T(8,128)(2,1)}), bf16[32,8,2432]{2,1,0:T(8,128)(2,1)S(1)}, u32[]{:S(2)}, u32[]{:S(2)}) async-start(bf16[32,8,2432]{2,1,0:T(8,128)(2,1)} %bitcast.26), calls=%async_computation.5 | async-start | bytes 2490368 | tf_op jit(solution)/shard_map/all_to_all | solution.py:547
  421.7 1.5 copy-start.10
  424.4 50.5 %all-to-all-start.3 = ((bf16[16,256,256]{2,1,0:T(8,128)(2,1)}), bf16[16,256,256]{2,1,0:T(8,128)(2,1)S(1)}, u32[]{:S(2)}, u32[]{:S(2)}) async-start(bf16[16,256,256]{2,1,0:T(8,128)(2,1)} %bitcast.187), calls=%async_computation.3 | async-start | bytes 4194304 | tf_op jit(solution)/shard_map/all_to_all | solution.py:594
  431.2 192.3 %all-gather.2.cloned.1.call-start = ((), (), s32[]{:S(2)}) async-start(), calls=%async_computation.6 | async-start | bytes 1323008 | tf_op jit(solution)/shard_map/all_gather | solution.py:549
  474.8 1.4 copy-start
  474.8 16.8 %copy-start.11 = (f32[1,1,128,768]{3,1,2,0:T(1,128)S(1)}, f32[1,1,128,768]{3,1,2,0:T(1,128)}, u32[]{:S(2)}) copy-start(f32[1,1,128,768]{3,1,2,0:T(1,128)} %copy.57) | copy-start | bytes 1179652
  476.2 81.7 %all-to-all-start.2 = ((bf16[16,256,256]{2,1,0:T(8,128)(2,1)}), bf16[16,256,256]{2,1,0:T(8,128)(2,1)}, u32[]{:S(2)}, u32[]{:S(2)}) async-start(bf16[16,256,256]{2,1,0:T(8,128)(2,1)} %bitcast.186), calls=%async_computation.2 | async-start | bytes 4194304 | tf_op jit(solution)/shard_map/all_to_all | solution.py:594
  557.9 65.6 %copy-start.14 = (f32[3,128,256]{2,1,0:T(8,128)S(1)}, f32[3,128,256]{2,1,0:T(8,128)}, u32[]{:S(2)}) copy-start(f32[3,128,256]{2,1,0:T(8,128)} %param.31) | copy-start | bytes 1179652
  624.8 1.6 copy-start.1
  633.6 1.9 copy-start.2
  633.6 1.9 copy-start.3
  633.6 1.9 copy-start.4
  635.5 7.4 %copy-start.25 = (f32[3,512]{1,0:T(4,128)S(1)}, f32[3,512]{1,0:T(4,128)}, u32[]{:S(2)}) copy-start(f32[3,512]{1,0:T(4,128)} %param.34) | copy-start | bytes 18436
  (6 other events, 6.2 us)
Sparse Core Ops, SparseCore 0:
  436.2 54.2 all-gather.1

commit v2 on v1

--- a/solution.py
+++ b/solution.py
@@ -257,7 +257,7 @@
 
 def middle_kernel(
     scal, table, x, cot, ctx, w_out, w_up, w_down, up_shift, vec,
-    out_o, gz1_o, gctx_o, delta_o, gdown_o, gup_o, gout_o, gub_o, gvec_o, act, slope,
+    out_o, gz1_o, gctx_o, delta_o, pack0, pack1, pack2, pack3, gdown_o, gup_o, gout_o, gub_o, gvec_o, act, slope,
 ):
     step = pl.program_id(0)
     rows = x.shape[0]
@@ -331,6 +331,30 @@
         part = sums[0:4, n * BLOCK : (n + 1) * BLOCK]
         delta_o[n : n + 1, :] = jnp.concatenate([part[h : h + 1, :] for h in range(4)], axis=1)
 
+    @pl.when(step == pl.num_programs(0) - 1)
+    def _():
+        for r, pack in enumerate((pack0, pack1, pack2, pack3)):
+            piece = scal[1] ^ r
+            shard, core = piece // 2, piece % 2
+            here = pl.ds(pl.multiple_of(piece * 64, 64), 64)
+            pack[:, 0:1024] = gup_o[here, :].astype(LOW)
+            pack[:, 1024:1280] = gout_o[here, :].astype(LOW)
+            for g in range(4):
+                at = pl.ds(pl.multiple_of(shard * 512 + g * 128 + core * 64, 64), 64)
+                pack[:, 1280 + 256 * g : 1536 + 256 * g] = gdown_o[at, :].astype(LOW)
+            lines = [gub_o[:, pl.ds(pl.multiple_of(shard * 512 + 128 * n, 128), 128)] for n in range(4)]
+            first = shard == 0
+            for n in range(4):
+                line = jnp.where(first, gvec_o[n : n + 1, :], gvec_o[4 + n : 5 + n, :])
+                lines += [line[:, 0:128], line[:, 128:256]]
+            put_extra(pack, 2304, lines, core)
+
+
+def put_extra(pack, at, lines, core):
+    some = jnp.concatenate(lines + [jnp.zeros((16 - len(lines), HALF), F32)], axis=0)
+    pack[0:16, at : at + HALF] = jnp.where(core == 0, some, 0.0).astype(LOW)
+    pack[16:64, at : at + HALF] = jnp.zeros((48, HALF), LOW)
+
 
 def middle(scal, table, x, cot, ctx, w_out, w_up, w_down, up_shift, vec):
     length = x.shape[0]
@@ -352,15 +376,18 @@
             ],
             out_specs=[
                 wide, wide, wide, pl.BlockSpec((rows // BLOCK, 256), lambda i, s: (i, 0)),
-                whole(1024, 256), whole(256, 1024), whole(256, 256), whole(1, 1024), whole(8, 256),
+                whole(64, 2432), whole(64, 2432), whole(64, 2432), whole(64, 2432),
             ],
-            scratch_shapes=[pltpu.VMEM((rows, 1024), LOW), pltpu.VMEM((rows, 1024), F32)],
+            scratch_shapes=[
+                pltpu.VMEM((1024, 256), F32), pltpu.VMEM((256, 1024), F32), pltpu.VMEM((256, 256), F32),
+                pltpu.VMEM((1, 1024), F32), pltpu.VMEM((8, 256), F32),
+                pltpu.VMEM((rows, 1024), LOW), pltpu.VMEM((rows, 1024), F32),
+            ],
         ),
         out_shape=(
             shape((length, 256), LOW), shape((length, 256), F32), shape((length, 256), LOW),
-            shape((length // BLOCK, 256), F32), shape((1024, 256), F32), shape((256, 1024), F32),
-            shape((256, 256), F32), shape((1, 1024), F32), shape((8, 256), F32),
-        ),
+            shape((length // BLOCK, 256), F32),
+        ) + (shape((64, 2432), LOW),) * 4,
         compiler_params=pltpu.CompilerParams(vmem_limit_bytes=VMEM_LIMIT),
         cost_estimate=pl.CostEstimate(flops=16_000_000_000, bytes_accessed=20_000_000, transcendentals=10_000_000),
         name="middle",
@@ -369,7 +396,7 @@
 
 def backward_kernel(
     scal, drawn, table, q, k, v, gctx, lse, delta, gz1, x, w,
-    gin_o, gw_o, gs_o, picks, kg, vg, dq, dk, dv,
+    gin_o, pack0, pack1, pack2, pack3, picks, kg, vg, dq, dk, dv, gw_o,
 ):
     length = x.shape[0]
     blocks = length // BLOCK
@@ -459,7 +486,16 @@
         gw_o[...] += dot_tn(x[rows, :], dqkv)
         return shifts + jnp.sum(dqkv.astype(F32), axis=0, keepdims=True)
 
-    gs_o[...] = lax.fori_loop(0, length // 512, finish, jnp.zeros((1, 768), F32))
+    shifts = lax.fori_loop(0, length // 512, finish, jnp.zeros((1, 768), F32))
+    for r, pack in enumerate((pack0, pack1, pack2, pack3)):
+        piece = scal[1] ^ r
+        core = piece % 2
+        pack[:, 0:768] = gw_o[pl.ds(pl.multiple_of(piece * 64, 64), 64), :].astype(LOW)
+        mine = jnp.where(piece // 2 == 0, shifts, 0.0)
+        lines = [jnp.zeros((4, HALF), F32)] + [mine[:, a : a + HALF] for a in (0, 128, 512, 640)]
+        lines += [jnp.zeros((8, HALF), F32)]
+        pack[:, 768:896] = jnp.zeros((64, HALF), LOW)
+        pack[0:16, 768:896] = jnp.where(core == 0, jnp.concatenate(lines, axis=0), 0.0).astype(LOW)
 
 
 def backward_attention(scal, drawn, table, q, k, v, gctx, lse, delta, gz1, x, w):
@@ -467,9 +503,9 @@
     shape = jax.ShapeDtypeStruct
     return pl.pallas_call(
         backward_kernel,
-        out_shape=(shape((length, 256), LOW), shape((256, 768), F32), shape((1, 768), F32)),
+        out_shape=(shape((length, 256), LOW),) + (shape((64, 896), LOW),) * 4,
         in_specs=[smem(), smem()] + [vmem()] * 10,
-        out_specs=[vmem()] * 3,
+        out_specs=[vmem()] * 5,
         scratch_shapes=[
             pltpu.VMEM((256, 256), LOW),
             pltpu.VMEM((2, 512, 256), LOW),
@@ -477,6 +513,7 @@
             pltpu.VMEM((length, 256), LOW),
             pltpu.VMEM((length, 256), F32),
             pltpu.VMEM((length, 256), F32),
+            pltpu.VMEM((256, 768), F32),
         ],
         compiler_params=pltpu.CompilerParams(vmem_limit_bytes=VMEM_LIMIT),
         cost_estimate=pl.CostEstimate(flops=40_000_000_000, bytes_accessed=20_000_000, transcendentals=10_000_000),
@@ -489,38 +526,62 @@
     return jnp.broadcast_to(column[:, :, None], (3, BLOCK, HALF))
 
 
-def reorder_kernel(scatter, order, src, dst, sems):
+def reorder_kernel(scatter, order, src, *rest):
+    *_, dst, held, arrived, left = rest
     count = src.shape[0]
-    copies = []
+    loads, stores = [], []
     for j in range(count):
         one = order[j]
-        if scatter:
-            copies.append(pltpu.make_async_copy(src.at[j], dst.at[one], sems.at[j]))
-        else:
-            copies.append(pltpu.make_async_copy(src.at[one], dst.at[j], sems.at[j]))
-        copies[-1].start()
-    for copy in copies:
-        copy.wait()
-
-
-def reorder(order, src, scatter):
+        loads.append(pltpu.make_async_copy(src.at[j if scatter else one], held.at[j], arrived.at[j]))
+        stores.append(pltpu.make_async_copy(held.at[j], dst.at[one if scatter else j], left.at[j]))
+        loads[-1].start()
+    for load, store in zip(loads, stores):
+        load.wait()
+        store.start()
+    for store in stores:
+        store.wait()
+
+
+def reorder(order, src, scatter, after=()):
     return pl.pallas_call(
         functools.partial(reorder_kernel, scatter),
         out_shape=jax.ShapeDtypeStruct(src.shape, src.dtype),
-        in_specs=[smem(), pl.BlockSpec(memory_space=pl.ANY)],
+        in_specs=[smem()] + [pl.BlockSpec(memory_space=pl.ANY)] * (1 + len(after)),
         out_specs=pl.BlockSpec(memory_space=pl.ANY),
-        scratch_shapes=[pltpu.SemaphoreType.DMA((src.shape[0],))],
-        cost_estimate=pl.CostEstimate(flops=0, bytes_accessed=2 * src.size * 2, transcendentals=0),
+        scratch_shapes=[
+            pltpu.VMEM(src.shape, src.dtype),
+            pltpu.SemaphoreType.DMA((src.shape[0],)),
+            pltpu.SemaphoreType.DMA((src.shape[0],)),
+        ],
+        cost_estimate=pl.CostEstimate(flops=0, bytes_accessed=4 * src.size, transcendentals=0),
         name="reorder",
-    )(order, src)
-
-
-def exchange_weights(shard_index, parts):
+    )(order, src, *after)
+
+
+def hold(values, after):
+    count = len(values)
+    anywhere = pl.BlockSpec(memory_space=pl.ANY)
+    return pl.pallas_call(
+        lambda *refs: None,
+        out_shape=tuple(jax.ShapeDtypeStruct(v.shape, v.dtype) for v in values),
+        in_specs=[anywhere] * (count + len(after)),
+        out_specs=(anywhere,) * count,
+        input_output_aliases={n: n for n in range(count)},
+        name="hold",
+    )(*values, *after)
+
+
+def pack_weights(parts):
     w_qkv, w_out, w_up, w_down, up_bias, vectors = parts
     rows = w_qkv.shape[0]
     down = w_down.reshape(4, rows, -1)
     pack = jnp.concatenate([w_qkv, w_out, w_up] + [down[n] for n in range(4)], axis=1)
     small = jnp.concatenate([up_bias.reshape(-1, 256), vectors], axis=0)
+    return pack, small
+
+
+def exchange_weights(shard_index, pack, small):
+    rows = pack.shape[0]
     swap = [(0, 1), (1, 0)]
     other, other_small = lax.ppermute(pack, "shard", swap), lax.ppermute(small, "shard", swap)
     first = shard_index == 0
@@ -539,14 +600,45 @@
     return cols(0, 768), cols(768, 1024), cols(1024, 2048), full_down, full_bias, full_vec
 
 
-def sum_over_devices(pack):
-    shards, rows, columns = pack.shape
+def trade(pieces):
     count = lax.axis_size("dp")
-    pieces = jnp.transpose(pack.reshape(shards, count, rows // count, columns), (1, 0, 2, 3))
-    pieces = pieces.reshape(count * shards, rows // count, columns)
-    got = lax.all_to_all(pieces, ("dp", "shard"), split_axis=0, concat_axis=0, tiled=True)
-    mine = jnp.sum(got.astype(F32), axis=0)
-    return lax.all_gather(mine, "dp", axis=0, tiled=True)
+    held = [pieces[0]]
+    for n in (1, 2, 3):
+        pairs = [(d * 2 + s, (d ^ (n % 2)) * 2 + (s ^ (n // 2))) for d in range(count) for s in range(2)]
+        held.append(lax.ppermute(pieces[n], ("dp", "shard"), pairs))
+    return held
+
+
+def total(pieces):
+    return sum(piece.astype(F32) for piece in pieces)
+
+
+def sum_rest(part, data_index):
+    count = lax.axis_size("dp")
+    groups = count // 4
+    half = part.shape[0] // 2
+    bit = (data_index // 2) % 2
+    flip = [(d, d ^ 2) for d in range(count)]
+    keep = lax.dynamic_slice_in_dim(part, bit * half, half, 0)
+    give = lax.dynamic_slice_in_dim(part, (1 - bit) * half, half, 0)
+    part = keep + lax.ppermute(give.astype(LOW), "dp", flip).astype(F32)
+    at = data_index // 4
+    small = half // groups
+    hops = [[(d, (d + 4 * k) % count) for d in range(count)] for k in range(1, groups)]
+
+    def piece(k):
+        return lax.dynamic_slice_in_dim(part, lax.rem(at + k, groups) * small, small, 0)
+
+    mine = piece(0)
+    got = [lax.ppermute(piece(k + 1).astype(LOW), "dp", hop) for k, hop in enumerate(hops)]
+    for one in got:
+        mine = mine + one.astype(F32)
+    mine = mine.astype(LOW)
+    near = jnp.stack([mine] + [lax.ppermute(mine, "dp", hop) for hop in hops])
+    core = [(d, d ^ 1) for d in range(count)]
+    across = lax.ppermute(near, "dp", flip)
+    near_core, across_core = lax.ppermute(near, "dp", core), lax.ppermute(across, "dp", core)
+    return jnp.stack([near, across, near_core, across_core]).astype(F32)
 
 
 def adam_update(grad, state, decay):
@@ -557,6 +649,71 @@
     direction = first_new / correct_one / (jnp.sqrt(second_new / correct_two) + ADAM_EPSILON)
     master_new = state[0] - LEARNING_RATE * (direction + decay * state[0])
     return (master_new, first_new, second_new)
+
+
+def update_kernel(
+    where, parts, s_qkv, s_out, s_up, s_down, s_bias, s_vec,
+    g_qkv, g_out, g_up, g_down, g_bias, g_vec, o_master, o_first, o_second, grads,
+):
+    groups, small = parts.shape[1:3]
+    index = where[0]
+    for core in range(2):
+        for side in range(2):
+            base = ((index % 2) ^ core) * 64 + (((index // 2) % 2) ^ side) * 32
+            for k in range(groups):
+                at = base + lax.rem(index // 4 + groups - k, groups) * small
+                grads[pl.ds(pl.multiple_of(at, small), small), :] = parts[2 * core + side, k]
+    outs = (o_master, o_first, o_second)
+
+    def place(base, grad, state, decay):
+        rows, columns = grad.shape
+        wide = columns // HALF
+        for out, value in zip(outs, adam_update(grad, state, decay)):
+            for c in range(wide):
+                at = pl.ds(base + c, rows, stride=wide) if wide > 1 else pl.ds(base, rows)
+                out[at, :] = value[:, c * HALF : (c + 1) * HALF]
+
+    qkv, outer, up = grads[:, 2304:3072], grads[:, 1024:1280], grads[:, 0:1024]
+    g_qkv[...] = qkv
+    g_out[...] = outer
+    g_up[...] = up
+    place(0, qkv, s_qkv, WEIGHT_DECAY)
+    place(768, outer, s_out, WEIGHT_DECAY)
+    place(1024, up, s_up, WEIGHT_DECAY)
+    for n in range(4):
+        rows = slice(128 * n, 128 * n + 128)
+        down = grads[:, 1280 + 256 * n : 1536 + 256 * n]
+        g_down[rows, :] = down
+        place(2048 + 256 * n, down, s_down[:, rows, :], WEIGHT_DECAY)
+    extra = grads[0:16, 3072:3200]
+    g_bias[...] = extra[0:4]
+    place(3072, extra[0:4], s_bias, 0.0)
+    vec = jnp.concatenate(
+        [jnp.concatenate([extra[4 + 2 * n : 5 + 2 * n], extra[5 + 2 * n : 6 + 2 * n]], axis=1) for n in range(4)], axis=0
+    )
+    g_vec[...] = vec
+    place(3076, vec, s_vec, 0.0)
+
+
+def update(data_index, parts, states):
+    shape = lambda *dims: jax.ShapeDtypeStruct(dims, F32)
+    s_qkv, s_out, s_up, s_down, s_bias, s_vec = states
+    flat = shape(3084, HALF)
+    *grads, master, first, second = pl.pallas_call(
+        update_kernel,
+        out_shape=(
+            shape(128, 768), shape(128, 256), shape(128, 1024), shape(512, 256), shape(4, HALF), shape(4, 256),
+            flat, flat, flat,
+        ),
+        in_specs=[smem()] + [vmem()] * 7,
+        out_specs=[vmem()] * 9,
+        scratch_shapes=[pltpu.VMEM((128, 3200), F32)],
+        compiler_params=pltpu.CompilerParams(vmem_limit_bytes=VMEM_LIMIT),
+        cost_estimate=pl.CostEstimate(flops=10_000_000, bytes_accessed=14_000_000, transcendentals=400_000),
+        name="update",
+    )(data_index.reshape(1), parts, s_qkv, s_out, s_up, s_down, s_bias.reshape(3, 4, HALF), s_vec)
+    grads[4] = grads[4].reshape(-1)
+    return tuple(grads) + tuple(row.reshape(1, -1) for row in (master, first, second))
 
 
 def on_device(
@@ -568,63 +725,53 @@
     data_index = lax.axis_index("dp")
     row_seqs, rows_here, width = hidden.shape
     length = row_seqs * rows_here
+    pack, small = pack_weights((w_qkv, w_out, w_up, w_down, up_bias, vectors))
+    pack, small, assign = lax.optimization_barrier((pack, small, assign))
     order = lax.dynamic_index_in_dim(assign.reshape(row_seqs, shard_count), shard_index, 1, keepdims=False)
+
+    def to_slot(rows):
+        return lax.all_to_all(rows, "dp", split_axis=0, concat_axis=0, tiled=True).reshape(length, width)
+
+    x = to_slot(reorder(order, hidden, False))
     own = shard_index * row_seqs + lax.dynamic_index_in_dim(order, data_index, 0, keepdims=False)
-    live = lax.dynamic_slice_in_dim(live_blocks, own, 1)
+    live = lax.dynamic_index_in_dim(live_blocks, own, 0, keepdims=False)
+    scal = jnp.stack([live, 2 * shard_index + data_index % 2])
     tail = lax.dynamic_index_in_dim(tail_live, own, 0, keepdims=False)
-
-    def to_slot(rows):
-        return lax.all_to_all(rows, "dp", split_axis=0, concat_axis=0, tiled=True)
-
-    x = to_slot(reorder(order, hidden, False)).reshape(length, width)
-    cot = to_slot(reorder(order, cotangent, False)).reshape(length, width)
-    w_qkv, w_out, w_up, w_down, up_bias, vectors = exchange_weights(
-        shard_index, (w_qkv, w_out, w_up, w_down, up_bias, vectors)
-    )
+    w_qkv, w_out, w_up, w_down, up_bias, vectors = exchange_weights(shard_index, pack, small)
     vec = vectors.astype(F32)
     shift = jnp.concatenate([vec[0], jnp.zeros_like(vec[0]), vec[1]])[None]
+    up_shift = up_bias.astype(F32)[None]
     table = bias_table(tail)
     drawn = random_blocks.reshape(-1)
-    q, k, v, ctx, lse = forward_attention(live, drawn, table, x, w_qkv, shift)
-    out, gz1, gctx, delta, gdown, gup, gout, gub, gvec = middle(
-        live, table, x, cot, ctx, w_out, w_up, w_down, up_bias.astype(F32)[None], vec
+    ready = (w_qkv, w_out, w_up, w_down, up_shift, vec, shift, table)
+    cot = to_slot(reorder(order, cotangent, False, ready))
+    q, k, v, ctx, lse = forward_attention(scal, drawn, table, x, w_qkv, shift)
+    out, gz1, gctx, delta, *early = middle(
+        scal, table, x, cot, ctx, w_out, w_up, w_down, up_shift, vec
     )
 
     def from_slot(rows):
-        back = lax.all_to_all(
+        return lax.all_to_all(
             rows.reshape(row_seqs, rows_here, width), "dp", split_axis=0, concat_axis=0, tiled=True
         )
-        return reorder(order, back, True)
-
-    layer_out = from_slot(out)
-    half = gup.shape[0] // 2
-
-    def extra(*pieces):
-        block = jnp.concatenate([piece.reshape(shard_count, -1, HALF) for piece in pieces], axis=1)
-        return jnp.pad(block, ((0, 0), (0, half - block.shape[1]), (0, 0)))
-
-    down = jnp.transpose(gdown.reshape(2, 4, half, 256), (0, 2, 1, 3)).reshape(2, half, 1024)
-    early = jnp.concatenate(
-        [gup.reshape(2, half, 1024), gout.reshape(2, half, 256), down, extra(gub, gvec)], axis=2
-    ).astype(LOW)
-    early = sum_over_devices(early)
-    gin, gw, gs = backward_attention(live, drawn, table, q, k, v, gctx, lse, delta, gz1, x, w_qkv)
-    input_grad = from_slot(gin)
-    ends = jnp.concatenate([gs[:, :256], gs[:, 512:], jnp.zeros((6, 256), F32)])
-    late = jnp.concatenate([gw.reshape(2, half, 768), extra(ends)], axis=2).astype(LOW)
-    late = sum_over_devices(late)
-    grad_qkv = late[:, :768]
-    grad_up = early[:, :1024]
-    grad_out = early[:, 1024:1280]
-    grad_down = jnp.concatenate([early[:, 1280 + 256 * n : 1536 + 256 * n] for n in range(4)], axis=0)
-    grad_ubias = early[0:4, 2304:].reshape(-1)
-    grad_vec = early[4:12, 2304:].reshape(4, 256) + late[0:8, 768:].reshape(4, 256)
-    grads = (grad_qkv, grad_out, grad_up, grad_down, grad_ubias, grad_vec)
-    states = (state_qkv, state_out, state_up, state_down, state_ubias, state_vec)
-    decays = (WEIGHT_DECAY, WEIGHT_DECAY, WEIGHT_DECAY, WEIGHT_DECAY, 0.0, 0.0)
-    updated = [adam_update(*group) for group in zip(grads, states, decays)]
-    rows = [jnp.concatenate([entry[n].reshape(1, -1) for entry in updated], axis=1) for n in range(3)]
-    return (layer_out, input_grad) + grads + tuple(rows)
+
+    back_out = from_slot(out)
+    early = trade(early)
+    gin, *late = backward_attention(scal, drawn, table, q, k, v, gctx, lse, delta, gz1, x, w_qkv)
+    gin, *late = hold((gin, *late), (back_out, *early[1:]))
+    back_gin = from_slot(gin)
+
+    def sum_all(early, late):
+        early, late = total(early), total(trade(late))
+        sums = jnp.concatenate([early[:, :2304], late[:, :768], early[:, 2304:] + late[:, 768:]], axis=1)
+        return sum_rest(sums, data_index)
+
+    made = jax.eval_shape(sum_all, early, late)
+    parts = lax.cond(live_blocks[0] > 0, sum_all, lambda *unused: jnp.zeros(made.shape, made.dtype), early, late)
+    layer_out = reorder(order, back_out, True)
+    updated = update(data_index, parts, (state_qkv, state_out, state_up, state_down, state_ubias, state_vec))
+    input_grad = reorder(order, back_gin, True)
+    return (layer_out, input_grad) + updated
 
 
 def solution(mesh):

time: 652 us -> 374 us (0.57)
  Pallas kernels: 438 us -> 196 us
  blocking collectives: 37.8 us -> 0 us
  waiting for transfers between devices: 59.9 us -> 78.8 us
  between operations: 15.4 us -> 2.3 us
  other arithmetic: 19.3 us -> 10.1 us
    pallas_call x4, Pallas kernels: 262 us -> 12.9 us  [reorder(): pl.pallas_call(functools.partial(reorder_kernel, scatter), out_shape=jax....]
    ppermute x0 -> x16, waiting for transfers between devices: none -> 51.4 us  [the longest x3 25.3 us: sum_rest(): lax.ppermute(piece(k + 1).astype(LOW), 'dp', hop)]
    all_to_all x2, waiting for transfers between devices: 38.8 us -> 0.01 us  [from_slot(): lax.all_to_all(rows.reshape(row_seqs, rows_here, width), 'dp', split_axis...]
    all_gather x1 -> x0, blocking collectives: 37.8 us -> none  [sum_over_devices(): return lax.all_gather(mine, 'dp', axis=0, tiled=True)]
    ppermute x0 -> x16, starting transfers between devices: none -> 15.3 us  [the longest x3 3.88 us: sum_rest(): near = jnp.stack([mine] + [lax.ppermute(mine, 'dp', hop) for hop in hops])]
    reshape x4 -> x3, local copies, waits for them, and re-layouts: 0.45 us -> 10.8 us  [the longest x1 9.5 us: update(): row.reshape(1, -1)]
    all_to_all x2, starting transfers between devices: 22.3 us -> 12 us  [from_slot(): lax.all_to_all(rows.reshape(row_seqs, rows_here, width), 'dp', split_axis...]
    unnamed x10 -> x0, other arithmetic: 9.64 us -> none
  transfers between devices with their start and end apart: 9 -> 22, of which waited for: 3 -> 11; matrix products, arithmetic and copies ran while one was open for 4% -> 9% of each run, Pallas kernels for 39% -> 39%
where the time goes in v2:
time: 374 us; the launch traced here: 373 us
  Pallas kernels  196 us (52%)
  waiting for transfers between devices  78.8 us (21%)
  starting transfers between devices  48.1 us (13%)
  local copies, waits for them, and re-layouts  37.9 us (10%)
  other arithmetic  10.1 us (3%)
    pallas_call x1, Pallas kernels, backward_attention(): pl.pallas_call(backward_kernel, out_shape=(shape((length, 256), LOW),) +...  75.9 us
    pallas_call x1, Pallas kernels, forward_attention(): pl.pallas_call(forward_kernel, out_shape=(rows, rows, rows, rows, jax.Sha...  57.5 us
    pallas_call x1, Pallas kernels, middle(): pl.pallas_call(middle_kernel, grid_spec=pltpu.PrefetchScalarGridSpec(num_...  42.3 us
    ppermute x3, waiting for transfers between devices, sum_rest(): lax.ppermute(piece(k + 1).astype(LOW), 'dp', hop)  25.3 us
    unnamed x24, local copies, waits for them, and re-layouts  19.9 us
    all_to_all x2, starting transfers between devices, to_slot(): lax.all_to_all(rows, 'dp', split_axis=0, concat_axis=0, tiled=True)  18.7 us
    ppermute x1, waiting for transfers between devices, exchange_weights(): lax.ppermute(pack, 'shard', swap)  15.8 us
    pallas_call x4, Pallas kernels, reorder(): pl.pallas_call(functools.partial(reorder_kernel, scatter), out_shape=jax....  12.9 us
  transfers between devices with their start and end apart: 22, of which 11 were waited for; matrix products, arithmetic and copies ran while one was open for 9% of the time, Pallas kernels for 39%

profile of v2, /device:TPU:0, one launch (start us, length us, event | category | flops | bytes accessed | tf_op | source)
XLA Modules:
  0.0 373.1 jit_solution(3927853387001995396)
XLA Ops:
  9.7 3.2 reorder.4
  12.9 7.4 %all-to-all-start = ((bf16[16,256,256]{2,1,0:T(8,128)(2,1)}), bf16[16,256,256]{2,1,0:T(8,128)(2,1)}, u32[]{:S(2)}, u32[]{:S(2)}) async-start(bf16[16,256,256]{2,1,0:T(8,128)(2,1)} %reorder.4), calls=%async_computation | async-start | bytes 4194304 | tf_op jit(solution)/shard_map/all_to_all | solution.py:733
  20.4 1.6 collective-permute-start.14
  25.7 15.8 %collective-permute-done.13 = bf16[128,3072]{1,0:T(8,128)(2,1)} collective-permute-done((bf16[128,3072]{1,0:T(8,128)(2,1)S(1)}, bf16[128,3072]{1,0:T(8,128)(2,1)}, u32[]{:S(2)}, u32[]{:S(2)}) %collective-permute-start.13) | collective-permute-done | bytes 786464 | tf_op jit(solution)/shard_map/ppermute | solution.py:586
  46.7 3.2 reorder.5
  49.9 11.6 %all-to-all-done = bf16[16,256,256]{2,1,0:T(8,128)(2,1)} async-done(((bf16[16,256,256]{2,1,0:T(8,128)(2,1)}), bf16[16,256,256]{2,1,0:T(8,128)(2,1)}, u32[]{:S(2)}, u32[]{:S(2)}) %all-to-all-start) | async-done | bytes 2097184 | tf_op jit(solution)/shard_map/all_to_all | solution.py:733
  61.6 11.2 %all-to-all-start.1 = ((bf16[16,256,256]{2,1,0:T(8,128)(2,1)}), bf16[16,256,256]{2,1,0:T(8,128)(2,1)S(1)}, u32[]{:S(2)}, u32[]{:S(2)}) async-start(bf16[16,256,256]{2,1,0:T(8,128)(2,1)} %reorder.5), calls=%async_computation.1 | async-start | bytes 4194304 | tf_op jit(solution)/shard_map/all_to_all | solution.py:733
  75.6 57.5 %attend_forward.1 = (bf16[4096,256]{1,0:T(8,128)(2,1)}, bf16[4096,256]{1,0:T(8,128)(2,1)}, bf16[4096,256]{1,0:T(8,128)(2,1)}, bf16[4096,256]{1,0:T(8,128)(2,1)}, f32[64,256]{1,0:T(8,128)}) custom-call(s32[2]{0:T(128)} %pad_add_fusion.scal, s32[768]{0:T(1024)} %reshape.117.drawn, f32[3,64,128]{2,1,0:T(8,128)} %broadcast_in_dim.20.rest_7_.table, ...), custom_call_target="tpu_custom_call" | custom-call | flops 16000000000 | bytes 12000000 | tf_op jit(solution)/shard_map/attend_forward/pallas_call | solution.py:214
  134.4 42.3 %middle.1 = (bf16[4096,256]{1,0:T(8,128)(2,1)}, f32[4096,256]{1,0:T(8,128)}, bf16[4096,256]{1,0:T(8,128)(2,1)}, f32[64,256]{1,0:T(8,128)}, bf16[64,2432]{1,0:T(8...) custom-call(s32[2]{0:T(128)} %pad_add_fusion.scal, ...), custom_call_target="tpu_custom_call" | custom-call | flops 16000000000 | bytes 20000000 | tf_op jit(solution)/shard_map/middle/pallas_call | solution.py:368
  176.8 6.0 %all-to-all-start.2 = ((bf16[16,256,256]{2,1,0:T(8,128)(2,1)}), bf16[16,256,256]{2,1,0:T(8,128)(2,1)S(1)}, u32[]{:S(2)}, u32[]{:S(2)}) async-start(bf16[16,256,256]{2,1,0:T(8,128)(2,1)} %bitcast.56), calls=%async_computation.2 | async-start | bytes 4194304 | tf_op jit(solution)/shard_map/all_to_all | solution.py:754
  184.4 1.5 collective-permute-start.16
  185.9 75.9 %attend_backward.1 = (bf16[4096,256]{1,0:T(8,128)(2,1)}, bf16[64,896]{1,0:T(8,128)(2,1)S(1)}, bf16[64,896]{1,0:T(8,128)(2,1)}, bf16[64,896]{1,0:T(8,128)(2,1)}, bf16[64,896]{1,0:T(8,128)(2,1)}) custom-call(s32[2]{0:T(128)} %pad_add_fusion.scal, s32[768]{0:T(1024)} %reshape.117.drawn, f32[3,64,128]{2,1,0:T(8,128)} %broadcast_in_dim.20.rest_7_.table, ...), custom_call_target="tpu_custom_call" | custom-call | flops 40000000000 | bytes 20000000 | tf_op jit(solution)/shard_map/attend_backward/pallas_call | solution.py:504
  263.2 6.0 %all-to-all-start.3 = ((bf16[16,256,256]{2,1,0:T(8,128)(2,1)}), bf16[16,256,256]{2,1,0:T(8,128)(2,1)S(1)}, u32[]{:S(2)}, u32[]{:S(2)}) async-start(bf16[16,256,256]{2,1,0:T(8,128)(2,1)} %bitcast.53), calls=%async_computation.3 | async-start | bytes 4194304 | tf_op jit(solution)/shard_map/all_to_all | solution.py:754
  269.2 68.9 %conditional.1 = (f32[4,4,8,3200]{3,2,1,0:T(8,128)}) conditional(s32[]{:T(128)} %bitcast.26, () %tuple.16, (bf16[64,2432]{1,0:T(8,128)(2,1)}, bf16[64,2432]{1,0:T(8,128)(2,1)S(1)}, bf16[64,2432]{1,0:T(8,128)(2,1)S(1)}, bf16[64,2432]{1,0:T(8,128)(2,1)S(1)}, bf16[64,896]{1,0:T(8,128)(2,1)S(1)}, /*index=5*/bf16[64,896]{1,0:T(8,128)(2,1)}, ...), branch_computations={%region_0.1_spmd, %region_1.2_spmd} | conditional | flops 4238424 | bytes 18572810 | solution.py:770
  269.7 1.5 collective-permute-start.1
  272.5 3.3 collective-permute-done.1
  278.2 2.1 collective-permute-start.3
  280.3 12.5 %collective-permute-done.3 = bf16[32,3200]{1,0:T(8,128)(2,1)S(1)} collective-permute-done((bf16[32,3200]{1,0:T(8,128)(2,1)S(1)}, bf16[32,3200]{1,0:T(8,128)(2,1)S(1)}, u32[]{:S(2)}, u32[]{:S(2)}) %collective-permute-start.3) | collective-permute-done | bytes 204832 | tf_op jit(solution)/shard_map/cond/branch_1_fun/ppermute | solution.py:624
  292.9 2.1 collective-permute-start.5
  295.0 1.7 collective-permute-start.6
  296.7 13.0 %collective-permute-done.4 = bf16[8,3200]{1,0:T(8,128)(2,1)S(1)} collective-permute-done((bf16[8,3200]{1,0:T(8,128)(2,1)S(1)}, bf16[8,3200]{1,0:T(8,128)(2,1)S(1)}, u32[]{:S(2)}, u32[]{:S(2)}) %collective-permute-start.4) | collective-permute-done | bytes 51232 | tf_op jit(solution)/shard_map/cond/branch_1_fun/ppermute | solution.py:633
  309.7 12.3 %collective-permute-done.5 = bf16[8,3200]{1,0:T(8,128)(2,1)S(1)} collective-permute-done((bf16[8,3200]{1,0:T(8,128)(2,1)S(1)}, bf16[8,3200]{1,0:T(8,128)(2,1)S(1)}, u32[]{:S(2)}, u32[]{:S(2)}) %collective-permute-start.5) | collective-permute-done | bytes 51232 | tf_op jit(solution)/shard_map/cond/branch_1_fun/ppermute | solution.py:633
  323.3 1.5 collective-permute-start.8
  325.9 2.6 collective-permute-done.7
  329.5 1.6 collective-permute-start.10
  331.2 4.2 %collective-permute-done.10 = bf16[4,8,3200]{2,1,0:T(8,128)(2,1)S(1)} collective-permute-done((bf16[4,8,3200]{2,1,0:T(8,128)(2,1)S(1)}, bf16[4,8,3200]{2,1,0:T(8,128)(2,1)S(1)}, u32[]{:S(2)}, u32[]{:S(2)}) %collective-permute-start.10) | collective-permute-done | bytes 204832 | tf_op jit(solution)/shard_map/cond/branch_1_fun/ppermute | solution.py:639
  335.4 1.4 collective-permute-done.12
  338.1 7.0 %update.1 = (f32[128,768]{1,0:T(8,128)}, f32[128,256]{1,0:T(8,128)}, f32[128,1024]{1,0:T(8,128)}, f32[512,256]{1,0:T(8,128)}, f32[4,128]{1,0:T(4,128)}, /*index=...) custom-call(s32[1]{0:T(128)} %bitcast.25.where, ...), custom_call_target="tpu_custom_call" | custom-call | flops 10000000 | bytes 14000000 | tf_op jit(solution)/shard_map/update/pallas_call | solution.py:702
  345.1 9.5 %copy_bitcast_fusion = (f32[1,394752]{1,0:T(1,128)}, f32[1,394752]{1,0:T(1,128)}) fusion(f32[1,1,3084,128]{3,2,1,0:T(8,128)} %bitcast.63, f32[1,1,3084,128]{3,2,1,0:T(8,128)} %bitcast.62), kind=kLoop, calls=%fused_computation.19 | loop fusion | bytes 6316032 | tf_op jit(solution)/shard_map/reshape | solution.py:716
  354.6 10.5 %copy.45 = f32[1,1,3084,128]{3,1,2,0:T(1,128)} copy(f32[1,1,3084,128]{3,2,1,0:T(8,128)S(1)} %bitcast.61) | data formatting | bytes 3158016
  365.1 3.2 reorder.6
  369.7 3.2 reorder.7
  (92 shorter events, 33.9 us)
Async XLA Ops:
  12.9 48.6 %all-to-all-start = ((bf16[16,256,256]{2,1,0:T(8,128)(2,1)}), bf16[16,256,256]{2,1,0:T(8,128)(2,1)}, u32[]{:S(2)}, u32[]{:S(2)}) async-start(bf16[16,256,256]{2,1,0:T(8,128)(2,1)} %reorder.4), calls=%async_computation | async-start | bytes 4194304 | tf_op jit(solution)/shard_map/all_to_all | solution.py:733
  20.4 4.1 %collective-permute-start.14 = (bf16[6,256]{1,0:T(8,128)(2,1)S(1)}, bf16[6,256]{1,0:T(8,128)(2,1)S(1)}, u32[]{:S(2)}, u32[]{:S(2)}) collective-permute-start(bf16[6,256]{1,0:T(8,128)(2,1)S(1)} %pad_maximum_fusion.4), channel_id=1, source_target_pairs={{0,1},{1,0},{2,3},{3,2},{4,5},{5,4},{6,7},{7,6},{8,9},{9,8},{10,11... | collective-permute-start | bytes 9224 | tf_op jit(solution)/shard_map/ppermute | solution.py:586
  22.0 19.6 %collective-permute-start.13 = (bf16[128,3072]{1,0:T(8,128)(2,1)S(1)}, bf16[128,3072]{1,0:T(8,128)(2,1)}, u32[]{:S(2)}, u32[]{:S(2)}) collective-permute-start(bf16[128,3072]{1,0:T(8,128)(2,1)S(1)} %slice_dynamic-update-slice_fusion), channel_id=1, source_target_pairs={{0,1},{1,0},{2,3},{3,2},{4,5},{5,4},{6,7},{7,6},{8,9},{9,8},{10,11... | collective-permute-start | bytes 2359304 | tf_op jit(solution)/shard_map/ppermute | solution.py:586
  24.5 19.1 %copy-start.6 = (f32[8,256]{1,0:T(8,128)}, f32[8,256]{1,0:T(8,128)S(1)}, u32[]{:S(2)}) copy-start(f32[8,256]{1,0:T(8,128)S(1)} %reshape.127.rest_5_.vec) | copy-start | bytes 24580
  49.9 22.9 %copy-start.8 = (s32[1,4,64,3]{2,1,3,0:T(4,128)S(1)}, s32[1,4,64,3]{2,1,3,0:T(4,128)}, u32[]{:S(2)}) copy-start(s32[1,4,64,3]{2,1,3,0:T(4,128)} %param.25) | copy-start | bytes 9220
  49.9 23.8 %copy-start.9 = (s32[32]{0:T(128)S(1)}, s32[32]{0:T(128)}, u32[]{:S(2)}) copy-start(s32[32]{0:T(128)} %param.23) | copy-start | bytes 388
  61.6 71.6 %all-to-all-start.1 = ((bf16[16,256,256]{2,1,0:T(8,128)(2,1)}), bf16[16,256,256]{2,1,0:T(8,128)(2,1)S(1)}, u32[]{:S(2)}, u32[]{:S(2)}) async-start(bf16[16,256,256]{2,1,0:T(8,128)(2,1)} %reorder.5), calls=%async_computation.1 | async-start | bytes 4194304 | tf_op jit(solution)/shard_map/all_to_all | solution.py:733
  133.1 1.3 copy-start.2
  176.8 6.6 %copy-start.7 = (f32[3,512]{1,0:T(4,128)S(1)}, f32[3,512]{1,0:T(4,128)}, u32[]{:S(2)}) copy-start(f32[3,512]{1,0:T(4,128)} %param.36) | copy-start | bytes 18436
  176.8 85.1 %all-to-all-start.2 = ((bf16[16,256,256]{2,1,0:T(8,128)(2,1)}), bf16[16,256,256]{2,1,0:T(8,128)(2,1)S(1)}, u32[]{:S(2)}, u32[]{:S(2)}) async-start(bf16[16,256,256]{2,1,0:T(8,128)(2,1)} %bitcast.56), calls=%async_computation.2 | async-start | bytes 4194304 | tf_op jit(solution)/shard_map/all_to_all | solution.py:754
  184.0 77.8 %collective-permute-start.15 = (bf16[64,2432]{1,0:T(8,128)(2,1)}, bf16[64,2432]{1,0:T(8,128)(2,1)S(1)}, u32[]{:S(2)}, u32[]{:S(2)}) collective-permute-start(bf16[64,2432]{1,0:T(8,128)(2,1)} %get-tuple-element.93), channel_id=1, source_target_pairs={{0,2},{1,3},{2,0},{3,1},{4,6},{5,7},{6,4},{7,5},{8,10},{9,11},{10,... | collective-permute-start | bytes 933896 | tf_op jit(solution)/shard_map/ppermute | solution.py:608
  184.4 77.4 %collective-permute-start.16 = (bf16[64,2432]{1,0:T(8,128)(2,1)}, bf16[64,2432]{1,0:T(8,128)(2,1)S(1)}, u32[]{:S(2)}, u32[]{:S(2)}) collective-permute-start(bf16[64,2432]{1,0:T(8,128)(2,1)} %get-tuple-element.94), channel_id=1, source_target_pairs={{0,1},{1,0},{2,3},{3,2},{4,5},{5,4},{6,7},{7,6},{8,9},{9,8},{10,11... | collective-permute-start | bytes 933896 | tf_op jit(solution)/shard_map/ppermute | solution.py:608
  185.9 75.9 %collective-permute-start.17 = (bf16[64,2432]{1,0:T(8,128)(2,1)}, bf16[64,2432]{1,0:T(8,128)(2,1)S(1)}, u32[]{:S(2)}, u32[]{:S(2)}) collective-permute-start(bf16[64,2432]{1,0:T(8,128)(2,1)} %get-tuple-element.95), channel_id=1, source_target_pairs={{0,3},{1,2},{2,1},{3,0},{4,7},{5,6},{6,5},{7,4},{8,11},{9,10},{10,... | collective-permute-start | bytes 933896 | tf_op jit(solution)/shard_map/ppermute | solution.py:608
  261.8 1.3 copy-start
  263.2 105.2 %all-to-all-start.3 = ((bf16[16,256,256]{2,1,0:T(8,128)(2,1)}), bf16[16,256,256]{2,1,0:T(8,128)(2,1)S(1)}, u32[]{:S(2)}, u32[]{:S(2)}) async-start(bf16[16,256,256]{2,1,0:T(8,128)(2,1)} %bitcast.53), calls=%async_computation.3 | async-start | bytes 4194304 | tf_op jit(solution)/shard_map/all_to_all | solution.py:754
  269.2 2.0 copy-start.4
  269.2 2.0 copy-start.5
  269.2 3.3 collective-permute-start
  269.7 6.2 %collective-permute-start.1 = (bf16[64,896]{1,0:T(8,128)(2,1)}, bf16[64,896]{1,0:T(8,128)(2,1)}, u32[]{:S(2)}, u32[]{:S(2)}) collective-permute-start(bf16[64,896]{1,0:T(8,128)(2,1)} %get-tuple-element.27), channel_id=1, source_target_pairs={{0,1},{1,0},{2,3},{3,2},{4,5},{5,4},{6,7},{7,6},{8,9},{9,8},{10,11... | collective-permute-start | bytes 344072 | tf_op jit(solution)/shard_map/cond/branch_1_fun/ppermute | solution.py:608
  271.2 5.7 %collective-permute-start.2 = (bf16[64,896]{1,0:T(8,128)(2,1)}, bf16[64,896]{1,0:T(8,128)(2,1)}, u32[]{:S(2)}, u32[]{:S(2)}) collective-permute-start(bf16[64,896]{1,0:T(8,128)(2,1)} %get-tuple-element.28), channel_id=1, source_target_pairs={{0,3},{1,2},{2,1},{3,0},{4,7},{5,6},{6,5},{7,4},{8,11},{9,10},{10,... | collective-permute-start | bytes 344072 | tf_op jit(solution)/shard_map/cond/branch_1_fun/ppermute | solution.py:608
  278.2 14.5 %collective-permute-start.3 = (bf16[32,3200]{1,0:T(8,128)(2,1)S(1)}, bf16[32,3200]{1,0:T(8,128)(2,1)S(1)}, u32[]{:S(2)}, u32[]{:S(2)}) collective-permute-start(bf16[32,3200]{1,0:T(8,128)(2,1)S(1)} %dynamic-slice_convert_fusion), channel_id=1, source_target_pairs={{0,4},{2,6},{4,0},{6,2},{8,12},{10,14},{12,8},{14,10},{16,20},{18,... | collective-permute-start | bytes 614408 | tf_op jit(solution)/shard_map/cond/branch_1_fun/ppermute | solution.py:624
  292.8 16.9 %collective-permute-start.4 = (bf16[8,3200]{1,0:T(8,128)(2,1)S(1)}, bf16[8,3200]{1,0:T(8,128)(2,1)S(1)}, u32[]{:S(2)}, u32[]{:S(2)}) collective-permute-start(bf16[8,3200]{1,0:T(8,128)(2,1)S(1)} %get-tuple-element.111), channel_id=1, source_target_pairs={{0,8},{2,10},{4,12},{6,14},{8,16},{10,18},{12,20},{14,22},{16,24},... | collective-permute-start | bytes 153608 | tf_op jit(solution)/shard_map/cond/branch_1_fun/ppermute | solution.py:633
  292.9 29.1 %collective-permute-start.5 = (bf16[8,3200]{1,0:T(8,128)(2,1)S(1)}, bf16[8,3200]{1,0:T(8,128)(2,1)S(1)}, u32[]{:S(2)}, u32[]{:S(2)}) collective-permute-start(bf16[8,3200]{1,0:T(8,128)(2,1)S(1)} %get-tuple-element.113), channel_id=1, source_target_pairs={{0,16},{2,18},{4,20},{6,22},{8,24},{10,26},{12,28},{14,30},{16,0},... | collective-permute-start | bytes 153608 | tf_op jit(solution)/shard_map/cond/branch_1_fun/ppermute | solution.py:633
  295.0 27.0 %collective-permute-start.6 = (bf16[8,3200]{1,0:T(8,128)(2,1)S(1)}, bf16[8,3200]{1,0:T(8,128)(2,1)S(1)}, u32[]{:S(2)}, u32[]{:S(2)}) collective-permute-start(bf16[8,3200]{1,0:T(8,128)(2,1)S(1)} %get-tuple-element.112), channel_id=1, source_target_pairs={{0,24},{2,26},{4,28},{6,30},{8,0},{10,2},{12,4},{14,6},{16,8},{18,... | collective-permute-start | bytes 153608 | tf_op jit(solution)/shard_map/cond/branch_1_fun/ppermute | solution.py:633
  322.0 6.5 %collective-permute-start.7 = (bf16[8,3200]{1,0:T(8,128)(2,1)S(1)}, bf16[8,3200]{1,0:T(8,128)(2,1)S(1)}, u32[]{:S(2)}, u32[]{:S(2)}) collective-permute-start(bf16[8,3200]{1,0:T(8,128)(2,1)S(1)} %add_convert_fusion), channel_id=1, source_target_pairs={{0,8},{2,10},{4,12},{6,14},{8,16},{10,18},{12,20},{14,22},{16,24},... | collective-permute-start | bytes 153608 | tf_op jit(solution)/shard_map/cond/branch_1_fun/ppermute | solution.py:637
  323.3 6.2 %collective-permute-start.8 = (bf16[8,3200]{1,0:T(8,128)(2,1)S(1)}, bf16[8,3200]{1,0:T(8,128)(2,1)S(1)}, u32[]{:S(2)}, u32[]{:S(2)}) collective-permute-start(bf16[8,3200]{1,0:T(8,128)(2,1)S(1)} %add_convert_fusion), channel_id=1, source_target_pairs={{0,16},{2,18},{4,20},{6,22},{8,24},{10,26},{12,28},{14,30},{16,0},... | collective-permute-start | bytes 153608 | tf_op jit(solution)/shard_map/cond/branch_1_fun/ppermute | solution.py:637
  324.8 4.7 %collective-permute-start.9 = (bf16[8,3200]{1,0:T(8,128)(2,1)S(1)}, bf16[8,3200]{1,0:T(8,128)(2,1)S(1)}, u32[]{:S(2)}, u32[]{:S(2)}) collective-permute-start(bf16[8,3200]{1,0:T(8,128)(2,1)S(1)} %add_convert_fusion), channel_id=1, source_target_pairs={{0,24},{2,26},{4,28},{6,30},{8,0},{10,2},{12,4},{14,6},{16,8},{18,... | collective-permute-start | bytes 153608 | tf_op jit(solution)/shard_map/cond/branch_1_fun/ppermute | solution.py:637
  329.5 5.8 %collective-permute-start.10 = (bf16[4,8,3200]{2,1,0:T(8,128)(2,1)S(1)}, bf16[4,8,3200]{2,1,0:T(8,128)(2,1)S(1)}, u32[]{:S(2)}, u32[]{:S(2)}) collective-permute-start(bf16[4,8,3200]{2,1,0:T(8,128)(2,1)S(1)} %get-tuple-element.115), channel_id=1, source_target_pairs={{0,4},{2,6},{4,0},{6,2},{8,12},{10,14},{12,8},{14,10},{16,20},{18,... | collective-permute-start | bytes 614408 | tf_op jit(solution)/shard_map/cond/branch_1_fun/ppermute | solution.py:639
  331.2 4.2 %collective-permute-start.11 = (bf16[4,8,3200]{2,1,0:T(8,128)(2,1)S(1)}, bf16[4,8,3200]{2,1,0:T(8,128)(2,1)S(1)}, u32[]{:S(2)}, u32[]{:S(2)}) collective-permute-start(bf16[4,8,3200]{2,1,0:T(8,128)(2,1)S(1)} %get-tuple-element.115), channel_id=1, source_target_pairs={{0,2},{2,0},{4,6},{6,4},{8,10},{10,8},{12,14},{14,12},{16,18},{18,... | collective-permute-start | bytes 614408 | tf_op jit(solution)/shard_map/cond/branch_1_fun/ppermute | solution.py:640
  335.4 1.5 collective-permute-start.12
  345.1 9.5 %copy-start.3 = (f32[3084,128]{1,0:T(8,128)S(1)}, f32[3084,128]{1,0:T(8,128)}, u32[]{:S(2)}) copy-start(f32[3084,128]{1,0:T(8,128)} %get-tuple-element.108) | copy-start | bytes 4737028
  368.4 1.3 copy-start.1

commit v3 on v2

v3 whole, which is shorter than its diff:
```python
import functools

import jax
import jax.numpy as jnp
from jax import lax
from jax.experimental import pallas as pl
from jax.experimental.pallas import tpu as pltpu
from jax.sharding import PartitionSpec as P

STEP = 1
QUERY_SCALE = 0.125
NORM_EPSILON = 1e-12
LEARNING_RATE = 0.02
WEIGHT_DECAY = 0.01
ADAM_EPSILON = 1e-08
FIRST_BETA = 0.5
SECOND_BETA = 0.5
MASK_VALUE = -1e30
NORMAL_PEAK = 0.3989422804014327

LOW = jnp.bfloat16
F32 = jnp.float32
VMEM_LIMIT = 60 * 1024 * 1024

BLOCK = 64
HALF = 128
GROUP = 31
AHEAD_ROWS = 1024
BEHIND_ROWS = 512
BACK = 10


def dot_nn(a, b):
    return lax.dot_general(a, b, (((1,), (0,)), ((), ())), preferred_element_type=F32)


def dot_nt(a, b):
    return lax.dot_general(a, b, (((1,), (1,)), ((), ())), preferred_element_type=F32)


def dot_tn(a, b):
    return lax.dot_general(a, b, (((0,), (0,)), ((), ())), preferred_element_type=F32)


def first_half(rows):
    return lax.broadcasted_iota(jnp.int32, (rows, HALF), 1) < BLOCK


def spread_heads(rows, picks):
    return jnp.concatenate([rows, rows, rows, rows], axis=0) * picks


def pick_heads(wide):
    low = first_half(BLOCK)
    left = jnp.where(low, wide[0:64, 0:HALF], wide[64:128, 0:HALF])
    right = jnp.where(low, wide[128:192, HALF:], wide[192:256, HALF:])
    return jnp.concatenate([left, right], axis=1)


def head_picks():
    row = lax.broadcasted_iota(jnp.int32, (256, 256), 0) // BLOCK
    col = lax.broadcasted_iota(jnp.int32, (256, 256), 1) // BLOCK
    return jnp.where(row == col, 1.0, 0.0).astype(LOW)


def gather_slot(ref, chosen, tile):
    a, b = chosen[2 * tile], chosen[2 * tile + 1]
    cols = pl.ds(tile * HALF, HALF)
    left = ref[pl.ds(pl.multiple_of(a * BLOCK, BLOCK), BLOCK), cols]
    right = ref[pl.ds(pl.multiple_of(b * BLOCK, BLOCK), BLOCK), cols]
    return jnp.where(first_half(BLOCK), left, right)


def turn_pairs(ref, turned):
    pairs = turned.shape[0] // 2

    def one(j, _):
        pair = ref[:, pl.ds(pl.multiple_of(j * HALF, HALF), HALF)]
        turned[j] = pair
        turned[pairs + j] = jnp.concatenate([pair[:, BLOCK:], pair[:, :BLOCK]], axis=1)
        return 0

    lax.fori_loop(0, pairs, one, 0, unroll=8)


def pick_turned(wide):
    low = first_half(BLOCK)
    left, right = wide[0:HALF, 0:HALF].T, wide[HALF:, HALF:].T
    return jnp.concatenate(
        [jnp.where(low, part[0:BLOCK], part[BLOCK:]) for part in (left, right)], axis=1
    )


class Unit:
    def __init__(self, i, live, drawn, blocks):
        last = live - 1

        def state(b):
            return (b >= last).astype(jnp.int32) + (b > last).astype(jnp.int32)

        after = jnp.minimum(i + 1, blocks - 1)
        self.near = [i - 1, i, after]
        self.near_state = [
            jnp.where(i >= 3, state(i - 1), 2),
            state(i),
            jnp.where(i + 1 < blocks, state(after), 2),
        ]
        self.fixed_state = [state(0 * i), state(0 * i + 1)]
        self.chosen = [
            [drawn[(h * blocks + i) * 3 + s] for h in range(4)] for s in range(3)
        ]
        self.chosen_state = [[state(b) for b in row] for row in self.chosen]

    def bias(self, table, slots):
        rows = []
        for n in slots:
            if n < 5:
                one = table[(self.fixed_state + self.near_state)[n]]
                rows.append(jnp.concatenate([one, one], axis=1))
            else:
                st = self.chosen_state[n - 5]
                low = first_half(BLOCK)
                rows.append(
                    jnp.concatenate(
                        [
                            jnp.where(low, table[st[0]], table[st[1]]),
                            jnp.where(low, table[st[2]], table[st[3]]),
                        ],
                        axis=1,
                    )
                )
        return jnp.concatenate(rows, axis=0)


def chunk_bias(table, live, first, count):
    last = live - 1
    rows = []
    for n in range(count):
        b = first + n
        st = (b >= last).astype(jnp.int32) + (b > last).astype(jnp.int32)
        one = table[st]
        rows.append(jnp.concatenate([one, one], axis=1))
    return jnp.concatenate(rows, axis=0)


def slot_rows(unit, ref):
    near = [ref[pl.ds(pl.multiple_of(b * BLOCK, BLOCK), BLOCK), :] for b in unit.near]
    rand = [jnp.concatenate([gather_slot(ref, unit.chosen[s], t) for t in range(2)], axis=1) for s in range(3)]
    return jnp.concatenate([ref[0:128, :]] + near + rand, axis=0)


def slot_turned(unit, first, turned):
    low = lax.broadcasted_iota(jnp.int32, (BLOCK, HALF), 1) < BLOCK
    every = [[b] * 4 for b in unit.near] + unit.chosen
    pairs = turned.shape[0] // 2
    tiles = [first]
    for n in range(3):
        parts = []
        for h in range(4):
            rows = pl.ds(h * BLOCK, BLOCK)
            a, b = every[2 * n][h], every[2 * n + 1][h]
            left = turned[(a & 1) * pairs + (a >> 1), rows, :]
            right = turned[(1 - (b & 1)) * pairs + (b >> 1), rows, :]
            parts.append(jnp.where(low, left, right))
        tiles.append(jnp.concatenate(parts, axis=0))
    return jnp.concatenate(tiles, axis=1)


def forward_kernel(
    scal, drawn, table, x, w, w_kt, w_vt, shift, shift_vt,
    q_o, k_o, v_o, kt_o, ctx_o, lse_o, picks, q_v, k_v, v_v, kt_v, vt, turned, sg, og, sems,
):
    length = x.shape[0]
    blocks = length // BLOCK
    live = scal[0]
    picks[...] = head_picks()

    def project(c, _):
        rows = pl.ds(pl.multiple_of(c * 512, 512), 512)
        xc = x[rows, :]
        out = (dot_nn(xc, w[...]) + shift[...]).astype(LOW)
        q_v[rows, :] = out[:, 0:256]
        k_v[rows, :] = out[:, 256:512]
        v_v[rows, :] = out[:, 512:768]
        kt_v[:, rows] = dot_nt(w_kt[...], xc).astype(LOW)
        vt[:, rows] = (dot_nt(w_vt[...], xc) + shift_vt[:, 0:1]).astype(LOW)
        return 0

    lax.fori_loop(0, length // 512, project, 0)
    copies = [
        pltpu.make_async_copy(here, there, sems.at[n])
        for n, (here, there) in enumerate(((q_v, q_o), (k_v, k_o), (v_v, v_o), (kt_v, kt_o)))
    ]
    for copy in copies:
        copy.start()
    turn_pairs(vt, turned)

    def group(j, _):
        idx = [2 + GROUP * j + u for u in range(GROUP)]
        units = [Unit(i, live, drawn, blocks) for i in idx]
        rows = [pl.ds(pl.multiple_of(i * BLOCK, BLOCK), BLOCK) for i in idx]
        bd = [spread_heads(q_v[r, :] * jnp.asarray(QUERY_SCALE, LOW), picks[...]) for r in rows]
        every = range(GROUP)
        s = [dot_nt(slot_rows(units[u], k_v), bd[u]) + units[u].bias(table, range(8)) for u in every]
        m = [jnp.max(s[u], axis=0, keepdims=True) for u in every]
        e = [jnp.exp(s[u] - m[u]) for u in every]
        total = [jnp.sum(e[u], axis=0, keepdims=True) for u in every]
        o = [
            dot_nn(slot_turned(units[u], vt[:, 0:128], turned), e[u].astype(LOW)) * (1.0 / total[u]) for u in every
        ]
        for u in every:
            ctx_o[rows[u], :] = pick_turned(o[u]).astype(LOW)
            lse_o[pl.ds(idx[u], 1), :] = m[u] + jnp.log(total[u])
        return 0

    lax.fori_loop(0, (blocks - 2) // GROUP, group, 0)

    bds = [
        spread_heads(q_v[g * 64 : g * 64 + 64, :] * jnp.asarray(QUERY_SCALE, LOW), picks[...]) for g in range(2)
    ]

    def score(c, peaks):
        rows = pl.ds(pl.multiple_of(c * 512, 512), 512)
        bias = chunk_bias(table, live, c * 8, 8)
        out = []
        for g in range(2):
            s = dot_nt(k_v[rows, :], bds[g]) + bias
            sg[g, rows, :] = s
            out.append(jnp.maximum(peaks[g], jnp.max(s, axis=0, keepdims=True)))
        return tuple(out)

    peaks = lax.fori_loop(0, length // 512, score, (jnp.full((1, 256), MASK_VALUE, F32),) * 2)

    og[...] = jnp.zeros_like(og)

    def mix(c, totals):
        rows = pl.ds(pl.multiple_of(c * 512, 512), 512)
        out = []
        for g in range(2):
            e = jnp.exp(sg[g, rows, :] - peaks[g])
            out.append(totals[g] + jnp.sum(e, axis=0, keepdims=True))
            og[g] += dot_nn(vt[:, rows], e.astype(LOW))
        return tuple(out)

    totals = lax.fori_loop(0, length // 512, mix, (jnp.zeros((1, 256), F32),) * 2)
    for g in range(2):
        ctx_o[g * 64 : g * 64 + 64, :] = pick_turned(og[g] * (1.0 / totals[g])).astype(LOW)
        lse_o[g : g + 1, :] = peaks[g] + jnp.log(totals[g])
    for copy in copies:
        copy.wait()


def vmem():
    return pl.BlockSpec(memory_space=pltpu.VMEM)


def smem():
    return pl.BlockSpec(memory_space=pltpu.SMEM)


def forward_attention(scal, drawn, table, x, w, w_kt, w_vt, shift, shift_vt):
    length = x.shape[0]
    blocks = length // BLOCK
    rows = jax.ShapeDtypeStruct((length, 256), LOW)
    return pl.pallas_call(
        forward_kernel,
        out_shape=(
            rows, rows, rows, jax.ShapeDtypeStruct((256, length), LOW), rows, jax.ShapeDtypeStruct((blocks, 256), F32),
        ),
        in_specs=[smem(), smem()] + [vmem()] * 7,
        out_specs=[pl.BlockSpec(memory_space=pl.ANY)] * 4 + [vmem()] * 2,
        scratch_shapes=[
            pltpu.VMEM((256, 256), LOW),
            pltpu.VMEM((length, 256), LOW),
            pltpu.VMEM((length, 256), LOW),
            pltpu.VMEM((length, 256), LOW),
            pltpu.VMEM((256, length), LOW),
            pltpu.VMEM((256, length), LOW),
            pltpu.VMEM((blocks, 256, HALF), LOW),
            pltpu.VMEM((2, length, 256), F32),
            pltpu.VMEM((2, 256, 256), F32),
            pltpu.SemaphoreType.DMA((4,)),
        ],
        compiler_params=pltpu.CompilerParams(vmem_limit_bytes=VMEM_LIMIT),
        cost_estimate=pl.CostEstimate(flops=16_000_000_000, bytes_accessed=12_000_000, transcendentals=10_000_000),
        name="attend_forward",
    )(scal, drawn, table, x, w, w_kt, w_vt, shift, shift_vt)


def normalize(summed):
    center = summed - jnp.mean(summed, axis=-1, keepdims=True)
    factor = lax.rsqrt(jnp.mean(center * center, axis=-1, keepdims=True) + NORM_EPSILON)
    return (center * factor, factor)


def normalize_back(grad_normed, normed, factor):
    return factor * (
        grad_normed
        - jnp.mean(grad_normed, axis=-1, keepdims=True)
        - normed * jnp.mean(grad_normed * normed, axis=-1, keepdims=True)
    )


ROOT_HALF = 0.7071067811865476


def gelu_parts(v):
    cumulative = 0.5 * (1.0 + lax.erf(v * ROOT_HALF))
    return v * cumulative, cumulative + v * (NORMAL_PEAK * jnp.exp(-0.5 * v * v))


def open_rows(table, scal, rows):
    last = scal[0] - 1
    marks = []
    for n in range(rows // BLOCK):
        b = pl.program_id(0) * (rows // BLOCK) + n
        one = table[(b >= last).astype(jnp.int32) + (b > last).astype(jnp.int32)]
        marks.append(jnp.concatenate([one, one], axis=1))
    return jnp.concatenate(marks, axis=0) == 0.0


def ahead_kernel(scal, table, x, ctx, w_out, w_up, w_down, up_shift, vec, out_o, one_o, two_o, stat_o, act_o, slope_o):
    rows = x.shape[0]

    def row(n):
        return vec[n : n + 1, :]

    attended = dot_nn(ctx[...], w_out[...]) + row(2)
    normed_one, factor_one = normalize(x[...].astype(F32) + attended)
    one_o[...] = normed_one
    first_out = normed_one * row(3) + row(4)
    first_low = first_out.astype(LOW)
    for c in range(0, 1024, 256):
        pre = dot_nn(first_low, w_up[:, c : c + 256]) + up_shift[:, c : c + 256]
        a, s = gelu_parts(pre)
        act_o[:, c : c + 256] = a.astype(LOW)
        slope_o[:, c : c + 256] = s.astype(LOW)
    branch = dot_nn(act_o[...], w_down[...]) + row(5)
    normed_two, factor_two = normalize(first_out + branch)
    two_o[...] = normed_two
    stat_o[...] = jnp.where(first_half(rows), factor_one, factor_two)
    out_o[...] = jnp.where(open_rows(table, scal, rows), normed_two * row(6) + row(7), 0.0).astype(LOW)


def ahead(scal, table, x, ctx, w_out, w_up, w_down, up_shift, vec):
    length = x.shape[0]
    rows = AHEAD_ROWS

    def wide(columns):
        return pl.BlockSpec((rows, columns), lambda i, s: (i, 0))

    def whole(*shape):
        return pl.BlockSpec(shape, lambda i, s: (0,) * len(shape))

    shape = jax.ShapeDtypeStruct
    return pl.pallas_call(
        ahead_kernel,
        grid_spec=pltpu.PrefetchScalarGridSpec(
            num_scalar_prefetch=1,
            grid=(length // rows,),
            in_specs=[
                whole(3, 64, 128), wide(256), wide(256), whole(256, 256), whole(256, 1024), whole(1024, 256),
                whole(1, 1024), whole(8, 256),
            ],
            out_specs=[wide(256), wide(256), wide(256), wide(HALF), wide(1024), wide(1024)],
        ),
        out_shape=(
            shape((length, 256), LOW), shape((length, 256), F32), shape((length, 256), F32),
            shape((length, HALF), F32), shape((length, 1024), LOW), shape((length, 1024), LOW),
        ),
        compiler_params=pltpu.CompilerParams(vmem_limit_bytes=VMEM_LIMIT),
        cost_estimate=pl.CostEstimate(flops=5_000_000_000, bytes_accessed=34_000_000, transcendentals=10_000_000),
        name="ahead",
    )(scal, table, x, ctx, w_out, w_up, w_down, up_shift, vec)


def behind_kernel(
    scal, table, cot, ctx, one, two, stat, act, slope, w_out, w_up, w_down, vec,
    gz1_o, gctx_o, delta_o, pack0, pack1, pack2, pack3, gdown_o, gup_o, gout_o, gub_o, gvec_o, pre,
):
    step = pl.program_id(0)
    rows = cot.shape[0]

    @pl.when(step == 0)
    def _():
        for ref in (gdown_o, gup_o, gout_o, gub_o, gvec_o):
            ref[...] = jnp.zeros_like(ref)

    def row(n):
        return vec[n : n + 1, :]

    normed_one, normed_two = one[...], two[...]
    factor_one, factor_two = stat[:, 0:1], stat[:, BLOCK : BLOCK + 1]
    first_low = (normed_one * row(3) + row(4)).astype(LOW)
    grad_y = jnp.where(open_rows(table, scal, rows), cot[...].astype(F32), 0.0)
    grad_z2 = normalize_back(grad_y * row(6), normed_two, factor_two)
    grad_branch = grad_z2.astype(LOW)
    for c in range(0, 1024, 256):
        grad_act = dot_nt(grad_branch, w_down[c : c + 256, :])
        grad_pre = (grad_act * slope[:, c : c + 256].astype(F32)).astype(LOW)
        pre[:, c : c + 256] = grad_pre
        gub_o[:, c : c + 256] += jnp.sum(grad_pre.astype(F32), axis=0, keepdims=True)
    gdown_o[...] += dot_tn(act[...], grad_branch)
    grad_first = grad_z2 + dot_nt(pre[...], w_up[...])
    gup_o[...] += dot_tn(first_low, pre[...])
    grad_z1 = normalize_back(grad_first * row(3), normed_one, factor_one)
    gz1_o[...] = grad_z1
    grad_attended = grad_z1.astype(LOW)
    ctx_v = ctx[...]
    gout_o[...] += dot_tn(ctx_v, grad_attended)
    grad_context = dot_nt(grad_attended, w_out[...]).astype(LOW)
    gctx_o[...] = grad_context

    def add(n, values):
        gvec_o[n : n + 1, :] += jnp.sum(values, axis=0, keepdims=True)

    add(2, grad_attended.astype(F32))
    add(3, grad_first * normed_one)
    add(4, grad_first)
    add(5, grad_branch.astype(F32))
    add(6, grad_y * normed_two)
    add(7, grad_y)
    both = ctx_v.astype(F32) * grad_context.astype(F32)
    upper = both.astype(LOW)
    lower = (both - upper.astype(F32)).astype(LOW)
    group = lax.broadcasted_iota(jnp.int32, (8, 256), 1) // BLOCK
    ones = jnp.where(group == lax.broadcasted_iota(jnp.int32, (8, 256), 0), 1.0, 0.0).astype(LOW)
    sums = dot_nt(ones, upper) + dot_nt(ones, lower)
    for n in range(rows // BLOCK):
        part = sums[0:4, n * BLOCK : (n + 1) * BLOCK]
        delta_o[n : n + 1, :] = jnp.concatenate([part[h : h + 1, :] for h in range(4)], axis=1)

    @pl.when(step == pl.num_programs(0) - 1)
    def _():
        for r, pack in enumerate((pack0, pack1, pack2, pack3)):
            piece = scal[1] ^ r
            shard, core = piece // 2, piece % 2
            here = pl.ds(pl.multiple_of(piece * 64, 64), 64)
            pack[:, 0:1024] = gup_o[here, :].astype(LOW)
            pack[:, 1024:1280] = gout_o[here, :].astype(LOW)
            for g in range(4):
                at = pl.ds(pl.multiple_of(shard * 512 + g * 128 + core * 64, 64), 64)
                pack[:, 1280 + 256 * g : 1536 + 256 * g] = gdown_o[at, :].astype(LOW)
            lines = [gub_o[:, pl.ds(pl.multiple_of(shard * 512 + 128 * n, 128), 128)] for n in range(4)]
            first = shard == 0
            for n in range(4):
                line = jnp.where(first, gvec_o[n : n + 1, :], gvec_o[4 + n : 5 + n, :])
                lines += [line[:, 0:128], line[:, 128:256]]
            put_extra(pack, 2304, lines, core)


def put_extra(pack, at, lines, core):
    some = jnp.concatenate(lines + [jnp.zeros((16 - len(lines), HALF), F32)], axis=0)
    pack[0:16, at : at + HALF] = jnp.where(core == 0, some, 0.0).astype(LOW)
    pack[16:64, at : at + HALF] = jnp.zeros((48, HALF), LOW)


def behind(scal, table, cot, ctx, one, two, stat, act, slope, w_out, w_up, w_down, vec):
    length = cot.shape[0]
    rows = BEHIND_ROWS

    def wide(columns):
        return pl.BlockSpec((rows, columns), lambda i, s: (i, 0))

    def whole(*shape):
        return pl.BlockSpec(shape, lambda i, s: (0,) * len(shape))

    shape = jax.ShapeDtypeStruct
    return pl.pallas_call(
        behind_kernel,
        grid_spec=pltpu.PrefetchScalarGridSpec(
            num_scalar_prefetch=1,
            grid=(length // rows,),
            in_specs=[
                whole(3, 64, 128), wide(256), wide(256), wide(256), wide(256), wide(HALF), wide(1024), wide(1024),
                whole(256, 256), whole(256, 1024), whole(1024, 256), whole(8, 256),
            ],
            out_specs=[
                wide(256), wide(256), pl.BlockSpec((rows // BLOCK, 256), lambda i, s: (i, 0)),
                whole(64, 2432), whole(64, 2432), whole(64, 2432), whole(64, 2432),
            ],
            scratch_shapes=[
                pltpu.VMEM((1024, 256), F32), pltpu.VMEM((256, 1024), F32), pltpu.VMEM((256, 256), F32),
                pltpu.VMEM((1, 1024), F32), pltpu.VMEM((8, 256), F32), pltpu.VMEM((rows, 1024), LOW),
            ],
        ),
        out_shape=(
            shape((length, 256), F32), shape((length, 256), LOW), shape((length // BLOCK, 256), F32),
        ) + (shape((64, 2432), LOW),) * 4,
        compiler_params=pltpu.CompilerParams(vmem_limit_bytes=VMEM_LIMIT),
        cost_estimate=pl.CostEstimate(flops=10_000_000_000, bytes_accessed=40_000_000, transcendentals=0),
        name="behind",
    )(scal, table, cot, ctx, one, two, stat, act, slope, w_out, w_up, w_down, vec)


def backward_kernel(
    scal, drawn, table, q, k, v, kt, gctx, lse, delta, gz1, x, w,
    gin_o, pack0, pack1, pack2, pack3, picks, turned, dqg, dq, dk, dv, gw_o, gz1_v, x_v, gin_v, sems,
):
    length = x.shape[0]
    blocks = length // BLOCK
    live = scal[0]
    picks[...] = head_picks()
    dk[...] = jnp.zeros_like(dk)
    dv[...] = jnp.zeros_like(dv)
    loads = [pltpu.make_async_copy(gz1, gz1_v, sems.at[0]), pltpu.make_async_copy(x, x_v, sems.at[1])]
    for load in loads:
        load.start()
    turn_pairs(kt, turned)

    def spread(i):
        rows = pl.ds(pl.multiple_of(i * BLOCK, BLOCK), BLOCK)
        bdq = spread_heads(q[rows, :] * jnp.asarray(QUERY_SCALE, LOW), picks[...])
        bdo = spread_heads(gctx[rows, :], picks[...])
        return rows, bdq, bdo

    def group(idx):
        units = [Unit(i, live, drawn, blocks) for i in idx]
        spreads = [spread(i) for i in idx]
        every = range(len(idx))
        s = [dot_nt(slot_rows(units[u], k), spreads[u][1]) for u in every]
        g = [dot_nt(slot_rows(units[u], v), spreads[u][2]) for u in every]
        p = [jnp.exp(s[u] + units[u].bias(table, range(8)) - lse[pl.ds(idx[u], 1), :]) for u in every]
        ds = [(p[u] * (g[u] - delta[pl.ds(idx[u], 1), :])).astype(LOW) for u in every]
        dvs = [dot_nn(p[u].astype(LOW), spreads[u][2]) for u in every]
        dks = [dot_nn(ds[u], spreads[u][1]) for u in every]
        dqs = [dot_nn(slot_turned(units[u], kt[:, 0:128], turned), ds[u]) for u in every]
        low = first_half(BLOCK)
        for u in every:
            for acc, terms_ in ((dk, dks[u]), (dv, dvs[u])):
                acc[0:128, :] += terms_[0:128, :]
                for n in range(2, 8):
                    one = terms_[n * 64 : n * 64 + 64, :]
                    if n < 5:
                        at = pl.ds(pl.multiple_of(units[u].near[n - 2] * BLOCK, BLOCK), BLOCK)
                        acc[at, :] += one
                    else:
                        for h in range(4):
                            t = h // 2
                            at = pl.ds(pl.multiple_of(units[u].chosen[n - 5][h] * BLOCK, BLOCK), BLOCK)
                            cols = pl.ds(t * HALF, HALF)
                            mine = low if h % 2 == 0 else jnp.logical_not(low)
                            acc[at, cols] += jnp.where(mine, one[:, t * HALF : t * HALF + HALF], 0.0)
            dq[spreads[u][0], :] = (pick_turned(dqs[u]) * QUERY_SCALE).astype(LOW)

    def several(j, _):
        group([2 + BACK * j + u for u in range(BACK)])
        return 0

    lax.fori_loop(0, (blocks - 2) // BACK, several, 0)
    if (blocks - 2) % BACK:
        group([live * 0 + i for i in range(blocks - (blocks - 2) % BACK, blocks)])

    spreads = [spread(g)[1:] for g in range(2)]
    dqg[...] = jnp.zeros_like(dqg)

    def chunk(c, _):
        at = pl.ds(pl.multiple_of(c * 512, 512), 512)
        bias = chunk_bias(table, live, c * 8, 8)
        kh, vh, th = k[at, :], v[at, :], kt[:, at]
        two = range(2)
        s = [dot_nt(kh, spreads[g][0]) for g in two]
        t = [dot_nt(vh, spreads[g][1]) for g in two]
        p = [jnp.exp(s[g] + bias - lse[g : g + 1, :]) for g in two]
        ds = [(p[g] * (t[g] - delta[g : g + 1, :])).astype(LOW) for g in two]
        dvs = [dot_nn(p[g].astype(LOW), spreads[g][1]) for g in two]
        dks = [dot_nn(ds[g], spreads[g][0]) for g in two]
        for g in two:
            dqg[g] += dot_nn(th, ds[g])
        dv[at, :] += dvs[0] + dvs[1]
        dk[at, :] += dks[0] + dks[1]
        return 0

    lax.fori_loop(0, length // 512, chunk, 0, unroll=2)
    for g in range(2):
        dq[g * 64 : g * 64 + 64, :] = (pick_turned(dqg[g]) * QUERY_SCALE).astype(LOW)

    gw_o[...] = jnp.zeros_like(gw_o)
    for load in loads:
        load.wait()

    def finish(c, shifts):
        rows = pl.ds(pl.multiple_of(c * 512, 512), 512)
        dqkv = jnp.concatenate([dq[rows, :], dk[rows, :].astype(LOW), dv[rows, :].astype(LOW)], axis=1)
        gin_v[rows, :] = (gz1_v[rows, :] + dot_nt(dqkv, w[...])).astype(LOW)
        gw_o[...] += dot_tn(x_v[rows, :], dqkv)
        return shifts + jnp.sum(dqkv.astype(F32), axis=0, keepdims=True)

    shifts = lax.fori_loop(0, length // 512, finish, jnp.zeros((1, 768), F32))
    store = pltpu.make_async_copy(gin_v, gin_o, sems.at[2])
    store.start()
    for r, pack in enumerate((pack0, pack1, pack2, pack3)):
        piece = scal[1] ^ r
        core = piece % 2
        pack[:, 0:768] = gw_o[pl.ds(pl.multiple_of(piece * 64, 64), 64), :].astype(LOW)
        mine = jnp.where(piece // 2 == 0, shifts, 0.0)
        lines = [jnp.zeros((4, HALF), F32)] + [mine[:, a : a + HALF] for a in (0, 128, 512, 640)]
        lines += [jnp.zeros((8, HALF), F32)]
        pack[:, 768:896] = jnp.zeros((64, HALF), LOW)
        pack[0:16, 768:896] = jnp.where(core == 0, jnp.concatenate(lines, axis=0), 0.0).astype(LOW)
    store.wait()


def backward_attention(scal, drawn, table, q, k, v, kt, gctx, lse, delta, gz1, x, w):
    length = x.shape[0]
    shape = jax.ShapeDtypeStruct
    return pl.pallas_call(
        backward_kernel,
        out_shape=(shape((length, 256), LOW),) + (shape((64, 896), LOW),) * 4,
        in_specs=[smem(), smem()] + [vmem()] * 8 + [pl.BlockSpec(memory_space=pl.ANY)] * 2 + [vmem()],
        out_specs=[pl.BlockSpec(memory_space=pl.ANY)] + [vmem()] * 4,
        scratch_shapes=[
            pltpu.VMEM((256, 256), LOW),
            pltpu.VMEM((length // BLOCK, 256, HALF), LOW),
            pltpu.VMEM((2, 256, 256), F32),
            pltpu.VMEM((length, 256), LOW),
            pltpu.VMEM((length, 256), F32),
            pltpu.VMEM((length, 256), F32),
            pltpu.VMEM((256, 768), F32),
            pltpu.VMEM((length, 256), F32),
            pltpu.VMEM((length, 256), LOW),
            pltpu.VMEM((length, 256), LOW),
            pltpu.SemaphoreType.DMA((3,)),
        ],
        compiler_params=pltpu.CompilerParams(vmem_limit_bytes=VMEM_LIMIT),
        cost_estimate=pl.CostEstimate(flops=40_000_000_000, bytes_accessed=20_000_000, transcendentals=10_000_000),
        name="attend_backward",
    )(scal, drawn, table, q, k, v, kt, gctx, lse, delta, gz1, x, w)


def bias_table(tail):
    column = jnp.stack([jnp.zeros_like(tail, F32), jnp.where(tail == 1, 0.0, MASK_VALUE), jnp.full(tail.shape, MASK_VALUE, F32)])
    return jnp.broadcast_to(column[:, :, None], (3, BLOCK, HALF))


def reorder_kernel(scatter, where, assign, src, *rest):
    *_, dst, held, arrived, left = rest
    count = src.shape[0]
    shards = assign.shape[0] // count
    loads, stores = [], []
    for j in range(count):
        one = assign[shards * j + where[0]]
        loads.append(pltpu.make_async_copy(src.at[j if scatter else one], held.at[j], arrived.at[j]))
        stores.append(pltpu.make_async_copy(held.at[j], dst.at[one if scatter else j], left.at[j]))
        loads[-1].start()
    for load, store in zip(loads, stores):
        load.wait()
        store.start()
    for store in stores:
        store.wait()


def reorder(shard, assign, src, scatter, after=()):
    return pl.pallas_call(
        functools.partial(reorder_kernel, scatter),
        out_shape=jax.ShapeDtypeStruct(src.shape, src.dtype),
        in_specs=[smem(), smem()] + [pl.BlockSpec(memory_space=pl.ANY)] * (1 + len(after)),
        out_specs=pl.BlockSpec(memory_space=pl.ANY),
        scratch_shapes=[
            pltpu.VMEM(src.shape, src.dtype),
            pltpu.SemaphoreType.DMA((src.shape[0],)),
            pltpu.SemaphoreType.DMA((src.shape[0],)),
        ],
        compiler_params=pltpu.CompilerParams(vmem_limit_bytes=8 * 1024 * 1024),
        cost_estimate=pl.CostEstimate(flops=0, bytes_accessed=4 * src.size, transcendentals=0),
        name="reorder",
    )(shard, assign, src, *after)


def hold(values, after):
    count = len(values)
    anywhere = pl.BlockSpec(memory_space=pl.ANY)
    return pl.pallas_call(
        lambda *refs: None,
        out_shape=tuple(jax.ShapeDtypeStruct(v.shape, v.dtype) for v in values),
        in_specs=[anywhere] * (count + len(after)),
        out_specs=(anywhere,) * count,
        input_output_aliases={n: n for n in range(count)},
        name="hold",
    )(*values, *after)


def pack_kernel(w_qkv, w_out, w_up, w_down, up_bias, vectors, after, out):
    rows = w_qkv.shape[0]
    out[0:rows, 0:768] = w_qkv[...]
    out[0:rows, 768:1024] = w_out[...]
    out[0:rows, 1024:2048] = w_up[...]
    for n in range(4):
        out[0:rows, 2048 + 256 * n : 2304 + 256 * n] = w_down[rows * n : rows * (n + 1), :]
    lines = [up_bias[...].astype(F32)] + [vectors[n : n + 1, :].astype(F32) for n in range(4)]
    line = jnp.concatenate(lines + [jnp.zeros((1, 3072 - 1536), F32)], axis=1)
    out[rows : rows + 16, :] = jnp.broadcast_to(line, (16, 3072)).astype(LOW)


def pack_weights(parts, after):
    w_qkv, w_out, w_up, w_down, up_bias, vectors = parts
    return pl.pallas_call(
        pack_kernel,
        out_shape=jax.ShapeDtypeStruct((w_qkv.shape[0] + 16, 3072), LOW),
        in_specs=[vmem()] * 6 + [pl.BlockSpec(memory_space=pl.ANY)],
        out_specs=vmem(),
        compiler_params=pltpu.CompilerParams(vmem_limit_bytes=8 * 1024 * 1024),
        name="pack_weights",
    )(w_qkv, w_out, w_up, w_down, up_bias.reshape(1, -1), vectors, after)


def unpack_kernel(shard, own, got, w_qkv, w_out, w_up, w_down, w_kt, w_vt, up_shift, vec, shift, shift_vt):
    rows = own.shape[0] - 16
    first = shard[0] == 0

    def half(n, at, cols):
        mine, other = own[at, cols], got[at, cols]
        return jnp.where(first == (n == 0), mine, other)

    for n in range(2):
        here = slice(n * rows, (n + 1) * rows)
        w_qkv[here, :] = half(n, slice(0, rows), slice(0, 768))
        w_out[here, :] = half(n, slice(0, rows), slice(768, 1024))
        w_up[here, :] = half(n, slice(0, rows), slice(1024, 2048))
        for g in range(4):
            at = (4 * n + g) * rows
            w_down[at : at + rows, :] = half(n, slice(0, rows), slice(2048 + 256 * g, 2304 + 256 * g))
        line = half(n, slice(rows, rows + 16), slice(0, 1536)).astype(F32)[0:1]
        up_shift[:, 512 * n : 512 * n + 512] = line[:, 0:512]
        for g in range(4):
            vec[4 * n + g : 4 * n + g + 1, :] = line[:, 512 + 256 * g : 768 + 256 * g]
    shift[...] = jnp.concatenate([vec[0:1, :], jnp.zeros((1, 256), F32), vec[1:2, :]], axis=1)
    w_kt[...] = w_qkv[:, 256:512].astype(F32).T.astype(LOW)
    w_vt[...] = w_qkv[:, 512:768].astype(F32).T.astype(LOW)
    shift_vt[...] = jnp.broadcast_to(vec[1:2, :], (HALF, 256)).T


def unpack_weights(shard, own, got):
    shape = jax.ShapeDtypeStruct
    return pl.pallas_call(
        unpack_kernel,
        out_shape=(
            shape((256, 768), LOW), shape((256, 256), LOW), shape((256, 1024), LOW), shape((1024, 256), LOW),
            shape((256, 256), LOW), shape((256, 256), LOW), shape((1, 1024), F32), shape((8, 256), F32),
            shape((1, 768), F32), shape((256, HALF), F32),
        ),
        in_specs=[smem(), vmem(), vmem()],
        out_specs=[vmem()] * 10,
        compiler_params=pltpu.CompilerParams(vmem_limit_bytes=16 * 1024 * 1024),
        name="unpack_weights",
    )(shard, own, got)


def trade(pieces):
    count = lax.axis_size("dp")
    held = [pieces[0]]
    for n in (1, 2, 3):
        pairs = [(d * 2 + s, (d ^ (n % 2)) * 2 + (s ^ (n // 2))) for d in range(count) for s in range(2)]
        held.append(lax.ppermute(pieces[n], ("dp", "shard"), pairs))
    return held


def total(pieces):
    return sum(piece.astype(F32) for piece in pieces)


def sum_rest(part, data_index):
    count = lax.axis_size("dp")
    groups = count // 4
    half = part.shape[0] // 2
    bit = (data_index // 2) % 2
    flip = [(d, d ^ 2) for d in range(count)]
    keep = lax.dynamic_slice_in_dim(part, bit * half, half, 0)
    give = lax.dynamic_slice_in_dim(part, (1 - bit) * half, half, 0)
    part = keep + lax.ppermute(give.astype(LOW), "dp", flip).astype(F32)
    at = data_index // 4
    small = half // groups
    hops = [[(d, (d + 4 * k) % count) for d in range(count)] for k in range(1, groups)]

    def piece(k):
        return lax.dynamic_slice_in_dim(part, lax.rem(at + k, groups) * small, small, 0)

    mine = piece(0)
    got = [lax.ppermute(piece(k + 1).astype(LOW), "dp", hop) for k, hop in enumerate(hops)]
    for one in got:
        mine = mine + one.astype(F32)
    mine = mine.astype(LOW)
    near = jnp.stack([mine] + [lax.ppermute(mine, "dp", hop) for hop in hops])
    core = [(d, d ^ 1) for d in range(count)]
    across = lax.ppermute(near, "dp", flip)
    near_core, across_core = lax.ppermute(near, "dp", core), lax.ppermute(across, "dp", core)
    return jnp.stack([near, across, near_core, across_core]).astype(F32)


def adam_update(grad, state, decay):
    correct_one = 1.0 - FIRST_BETA**STEP
    correct_two = 1.0 - SECOND_BETA**STEP
    first_new = FIRST_BETA * state[1] + (1.0 - FIRST_BETA) * grad
    second_new = SECOND_BETA * state[2] + (1.0 - SECOND_BETA) * grad * grad
    direction = first_new / correct_one / (jnp.sqrt(second_new / correct_two) + ADAM_EPSILON)
    master_new = state[0] - LEARNING_RATE * (direction + decay * state[0])
    return (master_new, first_new, second_new)


def update_kernel(
    where, parts, s_qkv, s_out, s_up, s_down, s_bias, s_vec,
    g_qkv, g_out, g_up, g_down, g_bias, g_vec, o_master, o_first, o_second, grads, flat, sems,
):
    groups, small = parts.shape[1:3]
    index = where[0]
    for core in range(2):
        for side in range(2):
            base = ((index % 2) ^ core) * 64 + (((index // 2) % 2) ^ side) * 32
            for k in range(groups):
                at = base + lax.rem(index // 4 + groups - k, groups) * small
                grads[pl.ds(pl.multiple_of(at, small), small), :] = parts[2 * core + side, k]
    outs = [flat.at[n] for n in range(3)]

    def place(base, grad, state, decay):
        rows, columns = grad.shape
        wide = columns // HALF
        for out, value in zip(outs, adam_update(grad, state, decay)):
            for c in range(wide):
                at = pl.ds(base + c, rows, stride=wide) if wide > 1 else pl.ds(base, rows)
                out[at, :] = value[:, c * HALF : (c + 1) * HALF]

    qkv, outer, up = grads[:, 2304:3072], grads[:, 1024:1280], grads[:, 0:1024]
    g_qkv[...] = qkv
    g_out[...] = outer
    g_up[...] = up
    place(0, qkv, s_qkv, WEIGHT_DECAY)
    place(768, outer, s_out, WEIGHT_DECAY)
    place(1024, up, s_up, WEIGHT_DECAY)
    for n in range(4):
        rows = slice(128 * n, 128 * n + 128)
        down = grads[:, 1280 + 256 * n : 1536 + 256 * n]
        g_down[rows, :] = down
        place(2048 + 256 * n, down, s_down[:, rows, :], WEIGHT_DECAY)
    extra = grads[0:16, 3072:3200]
    g_bias[...] = extra[0:4]
    place(3072, extra[0:4], s_bias, 0.0)
    vec = jnp.concatenate(
        [jnp.concatenate([extra[4 + 2 * n : 5 + 2 * n], extra[5 + 2 * n : 6 + 2 * n]], axis=1) for n in range(4)], axis=0
    )
    g_vec[...] = vec
    place(3076, vec, s_vec, 0.0)
    copies = [
        pltpu.make_async_copy(flat.at[n], there.reshape(flat.shape[1:]), sems.at[n])
        for n, there in enumerate((o_master, o_first, o_second))
    ]
    for copy in copies:
        copy.start()
    for copy in copies:
        copy.wait()


def update(data_index, parts, states):
    shape = lambda *dims: jax.ShapeDtypeStruct(dims, F32)
    s_qkv, s_out, s_up, s_down, s_bias, s_vec = states
    flat = shape(1, 3084 * HALF)
    *grads, master, first, second = pl.pallas_call(
        update_kernel,
        out_shape=(
            shape(128, 768), shape(128, 256), shape(128, 1024), shape(512, 256), shape(4, HALF), shape(4, 256),
            flat, flat, flat,
        ),
        in_specs=[smem()] + [vmem()] * 7,
        out_specs=[vmem()] * 6 + [pl.BlockSpec(memory_space=pl.ANY)] * 3,
        scratch_shapes=[
            pltpu.VMEM((128, 3200), F32), pltpu.VMEM((3, 3084, HALF), F32), pltpu.SemaphoreType.DMA((3,)),
        ],
        compiler_params=pltpu.CompilerParams(vmem_limit_bytes=VMEM_LIMIT),
        cost_estimate=pl.CostEstimate(flops=10_000_000, bytes_accessed=14_000_000, transcendentals=400_000),
        name="update",
    )(data_index.reshape(1), parts, s_qkv, s_out, s_up, s_down, s_bias.reshape(3, 4, HALF), s_vec)
    grads[4] = grads[4].reshape(-1)
    return tuple(grads) + (master, first, second)


def on_device(
    hidden, cotangent, assign, live_blocks, tail_live, random_blocks, w_qkv, w_out, w_up, w_down, up_bias, vectors,
    state_qkv, state_out, state_up, state_down, state_ubias, state_vec,
):
    shard_count = lax.axis_size("shard")
    shard_index = lax.axis_index("shard")
    data_index = lax.axis_index("dp")
    row_seqs, rows_here, width = hidden.shape
    length = row_seqs * rows_here
    shard = shard_index.reshape(1)

    def to_slot(rows):
        return lax.all_to_all(rows, "dp", split_axis=0, concat_axis=0, tiled=True).reshape(length, width)

    sent = reorder(shard, assign, hidden, False)
    x = to_slot(sent)
    pack = pack_weights((w_qkv, w_out, w_up, w_down, up_bias, vectors), sent)
    got = lax.ppermute(pack, "shard", [(0, 1), (1, 0)])
    w_qkv, w_out, w_up, w_down, w_kt, w_vt, up_shift, vec, shift, shift_vt = unpack_weights(shard, pack, got)
    slot = assign[data_index * shard_count + shard_index]
    own = shard_index * row_seqs + slot
    scal = jnp.stack([live_blocks[own], 2 * shard_index + data_index % 2])
    table = bias_table(lax.dynamic_index_in_dim(tail_live, own, 0, keepdims=False))
    drawn = random_blocks.reshape(-1)
    ready = (w_qkv, scal, table, drawn)
    cot = to_slot(reorder(shard, assign, cotangent, False, ready))
    q, k, v, kt, ctx, lse = forward_attention(scal, drawn, table, x, w_qkv, w_kt, w_vt, shift, shift_vt)
    out, *kept = ahead(scal, table, x, ctx, w_out, w_up, w_down, up_shift, vec)

    def from_slot(rows):
        return lax.all_to_all(
            rows.reshape(row_seqs, rows_here, width), "dp", split_axis=0, concat_axis=0, tiled=True
        )

    back_out = from_slot(out)
    gz1, gctx, delta, *early = behind(scal, table, cot, ctx, *kept, w_out, w_up, w_down, vec)
    early = trade(early)
    gin, *late = backward_attention(scal, drawn, table, q, k, v, kt, gctx, lse, delta, gz1, x, w_qkv)
    gin, *late = hold((gin, *late), (back_out, *early[1:]))
    back_gin = from_slot(gin)

    def sum_all(early, late, back_out):
        early, late = total(early), total(trade(late))
        sums = jnp.concatenate([early[:, :2304], late[:, :768], early[:, 2304:] + late[:, 768:]], axis=1)
        return sum_rest(sums, data_index), reorder(shard, assign, back_out, True)

    made = jax.eval_shape(sum_all, early, late, back_out)
    parts, layer_out = lax.cond(
        live_blocks[0] > 0,
        sum_all,
        lambda *unused: jax.tree.map(lambda one: jnp.zeros(one.shape, one.dtype), made),
        early, late, back_out,
    )
    updated = update(data_index, parts, (state_qkv, state_out, state_up, state_down, state_ubias, state_vec))
    input_grad = reorder(shard, assign, back_gin, True)
    return (layer_out, input_grad) + updated


def solution(mesh):
    placed = (
        P("shard", "dp", None), P("shard", "dp", None), P(), P(), P(), P(("dp", "shard"), None, None, None),
        P("shard", None), P("shard", None), P("shard", None), P("shard", None), P("shard"), P("shard", None),
        P(None, "shard", None), P(None, "shard", None), P(None, "shard", None), P(None, "shard", None),
        P(None, "shard"), P(None, "shard", None),
    )
    return jax.shard_map(
        on_device,
        mesh=mesh,
        in_specs=placed,
        out_specs=(
            P("shard", "dp", None), P("shard", "dp", None), P("shard", None), P("shard", None), P("shard", None),
            P("shard", None), P("shard"), P("shard", None), P("shard", None), P("shard", None), P("shard", None),
        ),
        check_vma=False,
    )
```

time: 374 us -> 297 us (0.79)
  Pallas kernels: 196 us -> 155 us
  local copies, waits for them, and re-layouts: 37.9 us -> 14.3 us
  waiting for transfers between devices: 78.8 us -> 73.7 us
  other arithmetic: 10.1 us -> 5.24 us
    pallas_call x2 -> x5, Pallas kernels: 99.8 us -> 72.9 us  [the longest x1 30.1 us: forward_attention(): pl.pallas_call(forward_kernel, out_shape=(rows, rows, rows, jax.ShapeDtyp...]
    pallas_call x1, Pallas kernels: 75.9 us -> 55.3 us  [backward_attention(): pl.pallas_call(backward_kernel, out_shape=(shape((length, 256), LOW),) +...]
    reshape x4 -> x1, local copies, waits for them, and re-layouts: 11.8 us -> 0.01 us  [pack_weights(): up_bias.reshape(1, -1)]
    unnamed x24 -> x55, local copies, waits for them, and re-layouts: 19.9 us -> 12.1 us
    all_to_all x2, waiting for transfers between devices: 11.6 us -> 4.57 us  [to_slot(): lax.all_to_all(rows, 'dp', split_axis=0, concat_axis=0, tiled=True)]
    pallas_call x4, Pallas kernels: 12.9 us -> 18 us  [reorder(): pl.pallas_call(functools.partial(reorder_kernel, scatter), out_shape=jax....]
    another operation x6 -> x1, other arithmetic: 4.87 us -> 0.72 us  [on_device(): scal = jnp.stack([live_blocks[own], 2 * shard_index + data_index % 2])]
    ppermute x2 -> x1, waiting for transfers between devices: 15.8 us -> 16.9 us  [on_device(): got = lax.ppermute(pack, 'shard', [(0, 1), (1, 0)])]
  transfers between devices with their start and end apart: 22 -> 21, of which waited for: 11 -> 11; matrix products, arithmetic and copies ran while one was open for 9% -> 3% of each run, Pallas kernels for 39% -> 49%
where the time goes in v3:
time: 297 us; the launch traced here: 296 us
  Pallas kernels  155 us (52%)
  waiting for transfers between devices  73.7 us (25%)
  starting transfers between devices  44.9 us (15%)
  local copies, waits for them, and re-layouts  14.3 us (5%)
  other arithmetic  5.24 us (2%)
    pallas_call x1, Pallas kernels, backward_attention(): pl.pallas_call(backward_kernel, out_shape=(shape((length, 256), LOW),) +...  55.3 us
    pallas_call x1, Pallas kernels, forward_attention(): pl.pallas_call(forward_kernel, out_shape=(rows, rows, rows, jax.ShapeDtyp...  30.1 us
    ppermute x3, waiting for transfers between devices, sum_rest(): lax.ppermute(piece(k + 1).astype(LOW), 'dp', hop)  27.1 us
    pallas_call x1, Pallas kernels, behind(): pl.pallas_call(behind_kernel, grid_spec=pltpu.PrefetchScalarGridSpec(num_...  23.2 us
    all_to_all x2, starting transfers between devices, to_slot(): lax.all_to_all(rows, 'dp', split_axis=0, concat_axis=0, tiled=True)  18.8 us
    pallas_call x1, Pallas kernels, ahead(): pl.pallas_call(ahead_kernel, grid_spec=pltpu.PrefetchScalarGridSpec(num_s...  18 us
    pallas_call x4, Pallas kernels, reorder(): pl.pallas_call(functools.partial(reorder_kernel, scatter), out_shape=jax....  18 us
    ppermute x1, waiting for transfers between devices, on_device(): got = lax.ppermute(pack, 'shard', [(0, 1), (1, 0)])  16.9 us
  transfers between devices with their start and end apart: 21, of which 11 were waited for; matrix products, arithmetic and copies ran while one was open for 3% of the time, Pallas kernels for 49%

profile of v3, /device:TPU:0, one launch (start us, length us, event | category | flops | bytes accessed | tf_op | source)
XLA Modules:
  0.0 295.7 jit_solution(6826875128704137355)
XLA Ops:
  0.7 1.6 copy-done
  2.2 5.1 %reorder.5.after = bf16[16,256,256]{2,1,0:T(8,128)(2,1)} custom-call(s32[1]{0:T(128)} %bitcast.11.where.shard, s32[32]{0:T(128)} %assign.5, bf16[16,256,256]{2,1,0:T(8,128)(2,1)S(1)} %copy-done), custom_call_target="tpu_custom_call" | custom-call | bytes 4194304 | tf_op jit(solution)/shard_map/reorder/pallas_call | solution.py:654
  7.4 7.6 %all-to-all-start.1 = ((bf16[16,256,256]{2,1,0:T(8,128)(2,1)}), bf16[16,256,256]{2,1,0:T(8,128)(2,1)}, u32[]{:S(2)}, u32[]{:S(2)}) async-start(bf16[16,256,256]{2,1,0:T(8,128)(2,1)} %reorder.5.after), calls=%async_computation.1 | async-start | bytes 4194304 | tf_op jit(solution)/shard_map/all_to_all | solution.py:887
  16.9 1.6 collective-permute-start.13
  22.1 16.9 %collective-permute-done.13.got = bf16[144,3072]{1,0:T(8,128)(2,1)} collective-permute-done((bf16[144,3072]{1,0:T(8,128)(2,1)S(1)}, bf16[144,3072]{1,0:T(8,128)(2,1)}, u32[]{:S(2)}, u32[]{:S(2)}) %collective-permute-start.13) | collective-permute-done | bytes 884768 | tf_op jit(solution)/shard_map/ppermute | solution.py:892
  38.9 1.5 unpack_weights.1
  46.5 4.9 %reorder.6 = bf16[16,256,256]{2,1,0:T(8,128)(2,1)} custom-call(s32[1]{0:T(128)} %bitcast.11.where.shard, s32[32]{0:T(128)S(1)} %copy-done.23, bf16[16,256,256]{2,1,0:T(8,128)(2,1)S(1)} %copy-done.1, bf16[256,768]{1,0:T(8,128)(2,1)S(1)} %get-tuple-element.97.rest_0_.w, s32[2]{0:T(128)S(1)} %pad_add_fusion.rest_1_.scal, ...), custom_call_target="tpu_custom_call" | custom-call | bytes 4194304 | tf_op jit(solution)/shard_map/reorder/pallas_call | solution.py:654
  51.5 4.6 %all-to-all-done.1 = bf16[16,256,256]{2,1,0:T(8,128)(2,1)} async-done(((bf16[16,256,256]{2,1,0:T(8,128)(2,1)}), bf16[16,256,256]{2,1,0:T(8,128)(2,1)}, u32[]{:S(2)}, u32[]{:S(2)}) %all-to-all-start.1) | async-done | bytes 2097184 | tf_op jit(solution)/shard_map/all_to_all | solution.py:887
  56.1 11.2 %all-to-all-start = ((bf16[16,256,256]{2,1,0:T(8,128)(2,1)}), bf16[16,256,256]{2,1,0:T(8,128)(2,1)S(1)}, u32[]{:S(2)}, u32[]{:S(2)}) async-start(bf16[16,256,256]{2,1,0:T(8,128)(2,1)} %reorder.6), calls=%async_computation | async-start | bytes 4194304 | tf_op jit(solution)/shard_map/all_to_all | solution.py:887
  67.3 30.1 %attend_forward.1 = (bf16[4096,256]{1,0:T(8,128)(2,1)}, bf16[4096,256]{1,0:T(8,128)(2,1)}, bf16[4096,256]{1,0:T(8,128)(2,1)}, bf16[256,4096]{1,0:T(8,128)(2,1)},...) custom-call(s32[2]{0:T(128)} %copy-done.10, s32[768]{0:T(1024)} %copy-done.8, f32[3,64,128]{2,1,0:T(8,128)} %copy-done.3, ...), custom_call_target="tpu_custom_call" | custom-call | flops 16000000000 | bytes 12000000 | tf_op jit(solution)/shard_map/attend_forward/pallas_call | solution.py:265
  97.4 18.0 %ahead.1 = (bf16[4096,256]{1,0:T(8,128)(2,1)}, f32[4096,256]{1,0:T(8,128)}, f32[4096,256]{1,0:T(8,128)}, f32[4096,128]{1,0:T(8,128)}, bf16[4096,1024]{1,0:T(8,128)(2,1)}, /*index=5*/bf16[4096,1024]{1,0:T(8,128)(2,1)}) custom-call(s32[2]{0:T(128)} %copy-done.10, f32[3,64,128]{2,1,0:T(8,128)} %copy-done.3, bf16[4096,256]{1,0:T(8,128)(2,1)} %bitcast.13.x, ...), custom_call_target="tpu_custom_call" | custom-call | flops 5000000000 | bytes 34000000 | tf_op jit(solution)/shard_map/ahead/pallas_call | solution.py:356
  116.8 6.0 %all-to-all-start.2 = ((bf16[16,256,256]{2,1,0:T(8,128)(2,1)}), bf16[16,256,256]{2,1,0:T(8,128)(2,1)S(1)}, u32[]{:S(2)}, u32[]{:S(2)}) async-start(bf16[16,256,256]{2,1,0:T(8,128)(2,1)} %bitcast.22), calls=%async_computation.2 | async-start | bytes 4194304 | tf_op jit(solution)/shard_map/all_to_all | solution.py:905
  122.8 23.2 %behind.1 = (f32[4096,256]{1,0:T(8,128)}, bf16[4096,256]{1,0:T(8,128)(2,1)}, f32[64,256]{1,0:T(8,128)}, bf16[64,2432]{1,0:T(8,128)(2,1)}, bf16[64,2432]{1,0:T(8,...) custom-call(s32[2]{0:T(128)} %copy-done.10, f32[3,64,128]{2,1,0:T(8,128)} %copy-done.3, ...), custom_call_target="tpu_custom_call" | custom-call | flops 10000000000 | bytes 40000000 | tf_op jit(solution)/shard_map/behind/pallas_call | solution.py:469
  146.5 1.5 collective-permute-start.15
  148.0 55.3 %attend_backward.1 = (bf16[4096,256]{1,0:T(8,128)(2,1)}, bf16[64,896]{1,0:T(8,128)(2,1)S(1)}, bf16[64,896]{1,0:T(8,128)(2,1)}, bf16[64,896]{1,0:T(8,128)(2,1)}, bf16[64,896]{1,0:T(8,128)(2,1)}) custom-call(s32[2]{0:T(128)} %copy-done.10, s32[768]{0:T(1024)} %copy-done.8, f32[3,64,128]{2,1,0:T(8,128)} %copy-done.3, bf16[4096,256]{1,0:T(8,128)(2,1)} %get-tuple-element.117.q, ...), custom_call_target="tpu_custom_call" | custom-call | flops 40000000000 | bytes 20000000 | tf_op jit(solution)/shard_map/attend_backward/pallas_call | solution.py:607
  204.6 6.1 %all-to-all-start.3 = ((bf16[16,256,256]{2,1,0:T(8,128)(2,1)}), bf16[16,256,256]{2,1,0:T(8,128)(2,1)S(1)}, u32[]{:S(2)}, u32[]{:S(2)}) async-start(bf16[16,256,256]{2,1,0:T(8,128)(2,1)} %bitcast.21), calls=%async_computation.3 | async-start | bytes 4194304 | tf_op jit(solution)/shard_map/all_to_all | solution.py:905
  212.1 69.9 %conditional.1 = (f32[4,4,8,3200]{3,2,1,0:T(8,128)}, bf16[16,256,256]{2,1,0:T(8,128)(2,1)}) conditional(s32[]{:T(128)} %bitcast.8, () %tuple.16, (bf16[64,2432]{1,0:T(8,128)(2,1)}, bf16[64,2432]{1,0:T(8,128)(2,1)S(1)}, bf16[64,2432]{1,0:T(8,128)(2,1)S(1)}, bf16[64,2432]{1,0:T(8,128)(2,1)}, bf16[64,896]{1,0:T(8,128)(2,1)S(1)}, ...), branch_computations={%region_0.1_spmd, %region_1.2_spmd} | conditional | flops 4238424 | bytes 21521910 | solution.py:922
  212.1 1.5 collective-permute-start.2
  215.4 2.0 collective-permute-done.2
  217.4 2.9 collective-permute-done.1
  221.6 2.0 collective-permute-start.3
  223.6 11.4 %collective-permute-done.3 = bf16[32,3200]{1,0:T(8,128)(2,1)S(1)} collective-permute-done((bf16[32,3200]{1,0:T(8,128)(2,1)S(1)}, bf16[32,3200]{1,0:T(8,128)(2,1)S(1)}, u32[]{:S(2)}, u32[]{:S(2)}) %collective-permute-start.3) | collective-permute-done | bytes 204832 | tf_op jit(solution)/shard_map/cond/branch_1_fun/ppermute | solution.py:770
  237.1 9.8 %collective-permute-done.6 = bf16[8,3200]{1,0:T(8,128)(2,1)S(1)} collective-permute-done((bf16[8,3200]{1,0:T(8,128)(2,1)S(1)}, bf16[8,3200]{1,0:T(8,128)(2,1)S(1)}, u32[]{:S(2)}, u32[]{:S(2)}) %collective-permute-start.6) | collective-permute-done | bytes 51232 | tf_op jit(solution)/shard_map/cond/branch_1_fun/ppermute | solution.py:779
  247.0 17.3 %collective-permute-done.5 = bf16[8,3200]{1,0:T(8,128)(2,1)S(1)} collective-permute-done((bf16[8,3200]{1,0:T(8,128)(2,1)S(1)}, bf16[8,3200]{1,0:T(8,128)(2,1)S(1)}, u32[]{:S(2)}, u32[]{:S(2)}) %collective-permute-start.5) | collective-permute-done | bytes 51232 | tf_op jit(solution)/shard_map/cond/branch_1_fun/ppermute | solution.py:779
  266.9 1.9 collective-permute-done.9
  268.8 1.5 collective-permute-done.8
  270.3 1.3 collective-permute-done.7
  271.7 1.6 collective-permute-start.10
  273.3 4.2 %collective-permute-done.10 = bf16[4,8,3200]{2,1,0:T(8,128)(2,1)S(1)} collective-permute-done((bf16[4,8,3200]{2,1,0:T(8,128)(2,1)S(1)}, bf16[4,8,3200]{2,1,0:T(8,128)(2,1)S(1)}, u32[]{:S(2)}, u32[]{:S(2)}) %collective-permute-start.10) | collective-permute-done | bytes 204832 | tf_op jit(solution)/shard_map/cond/branch_1_fun/ppermute | solution.py:785
  277.5 3.1 %reorder.4 = bf16[16,256,256]{2,1,0:T(8,128)(2,1)} custom-call(s32[1]{0:T(128)} %get-tuple-element.33.where, s32[32]{0:T(128)S(1)} %get-tuple-element.34.assign, bf16[16,256,256]{2,1,0:T(8,128)(2,1)} %get-tuple-element.35.src), custom_call_target="tpu_custom_call" | custom-call | bytes 4194304 | tf_op jit(solution)/shard_map/cond/branch_1_fun/reorder/pallas_call | solution.py:654
  282.0 8.7 %update.1 = (f32[128,768]{1,0:T(8,128)}, f32[128,256]{1,0:T(8,128)}, f32[128,1024]{1,0:T(8,128)}, f32[512,256]{1,0:T(8,128)}, f32[4,128]{1,0:T(4,128)}, /*index=...) custom-call(s32[1]{0:T(128)} %bitcast.16.where, ...), custom_call_target="tpu_custom_call" | custom-call | flops 10000000 | bytes 14000000 | tf_op jit(solution)/shard_map/update/pallas_call | solution.py:856
  290.6 4.9 %reorder.7 = bf16[16,256,256]{2,1,0:T(8,128)(2,1)} custom-call(s32[1]{0:T(128)} %bitcast.11.where.shard, s32[32]{0:T(128)S(1)} %copy-done.23, bf16[16,256,256]{2,1,0:T(8,128)(2,1)S(1)} %all-to-all-done.3.src), custom_call_target="tpu_custom_call" | custom-call | bytes 4194304 | tf_op jit(solution)/shard_map/reorder/pallas_call | solution.py:654
  (103 shorter events, 23.8 us)
Async XLA Ops:
  7.3 7.6 %copy-start.27 = (bf16[512]{0:T(512)(128)(2,1)S(1)}, bf16[512]{0:T(512)(128)(2,1)}, u32[]{:S(2)}) copy-start(bf16[512]{0:T(512)(128)(2,1)} %param.30) | copy-start | bytes 3076
  7.3 7.7 %copy-start.4 = (bf16[128,1024]{1,0:T(8,128)(2,1)S(1)}, bf16[128,1024]{1,0:T(8,128)(2,1)}, u32[]{:S(2)}) copy-start(bf16[128,1024]{1,0:T(8,128)(2,1)} %w_up.1) | copy-start | bytes 786436
  7.3 7.7 %copy-start.5 = (bf16[512,256]{1,0:T(8,128)(2,1)S(1)}, bf16[512,256]{1,0:T(8,128)(2,1)}, u32[]{:S(2)}) copy-start(bf16[512,256]{1,0:T(8,128)(2,1)} %w_down.1) | copy-start | bytes 786436
  7.3 7.7 %copy-start.9 = (bf16[4,256]{1,0:T(4,128)(2,1)S(1)}, bf16[4,256]{1,0:T(4,128)(2,1)}, u32[]{:S(2)}) copy-start(bf16[4,256]{1,0:T(4,128)(2,1)} %vectors.1) | copy-start | bytes 6148
  7.4 48.7 %all-to-all-start.1 = ((bf16[16,256,256]{2,1,0:T(8,128)(2,1)}), bf16[16,256,256]{2,1,0:T(8,128)(2,1)}, u32[]{:S(2)}, u32[]{:S(2)}) async-start(bf16[16,256,256]{2,1,0:T(8,128)(2,1)} %reorder.5.after), calls=%async_computation.1 | async-start | bytes 4194304 | tf_op jit(solution)/shard_map/all_to_all | solution.py:887
  15.0 5.8 %copy-start.26 = (s32[32]{0:T(128)S(1)}, s32[32]{0:T(128)}, u32[]{:S(2)}) copy-start(s32[32]{0:T(128)} %param.23) | copy-start | bytes 388
  16.8 29.7 %copy-start.1 = (bf16[16,256,256]{2,1,0:T(8,128)(2,1)S(1)}, bf16[16,256,256]{2,1,0:T(8,128)(2,1)}, u32[]{:S(2)}) copy-start(bf16[16,256,256]{2,1,0:T(8,128)(2,1)} %src.3) | copy-start | bytes 6291460
  16.9 22.1 %collective-permute-start.13 = (bf16[144,3072]{1,0:T(8,128)(2,1)S(1)}, bf16[144,3072]{1,0:T(8,128)(2,1)}, u32[]{:S(2)}, u32[]{:S(2)}) collective-permute-start(bf16[144,3072]{1,0:T(8,128)(2,1)S(1)} %pack_weights.1.own), channel_id=1, source_target_pairs={{0,1},{1,0},{2,3},{3,2},{4,5},{5,4},{6,7},{7,6},{8,9},{9,8},{10,11... | collective-permute-start | bytes 2654216 | tf_op jit(solution)/shard_map/ppermute | solution.py:892
  20.0 31.5 %copy-start.8 = (s32[768]{0:T(1024)}, s32[768]{0:T(1024)S(1)}, u32[]{:S(2)}) copy-start(s32[768]{0:T(1024)S(1)} %reshape.59.rest_3_.drawn) | copy-start | bytes 9220
  22.0 29.5 %copy-start.10 = (s32[2]{0:T(128)}, s32[2]{0:T(128)S(1)}, u32[]{:S(2)}) copy-start(s32[2]{0:T(128)S(1)} %pad_add_fusion.rest_1_.scal) | copy-start | bytes 28
  46.4 5.1 %copy-start.2 = (bf16[256,768]{1,0:T(8,128)(2,1)}, bf16[256,768]{1,0:T(8,128)(2,1)S(1)}, u32[]{:S(2)}) copy-start(bf16[256,768]{1,0:T(8,128)(2,1)S(1)} %get-tuple-element.97.rest_0_.w) | copy-start | bytes 1179652
  46.5 5.0 %copy-start.3 = (f32[3,64,128]{2,1,0:T(8,128)}, f32[3,64,128]{2,1,0:T(8,128)S(1)}, u32[]{:S(2)}) copy-start(f32[3,64,128]{2,1,0:T(8,128)S(1)} %broadcast_in_dim.13.rest_2_.table) | copy-start | bytes 294916
  56.1 59.3 %all-to-all-start = ((bf16[16,256,256]{2,1,0:T(8,128)(2,1)}), bf16[16,256,256]{2,1,0:T(8,128)(2,1)S(1)}, u32[]{:S(2)}, u32[]{:S(2)}) async-start(bf16[16,256,256]{2,1,0:T(8,128)(2,1)} %reorder.6), calls=%async_computation | async-start | bytes 4194304 | tf_op jit(solution)/shard_map/all_to_all | solution.py:887
  116.8 86.5 %all-to-all-start.2 = ((bf16[16,256,256]{2,1,0:T(8,128)(2,1)}), bf16[16,256,256]{2,1,0:T(8,128)(2,1)S(1)}, u32[]{:S(2)}, u32[]{:S(2)}) async-start(bf16[16,256,256]{2,1,0:T(8,128)(2,1)} %bitcast.22), calls=%async_computation.2 | async-start | bytes 4194304 | tf_op jit(solution)/shard_map/all_to_all | solution.py:905
  146.0 57.2 %collective-permute-start.14 = (bf16[64,2432]{1,0:T(8,128)(2,1)}, bf16[64,2432]{1,0:T(8,128)(2,1)S(1)}, u32[]{:S(2)}, u32[]{:S(2)}) collective-permute-start(bf16[64,2432]{1,0:T(8,128)(2,1)} %get-tuple-element.114), channel_id=1, source_target_pairs={{0,2},{1,3},{2,0},{3,1},{4,6},{5,7},{6,4},{7,5},{8,10},{9,11},{10,... | collective-permute-start | bytes 933896 | tf_op jit(solution)/shard_map/ppermute | solution.py:754
  146.5 56.8 %collective-permute-start.15 = (bf16[64,2432]{1,0:T(8,128)(2,1)}, bf16[64,2432]{1,0:T(8,128)(2,1)S(1)}, u32[]{:S(2)}, u32[]{:S(2)}) collective-permute-start(bf16[64,2432]{1,0:T(8,128)(2,1)} %get-tuple-element.115), channel_id=1, source_target_pairs={{0,1},{1,0},{2,3},{3,2},{4,5},{5,4},{6,7},{7,6},{8,9},{9,8},{10,11... | collective-permute-start | bytes 933896 | tf_op jit(solution)/shard_map/ppermute | solution.py:754
  148.0 55.3 %collective-permute-start.16 = (bf16[64,2432]{1,0:T(8,128)(2,1)}, bf16[64,2432]{1,0:T(8,128)(2,1)}, u32[]{:S(2)}, u32[]{:S(2)}) collective-permute-start(bf16[64,2432]{1,0:T(8,128)(2,1)} %get-tuple-element.116), channel_id=1, source_target_pairs={{0,3},{1,2},{2,1},{3,0},{4,7},{5,6},{6,5},{7,4},{8,11},{9,10},{10,... | collective-permute-start | bytes 933896 | tf_op jit(solution)/shard_map/ppermute | solution.py:754
  204.6 6.8 %copy-start.24 = (f32[3,512]{1,0:T(4,128)S(1)}, f32[3,512]{1,0:T(4,128)}, u32[]{:S(2)}) copy-start(f32[3,512]{1,0:T(4,128)} %param.36) | copy-start | bytes 18436
  204.6 86.0 %all-to-all-start.3 = ((bf16[16,256,256]{2,1,0:T(8,128)(2,1)}), bf16[16,256,256]{2,1,0:T(8,128)(2,1)S(1)}, u32[]{:S(2)}, u32[]{:S(2)}) async-start(bf16[16,256,256]{2,1,0:T(8,128)(2,1)} %bitcast.21), calls=%async_computation.3 | async-start | bytes 4194304 | tf_op jit(solution)/shard_map/all_to_all | solution.py:905
  212.1 5.3 %collective-permute-start.2 = (bf16[64,896]{1,0:T(8,128)(2,1)}, bf16[64,896]{1,0:T(8,128)(2,1)}, u32[]{:S(2)}, u32[]{:S(2)}) collective-permute-start(bf16[64,896]{1,0:T(8,128)(2,1)} %get-tuple-element.31), channel_id=1, source_target_pairs={{0,3},{1,2},{2,1},{3,0},{4,7},{5,6},{6,5},{7,4},{8,11},{9,10},{10,... | collective-permute-start | bytes 344072 | tf_op jit(solution)/shard_map/cond/branch_1_fun/ppermute | solution.py:754
  213.6 6.7 %collective-permute-start.1 = (bf16[64,896]{1,0:T(8,128)(2,1)}, bf16[64,896]{1,0:T(8,128)(2,1)}, u32[]{:S(2)}, u32[]{:S(2)}) collective-permute-start(bf16[64,896]{1,0:T(8,128)(2,1)} %get-tuple-element.30), channel_id=1, source_target_pairs={{0,1},{1,0},{2,3},{3,2},{4,5},{5,4},{6,7},{7,6},{8,9},{9,8},{10,11... | collective-permute-start | bytes 344072 | tf_op jit(solution)/shard_map/cond/branch_1_fun/ppermute | solution.py:754
  214.1 6.2 %collective-permute-start = (bf16[64,896]{1,0:T(8,128)(2,1)}, bf16[64,896]{1,0:T(8,128)(2,1)}, u32[]{:S(2)}, u32[]{:S(2)}) collective-permute-start(bf16[64,896]{1,0:T(8,128)(2,1)} %get-tuple-element.29), channel_id=1, source_target_pairs={{0,2},{1,3},{2,0},{3,1},{4,6},{5,7},{6,4},{7,5},{8,10},{9,11},{10,... | collective-permute-start | bytes 344072 | tf_op jit(solution)/shard_map/cond/branch_1_fun/ppermute | solution.py:754
  221.6 13.4 %collective-permute-start.3 = (bf16[32,3200]{1,0:T(8,128)(2,1)S(1)}, bf16[32,3200]{1,0:T(8,128)(2,1)S(1)}, u32[]{:S(2)}, u32[]{:S(2)}) collective-permute-start(bf16[32,3200]{1,0:T(8,128)(2,1)S(1)} %dynamic-slice_convert_fusion), channel_id=1, source_target_pairs={{0,4},{2,6},{4,0},{6,2},{8,12},{10,14},{12,8},{14,10},{16,20},{18,... | collective-permute-start | bytes 614408 | tf_op jit(solution)/shard_map/cond/branch_1_fun/ppermute | solution.py:770
  235.0 11.9 %collective-permute-start.6 = (bf16[8,3200]{1,0:T(8,128)(2,1)S(1)}, bf16[8,3200]{1,0:T(8,128)(2,1)S(1)}, u32[]{:S(2)}, u32[]{:S(2)}) collective-permute-start(bf16[8,3200]{1,0:T(8,128)(2,1)S(1)} %get-tuple-element.148), channel_id=1, source_target_pairs={{0,24},{2,26},{4,28},{6,30},{8,0},{10,2},{12,4},{14,6},{16,8},{18,... | collective-permute-start | bytes 153608 | tf_op jit(solution)/shard_map/cond/branch_1_fun/ppermute | solution.py:779
  236.0 28.2 %collective-permute-start.5 = (bf16[8,3200]{1,0:T(8,128)(2,1)S(1)}, bf16[8,3200]{1,0:T(8,128)(2,1)S(1)}, u32[]{:S(2)}, u32[]{:S(2)}) collective-permute-start(bf16[8,3200]{1,0:T(8,128)(2,1)S(1)} %get-tuple-element.149), channel_id=1, source_target_pairs={{0,16},{2,18},{4,20},{6,22},{8,24},{10,26},{12,28},{14,30},{16,0},... | collective-permute-start | bytes 153608 | tf_op jit(solution)/shard_map/cond/branch_1_fun/ppermute | solution.py:779
  236.0 28.2 %collective-permute-start.4 = (bf16[8,3200]{1,0:T(8,128)(2,1)S(1)}, bf16[8,3200]{1,0:T(8,128)(2,1)S(1)}, u32[]{:S(2)}, u32[]{:S(2)}) collective-permute-start(bf16[8,3200]{1,0:T(8,128)(2,1)S(1)} %get-tuple-element.147), channel_id=1, source_target_pairs={{0,8},{2,10},{4,12},{6,14},{8,16},{10,18},{12,20},{14,22},{16,24},... | collective-permute-start | bytes 153608 | tf_op jit(solution)/shard_map/cond/branch_1_fun/ppermute | solution.py:779
  264.3 4.6 %collective-permute-start.9 = (bf16[8,3200]{1,0:T(8,128)(2,1)S(1)}, bf16[8,3200]{1,0:T(8,128)(2,1)S(1)}, u32[]{:S(2)}, u32[]{:S(2)}) collective-permute-start(bf16[8,3200]{1,0:T(8,128)(2,1)S(1)} %add_convert_fusion), channel_id=1, source_target_pairs={{0,24},{2,26},{4,28},{6,30},{8,0},{10,2},{12,4},{14,6},{16,8},{18,... | collective-permute-start | bytes 153608 | tf_op jit(solution)/shard_map/cond/branch_1_fun/ppermute | solution.py:783
  265.2 5.1 %collective-permute-start.8 = (bf16[8,3200]{1,0:T(8,128)(2,1)S(1)}, bf16[8,3200]{1,0:T(8,128)(2,1)S(1)}, u32[]{:S(2)}, u32[]{:S(2)}) collective-permute-start(bf16[8,3200]{1,0:T(8,128)(2,1)S(1)} %add_convert_fusion), channel_id=1, source_target_pairs={{0,16},{2,18},{4,20},{6,22},{8,24},{10,26},{12,28},{14,30},{16,0},... | collective-permute-start | bytes 153608 | tf_op jit(solution)/shard_map/cond/branch_1_fun/ppermute | solution.py:783
  265.7 5.9 %collective-permute-start.7 = (bf16[8,3200]{1,0:T(8,128)(2,1)S(1)}, bf16[8,3200]{1,0:T(8,128)(2,1)S(1)}, u32[]{:S(2)}, u32[]{:S(2)}) collective-permute-start(bf16[8,3200]{1,0:T(8,128)(2,1)S(1)} %add_convert_fusion), channel_id=1, source_target_pairs={{0,8},{2,10},{4,12},{6,14},{8,16},{10,18},{12,20},{14,22},{16,24},... | collective-permute-start | bytes 153608 | tf_op jit(solution)/shard_map/cond/branch_1_fun/ppermute | solution.py:783
  271.7 5.8 %collective-permute-start.10 = (bf16[4,8,3200]{2,1,0:T(8,128)(2,1)S(1)}, bf16[4,8,3200]{2,1,0:T(8,128)(2,1)S(1)}, u32[]{:S(2)}, u32[]{:S(2)}) collective-permute-start(bf16[4,8,3200]{2,1,0:T(8,128)(2,1)S(1)} %get-tuple-element.151), channel_id=1, source_target_pairs={{0,4},{2,6},{4,0},{6,2},{8,12},{10,14},{12,8},{14,10},{16,20},{18,... | collective-permute-start | bytes 614408 | tf_op jit(solution)/shard_map/cond/branch_1_fun/ppermute | solution.py:785
  273.3 7.3 %collective-permute-start.11 = (bf16[4,8,3200]{2,1,0:T(8,128)(2,1)S(1)}, bf16[4,8,3200]{2,1,0:T(8,128)(2,1)S(1)}, u32[]{:S(2)}, u32[]{:S(2)}) collective-permute-start(bf16[4,8,3200]{2,1,0:T(8,128)(2,1)S(1)} %get-tuple-element.151), channel_id=1, source_target_pairs={{0,2},{2,0},{4,6},{6,4},{8,10},{10,8},{12,14},{14,12},{16,18},{18,... | collective-permute-start | bytes 614408 | tf_op jit(solution)/shard_map/cond/branch_1_fun/ppermute | solution.py:786
  277.5 3.1 %collective-permute-start.12 = (bf16[4,8,3200]{2,1,0:T(8,128)(2,1)S(1)}, bf16[4,8,3200]{2,1,0:T(8,128)(2,1)S(1)}, u32[]{:S(2)}, u32[]{:S(2)}) collective-permute-start(bf16[4,8,3200]{2,1,0:T(8,128)(2,1)S(1)} %collective-permute-done.10), channel_id=1, source_target_pairs={{0,2},{2,0},{4,6},{6,4},{8,10},{10,8},{12,14},{14,12},{16,18},{18,... | collective-permute-start | bytes 614408 | tf_op jit(solution)/shard_map/cond/branch_1_fun/ppermute | solution.py:786
  (17 other events, 20.5 us)

commit v4 on v3

--- a/solution.py
+++ b/solution.py
@@ -186,7 +186,7 @@
         vt[:, rows] = (dot_nt(w_vt[...], xc) + shift_vt[:, 0:1]).astype(LOW)
         return 0
 
-    lax.fori_loop(0, length // 512, project, 0)
+    lax.fori_loop(0, length // 512, project, 0, unroll=2)
     copies = [
         pltpu.make_async_copy(here, there, sems.at[n])
         for n, (here, there) in enumerate(((q_v, q_o), (k_v, k_o), (v_v, v_o), (kt_v, kt_o)))
@@ -229,7 +229,7 @@
             out.append(jnp.maximum(peaks[g], jnp.max(s, axis=0, keepdims=True)))
         return tuple(out)
 
-    peaks = lax.fori_loop(0, length // 512, score, (jnp.full((1, 256), MASK_VALUE, F32),) * 2)
+    peaks = lax.fori_loop(0, length // 512, score, (jnp.full((1, 256), MASK_VALUE, F32),) * 2, unroll=2)
 
     og[...] = jnp.zeros_like(og)
 
@@ -242,7 +242,7 @@
             og[g] += dot_nn(vt[:, rows], e.astype(LOW))
         return tuple(out)
 
-    totals = lax.fori_loop(0, length // 512, mix, (jnp.zeros((1, 256), F32),) * 2)
+    totals = lax.fori_loop(0, length // 512, mix, (jnp.zeros((1, 256), F32),) * 2, unroll=2)
     for g in range(2):
         ctx_o[g * 64 : g * 64 + 64, :] = pick_turned(og[g] * (1.0 / totals[g])).astype(LOW)
         lse_o[g : g + 1, :] = peaks[g] + jnp.log(totals[g])
@@ -289,6 +289,10 @@
 
 def normalize(summed):
     center = summed - jnp.mean(summed, axis=-1, keepdims=True)
+    return (*scaled(center), center)
+
+
+def scaled(center):
     factor = lax.rsqrt(jnp.mean(center * center, axis=-1, keepdims=True) + NORM_EPSILON)
     return (center * factor, factor)
 
@@ -304,9 +308,8 @@
 ROOT_HALF = 0.7071067811865476
 
 
-def gelu_parts(v):
-    cumulative = 0.5 * (1.0 + lax.erf(v * ROOT_HALF))
-    return v * cumulative, cumulative + v * (NORMAL_PEAK * jnp.exp(-0.5 * v * v))
+def gelu_weight(v):
+    return 0.5 * (1.0 + lax.erf(v * ROOT_HALF))
 
 
 def open_rows(table, scal, rows):
@@ -319,26 +322,25 @@
     return jnp.concatenate(marks, axis=0) == 0.0
 
 
-def ahead_kernel(scal, table, x, ctx, w_out, w_up, w_down, up_shift, vec, out_o, one_o, two_o, stat_o, act_o, slope_o):
+def ahead_kernel(scal, table, x, ctx, w_out, w_up, w_down, up_shift, vec, out_o, one_o, two_o, act, slope_o):
     rows = x.shape[0]
 
     def row(n):
         return vec[n : n + 1, :]
 
     attended = dot_nn(ctx[...], w_out[...]) + row(2)
-    normed_one, factor_one = normalize(x[...].astype(F32) + attended)
-    one_o[...] = normed_one
+    normed_one, _, center = normalize(x[...].astype(F32) + attended)
+    one_o[...] = center.astype(LOW)
     first_out = normed_one * row(3) + row(4)
     first_low = first_out.astype(LOW)
     for c in range(0, 1024, 256):
         pre = dot_nn(first_low, w_up[:, c : c + 256]) + up_shift[:, c : c + 256]
-        a, s = gelu_parts(pre)
-        act_o[:, c : c + 256] = a.astype(LOW)
-        slope_o[:, c : c + 256] = s.astype(LOW)
-    branch = dot_nn(act_o[...], w_down[...]) + row(5)
-    normed_two, factor_two = normalize(first_out + branch)
-    two_o[...] = normed_two
-    stat_o[...] = jnp.where(first_half(rows), factor_one, factor_two)
+        weight = gelu_weight(pre)
+        act[:, c : c + 256] = (pre * weight).astype(LOW)
+        slope_o[:, c : c + 256] = (weight + pre * (NORMAL_PEAK * jnp.exp(-0.5 * pre * pre))).astype(LOW)
+    branch = dot_nn(act[...], w_down[...]) + row(5)
+    normed_two, _, center = normalize(first_out + branch)
+    two_o[...] = center.astype(LOW)
     out_o[...] = jnp.where(open_rows(table, scal, rows), normed_two * row(6) + row(7), 0.0).astype(LOW)
 
 
@@ -362,11 +364,11 @@
                 whole(3, 64, 128), wide(256), wide(256), whole(256, 256), whole(256, 1024), whole(1024, 256),
                 whole(1, 1024), whole(8, 256),
             ],
-            out_specs=[wide(256), wide(256), wide(256), wide(HALF), wide(1024), wide(1024)],
+            out_specs=[wide(256), wide(256), wide(256), wide(1024), wide(1024)],
         ),
         out_shape=(
-            shape((length, 256), LOW), shape((length, 256), F32), shape((length, 256), F32),
-            shape((length, HALF), F32), shape((length, 1024), LOW), shape((length, 1024), LOW),
+            shape((length, 256), LOW), shape((length, 256), LOW), shape((length, 256), LOW),
+            shape((length, 1024), LOW), shape((length, 1024), LOW),
         ),
         compiler_params=pltpu.CompilerParams(vmem_limit_bytes=VMEM_LIMIT),
         cost_estimate=pl.CostEstimate(flops=5_000_000_000, bytes_accessed=34_000_000, transcendentals=10_000_000),
@@ -375,8 +377,8 @@
 
 
 def behind_kernel(
-    scal, table, cot, ctx, one, two, stat, act, slope, w_out, w_up, w_down, vec,
-    gz1_o, gctx_o, delta_o, pack0, pack1, pack2, pack3, gdown_o, gup_o, gout_o, gub_o, gvec_o, pre,
+    scal, table, cot, ctx, one, two, act, slope, w_out, w_up, w_down, vec,
+    gz1_o, gctx_o, delta_o, pack0, pack1, pack2, pack3, gdown_o, gup_o, gout_o, gub_o, gvec_o, back,
 ):
     step = pl.program_id(0)
     rows = cot.shape[0]
@@ -389,8 +391,8 @@
     def row(n):
         return vec[n : n + 1, :]
 
-    normed_one, normed_two = one[...], two[...]
-    factor_one, factor_two = stat[:, 0:1], stat[:, BLOCK : BLOCK + 1]
+    normed_one, factor_one = scaled(one[...].astype(F32))
+    normed_two, factor_two = scaled(two[...].astype(F32))
     first_low = (normed_one * row(3) + row(4)).astype(LOW)
     grad_y = jnp.where(open_rows(table, scal, rows), cot[...].astype(F32), 0.0)
     grad_z2 = normalize_back(grad_y * row(6), normed_two, factor_two)
@@ -398,11 +400,11 @@
     for c in range(0, 1024, 256):
         grad_act = dot_nt(grad_branch, w_down[c : c + 256, :])
         grad_pre = (grad_act * slope[:, c : c + 256].astype(F32)).astype(LOW)
-        pre[:, c : c + 256] = grad_pre
+        back[:, c : c + 256] = grad_pre
         gub_o[:, c : c + 256] += jnp.sum(grad_pre.astype(F32), axis=0, keepdims=True)
     gdown_o[...] += dot_tn(act[...], grad_branch)
-    grad_first = grad_z2 + dot_nt(pre[...], w_up[...])
-    gup_o[...] += dot_tn(first_low, pre[...])
+    grad_first = grad_z2 + dot_nt(back[...], w_up[...])
+    gup_o[...] += dot_tn(first_low, back[...])
     grad_z1 = normalize_back(grad_first * row(3), normed_one, factor_one)
     gz1_o[...] = grad_z1
     grad_attended = grad_z1.astype(LOW)
@@ -455,7 +457,7 @@
     pack[16:64, at : at + HALF] = jnp.zeros((48, HALF), LOW)
 
 
-def behind(scal, table, cot, ctx, one, two, stat, act, slope, w_out, w_up, w_down, vec):
+def behind(scal, table, cot, ctx, one, two, act, slope, w_out, w_up, w_down, vec):
     length = cot.shape[0]
     rows = BEHIND_ROWS
 
@@ -472,7 +474,7 @@
             num_scalar_prefetch=1,
             grid=(length // rows,),
             in_specs=[
-                whole(3, 64, 128), wide(256), wide(256), wide(256), wide(256), wide(HALF), wide(1024), wide(1024),
+                whole(3, 64, 128), wide(256), wide(256), wide(256), wide(256), wide(1024), wide(1024),
                 whole(256, 256), whole(256, 1024), whole(1024, 256), whole(8, 256),
             ],
             out_specs=[
@@ -490,7 +492,7 @@
         compiler_params=pltpu.CompilerParams(vmem_limit_bytes=VMEM_LIMIT),
         cost_estimate=pl.CostEstimate(flops=10_000_000_000, bytes_accessed=40_000_000, transcendentals=0),
         name="behind",
-    )(scal, table, cot, ctx, one, two, stat, act, slope, w_out, w_up, w_down, vec)
+    )(scal, table, cot, ctx, one, two, act, slope, w_out, w_up, w_down, vec)
 
 
 def backward_kernel(
@@ -517,31 +519,43 @@
     def group(idx):
         units = [Unit(i, live, drawn, blocks) for i in idx]
         spreads = [spread(i) for i in idx]
-        every = range(len(idx))
-        s = [dot_nt(slot_rows(units[u], k), spreads[u][1]) for u in every]
-        g = [dot_nt(slot_rows(units[u], v), spreads[u][2]) for u in every]
-        p = [jnp.exp(s[u] + units[u].bias(table, range(8)) - lse[pl.ds(idx[u], 1), :]) for u in every]
-        ds = [(p[u] * (g[u] - delta[pl.ds(idx[u], 1), :])).astype(LOW) for u in every]
-        dvs = [dot_nn(p[u].astype(LOW), spreads[u][2]) for u in every]
-        dks = [dot_nn(ds[u], spreads[u][1]) for u in every]
-        dqs = [dot_nn(slot_turned(units[u], kt[:, 0:128], turned), ds[u]) for u in every]
         low = first_half(BLOCK)
-        for u in every:
-            for acc, terms_ in ((dk, dks[u]), (dv, dvs[u])):
-                acc[0:128, :] += terms_[0:128, :]
-                for n in range(2, 8):
-                    one = terms_[n * 64 : n * 64 + 64, :]
-                    if n < 5:
-                        at = pl.ds(pl.multiple_of(units[u].near[n - 2] * BLOCK, BLOCK), BLOCK)
-                        acc[at, :] += one
-                    else:
-                        for h in range(4):
-                            t = h // 2
-                            at = pl.ds(pl.multiple_of(units[u].chosen[n - 5][h] * BLOCK, BLOCK), BLOCK)
-                            cols = pl.ds(t * HALF, HALF)
-                            mine = low if h % 2 == 0 else jnp.logical_not(low)
-                            acc[at, cols] += jnp.where(mine, one[:, t * HALF : t * HALF + HALF], 0.0)
-            dq[spreads[u][0], :] = (pick_turned(dqs[u]) * QUERY_SCALE).astype(LOW)
+        s, g, p, ds, dvs, dks, dqs = {}, {}, {}, {}, {}, {}, {}
+        count = len(idx)
+        for t in range(count + 1):
+            u = t - 0
+            if 0 <= u < count:
+                s[u] = dot_nt(slot_rows(units[u], k), spreads[u][1])
+            u = t - 0
+            if 0 <= u < count:
+                g[u] = dot_nt(slot_rows(units[u], v), spreads[u][2])
+            u = t - 0
+            if 0 <= u < count:
+                e = jnp.exp(s[u] + units[u].bias(table, range(8)) - lse[pl.ds(idx[u], 1), :])
+                ds[u] = (e * (g[u] - delta[pl.ds(idx[u], 1), :])).astype(LOW)
+                p[u] = e.astype(LOW)
+            u = t - 0
+            if 0 <= u < count:
+                dvs[u] = dot_nn(p[u], spreads[u][2])
+                dks[u] = dot_nn(ds[u], spreads[u][1])
+                dqs[u] = dot_nn(slot_turned(units[u], kt[:, 0:128], turned), ds[u])
+            u = t - 1
+            if 0 <= u < count:
+                for acc, terms_ in ((dk, dks[u]), (dv, dvs[u])):
+                    acc[0:128, :] += terms_[0:128, :]
+                    for n in range(2, 8):
+                        one = terms_[n * 64 : n * 64 + 64, :]
+                        if n < 5:
+                            at = pl.ds(pl.multiple_of(units[u].near[n - 2] * BLOCK, BLOCK), BLOCK)
+                            acc[at, :] += one
+                        else:
+                            for h in range(4):
+                                t_ = h // 2
+                                at = pl.ds(pl.multiple_of(units[u].chosen[n - 5][h] * BLOCK, BLOCK), BLOCK)
+                                cols = pl.ds(t_ * HALF, HALF)
+                                mine = low if h % 2 == 0 else jnp.logical_not(low)
+                                acc[at, cols] += jnp.where(mine, one[:, t_ * HALF : t_ * HALF + HALF], 0.0)
+                dq[spreads[u][0], :] = (pick_turned(dqs[u]) * QUERY_SCALE).astype(LOW)
 
     def several(j, _):
         group([2 + BACK * j + u for u in range(BACK)])
@@ -654,14 +668,15 @@
     return pl.pallas_call(
         functools.partial(reorder_kernel, scatter),
         out_shape=jax.ShapeDtypeStruct(src.shape, src.dtype),
-        in_specs=[smem(), smem()] + [pl.BlockSpec(memory_space=pl.ANY)] * (1 + len(after)),
-        out_specs=pl.BlockSpec(memory_space=pl.ANY),
+        in_specs=[smem(), smem(), pl.BlockSpec(memory_space=pltpu.HBM)]
+        + [pl.BlockSpec(memory_space=pltpu.HBM)] * len(after),
+        out_specs=pl.BlockSpec(memory_space=pltpu.HBM),
         scratch_shapes=[
             pltpu.VMEM(src.shape, src.dtype),
             pltpu.SemaphoreType.DMA((src.shape[0],)),
             pltpu.SemaphoreType.DMA((src.shape[0],)),
         ],
-        compiler_params=pltpu.CompilerParams(vmem_limit_bytes=8 * 1024 * 1024),
+        compiler_params=pltpu.CompilerParams(vmem_limit_bytes=VMEM_LIMIT),
         cost_estimate=pl.CostEstimate(flops=0, bytes_accessed=4 * src.size, transcendentals=0),
         name="reorder",
     )(shard, assign, src, *after)
@@ -669,7 +684,7 @@
 
 def hold(values, after):
     count = len(values)
-    anywhere = pl.BlockSpec(memory_space=pl.ANY)
+    anywhere = pl.BlockSpec(memory_space=pltpu.HBM)
     return pl.pallas_call(
         lambda *refs: None,
         out_shape=tuple(jax.ShapeDtypeStruct(v.shape, v.dtype) for v in values),
@@ -697,9 +712,9 @@
     return pl.pallas_call(
         pack_kernel,
         out_shape=jax.ShapeDtypeStruct((w_qkv.shape[0] + 16, 3072), LOW),
-        in_specs=[vmem()] * 6 + [pl.BlockSpec(memory_space=pl.ANY)],
+        in_specs=[vmem()] * 6 + [pl.BlockSpec(memory_space=pltpu.HBM)],
         out_specs=vmem(),
-        compiler_params=pltpu.CompilerParams(vmem_limit_bytes=8 * 1024 * 1024),
+        compiler_params=pltpu.CompilerParams(vmem_limit_bytes=VMEM_LIMIT),
         name="pack_weights",
     )(w_qkv, w_out, w_up, w_down, up_bias.reshape(1, -1), vectors, after)
 
@@ -741,7 +756,7 @@
         ),
         in_specs=[smem(), vmem(), vmem()],
         out_specs=[vmem()] * 10,
-        compiler_params=pltpu.CompilerParams(vmem_limit_bytes=16 * 1024 * 1024),
+        compiler_params=pltpu.CompilerParams(vmem_limit_bytes=VMEM_LIMIT),
         name="unpack_weights",
     )(shard, own, got)
 
@@ -779,12 +794,17 @@
     got = [lax.ppermute(piece(k + 1).astype(LOW), "dp", hop) for k, hop in enumerate(hops)]
     for one in got:
         mine = mine + one.astype(F32)
-    mine = mine.astype(LOW)
+    return mine.astype(LOW)
+
+
+def spread_sums(mine):
+    count = lax.axis_size("dp")
+    flip = [(d, d ^ 2) for d in range(count)]
+    hops = [[(d, (d + 4 * k) % count) for d in range(count)] for k in range(1, count // 4)]
     near = jnp.stack([mine] + [lax.ppermute(mine, "dp", hop) for hop in hops])
     core = [(d, d ^ 1) for d in range(count)]
     across = lax.ppermute(near, "dp", flip)
-    near_core, across_core = lax.ppermute(near, "dp", core), lax.ppermute(across, "dp", core)
-    return jnp.stack([near, across, near_core, across_core]).astype(F32)
+    return near, across, lax.ppermute(near, "dp", core), lax.ppermute(across, "dp", core)
 
 
 def adam_update(grad, state, decay):
@@ -798,17 +818,18 @@
 
 
 def update_kernel(
-    where, parts, s_qkv, s_out, s_up, s_down, s_bias, s_vec,
+    where, near, across, near_core, across_core, s_qkv, s_out, s_up, s_down, s_bias, s_vec, done_out, done_grad,
     g_qkv, g_out, g_up, g_down, g_bias, g_vec, o_master, o_first, o_second, grads, flat, sems,
 ):
-    groups, small = parts.shape[1:3]
+    groups, small = near.shape[:2]
+    parts = (near, across, near_core, across_core)
     index = where[0]
     for core in range(2):
         for side in range(2):
             base = ((index % 2) ^ core) * 64 + (((index // 2) % 2) ^ side) * 32
             for k in range(groups):
                 at = base + lax.rem(index // 4 + groups - k, groups) * small
-                grads[pl.ds(pl.multiple_of(at, small), small), :] = parts[2 * core + side, k]
+                grads[pl.ds(pl.multiple_of(at, small), small), :] = parts[2 * core + side][k].astype(F32)
     outs = [flat.at[n] for n in range(3)]
 
     def place(base, grad, state, decay):
@@ -849,7 +870,7 @@
         copy.wait()
 
 
-def update(data_index, parts, states):
+def update(data_index, parts, states, after):
     shape = lambda *dims: jax.ShapeDtypeStruct(dims, F32)
     s_qkv, s_out, s_up, s_down, s_bias, s_vec = states
     flat = shape(1, 3084 * HALF)
@@ -859,15 +880,15 @@
             shape(128, 768), shape(128, 256), shape(128, 1024), shape(512, 256), shape(4, HALF), shape(4, 256),
             flat, flat, flat,
         ),
-        in_specs=[smem()] + [vmem()] * 7,
-        out_specs=[vmem()] * 6 + [pl.BlockSpec(memory_space=pl.ANY)] * 3,
+        in_specs=[smem()] + [vmem()] * 10 + [pl.BlockSpec(memory_space=pltpu.HBM)] * 2,
+        out_specs=[vmem()] * 6 + [pl.BlockSpec(memory_space=pltpu.HBM)] * 3,
         scratch_shapes=[
             pltpu.VMEM((128, 3200), F32), pltpu.VMEM((3, 3084, HALF), F32), pltpu.SemaphoreType.DMA((3,)),
         ],
         compiler_params=pltpu.CompilerParams(vmem_limit_bytes=VMEM_LIMIT),
         cost_estimate=pl.CostEstimate(flops=10_000_000, bytes_accessed=14_000_000, transcendentals=400_000),
         name="update",
-    )(data_index.reshape(1), parts, s_qkv, s_out, s_up, s_down, s_bias.reshape(3, 4, HALF), s_vec)
+    )(data_index.reshape(1), *parts, s_qkv, s_out, s_up, s_down, s_bias.reshape(3, 4, HALF), s_vec, *after)
     grads[4] = grads[4].reshape(-1)
     return tuple(grads) + (master, first, second)
 
@@ -913,20 +934,18 @@
     gin, *late = hold((gin, *late), (back_out, *early[1:]))
     back_gin = from_slot(gin)
 
-    def sum_all(early, late, back_out):
+    def sum_all(early, late):
         early, late = total(early), total(trade(late))
         sums = jnp.concatenate([early[:, :2304], late[:, :768], early[:, 2304:] + late[:, 768:]], axis=1)
-        return sum_rest(sums, data_index), reorder(shard, assign, back_out, True)
-
-    made = jax.eval_shape(sum_all, early, late, back_out)
-    parts, layer_out = lax.cond(
-        live_blocks[0] > 0,
-        sum_all,
-        lambda *unused: jax.tree.map(lambda one: jnp.zeros(one.shape, one.dtype), made),
-        early, late, back_out,
-    )
-    updated = update(data_index, parts, (state_qkv, state_out, state_up, state_down, state_ubias, state_vec))
-    input_grad = reorder(shard, assign, back_gin, True)
+        return sum_rest(sums, data_index)
+
+    made = jax.eval_shape(sum_all, early, late)
+    mine = lax.cond(live_blocks[0] > 0, sum_all, lambda *unused: jnp.zeros(made.shape, made.dtype), early, late)
+    parts = spread_sums(mine)
+    layer_out = reorder(shard, assign, back_out, True, (mine,))
+    input_grad = reorder(shard, assign, back_gin, True, (parts[0],))
+    states = (state_qkv, state_out, state_up, state_down, state_ubias, state_vec)
+    updated = update(data_index, parts, states, (layer_out, input_grad))
     return (layer_out, input_grad) + updated
 
 

time: 297 us -> 283 us (0.953)
  Pallas kernels: 155 us -> 142 us
  local copies, waits for them, and re-layouts: 14.3 us -> 8.51 us
  waiting for transfers between devices: 73.7 us -> 77.1 us
    unnamed x55 -> x29, local copies, waits for them, and re-layouts: 12.1 us -> 4.46 us
    pallas_call x1, Pallas kernels: 55.3 us -> 48.9 us  [backward_attention(): pl.pallas_call(backward_kernel, out_shape=(shape((length, 256), LOW),) +...]
    pallas_call x4, Pallas kernels: 18 us -> 13 us  [reorder(): pl.pallas_call(functools.partial(reorder_kernel, scatter), out_shape=jax....]
    all_to_all x2, waiting for transfers between devices: 4.57 us -> 8.4 us  [to_slot(): lax.all_to_all(rows, 'dp', split_axis=0, concat_axis=0, tiled=True)]
  transfers between devices with their start and end apart: 21 -> 21, of which waited for: 11 -> 11; matrix products, arithmetic and copies ran while one was open for 3% -> 3% of each run, Pallas kernels for 49% -> 46%
where the time goes in v4:
time: 283 us; the launch traced here: 282 us
  Pallas kernels  142 us (50%)
  waiting for transfers between devices  77.1 us (27%)
  starting transfers between devices  45.5 us (16%)
  local copies, waits for them, and re-layouts  8.51 us (3%)
  other arithmetic  5.31 us (2%)
    pallas_call x1, Pallas kernels, backward_attention(): pl.pallas_call(backward_kernel, out_shape=(shape((length, 256), LOW),) +...  48.9 us
    pallas_call x1, Pallas kernels, forward_attention(): pl.pallas_call(forward_kernel, out_shape=(rows, rows, rows, jax.ShapeDtyp...  27.9 us
    ppermute x3, waiting for transfers between devices, sum_rest(): lax.ppermute(piece(k + 1).astype(LOW), 'dp', hop)  27.4 us
    pallas_call x1, Pallas kernels, behind(): pl.pallas_call(behind_kernel, grid_spec=pltpu.PrefetchScalarGridSpec(num_...  21.7 us
    all_to_all x2, starting transfers between devices, to_slot(): lax.all_to_all(rows, 'dp', split_axis=0, concat_axis=0, tiled=True)  18.7 us
    pallas_call x1, Pallas kernels, ahead(): pl.pallas_call(ahead_kernel, grid_spec=pltpu.PrefetchScalarGridSpec(num_s...  17.5 us
    ppermute x1, waiting for transfers between devices, on_device(): got = lax.ppermute(pack, 'shard', [(0, 1), (1, 0)])  15.9 us
    pallas_call x4, Pallas kernels, reorder(): pl.pallas_call(functools.partial(reorder_kernel, scatter), out_shape=jax....  13 us
  transfers between devices with their start and end apart: 21, of which 11 were waited for; matrix products, arithmetic and copies ran while one was open for 3% of the time, Pallas kernels for 46%

profile of v4, /device:TPU:0, one launch (start us, length us, event | category | flops | bytes accessed | tf_op | source)
XLA Modules:
  0.0 281.7 jit_solution(10012709710182552391)
XLA Ops:
  0.6 3.2 %reorder.4.after = bf16[16,256,256]{2,1,0:T(8,128)(2,1)} custom-call(s32[1]{0:T(128)} %bitcast.where.shard, s32[32]{0:T(128)} %assign.7, bf16[16,256,256]{2,1,0:T(8,128)(2,1)} %src.2), custom_call_target="tpu_custom_call" | custom-call | bytes 4194304 | tf_op jit(solution)/shard_map/reorder/pallas_call | solution.py:668
  3.9 7.4 %all-to-all-start = ((bf16[16,256,256]{2,1,0:T(8,128)(2,1)}), bf16[16,256,256]{2,1,0:T(8,128)(2,1)S(1)}, u32[]{:S(2)}, u32[]{:S(2)}) async-start(bf16[16,256,256]{2,1,0:T(8,128)(2,1)} %reorder.4.after), calls=%async_computation | async-start | bytes 4194304 | tf_op jit(solution)/shard_map/all_to_all | solution.py:908
  11.9 2.2 pack_weights.1.own
  14.1 1.5 collective-permute-start.7
  20.4 15.9 %collective-permute-done.7.got = bf16[144,3072]{1,0:T(8,128)(2,1)S(1)} collective-permute-done((bf16[144,3072]{1,0:T(8,128)(2,1)}, bf16[144,3072]{1,0:T(8,128)(2,1)S(1)}, u32[]{:S(2)}, u32[]{:S(2)}) %collective-permute-start.7) | collective-permute-done | bytes 884768 | tf_op jit(solution)/shard_map/ppermute | solution.py:913
  37.2 2.8 %unpack_weights.1 = (bf16[256,768]{1,0:T(8,128)(2,1)}, bf16[256,256]{1,0:T(8,128)(2,1)}, bf16[256,1024]{1,0:T(8,128)(2,1)}, bf16[1024,256]{1,0:T(8,128)(2,1)}, b...) custom-call(s32[1]{0:T(128)} %bitcast.where.shard, ...), custom_call_target="tpu_custom_call" | custom-call | tf_op jit(solution)/shard_map/unpack_weights/pallas_call | solution.py:750
  40.8 3.3 %reorder.5 = bf16[16,256,256]{2,1,0:T(8,128)(2,1)} custom-call(s32[1]{0:T(128)} %bitcast.where.shard, s32[32]{0:T(128)} %assign.7, bf16[16,256,256]{2,1,0:T(8,128)(2,1)} %src.3, bf16[256,768]{1,0:T(8,128)(2,1)} %get-tuple-element.88.w.rest_0_, s32[2]{0:T(128)} %pad_add_fusion.scal.rest_1_, f32[3,64,128]{2,1,0:T(8,128)} %broadcast_in_dim.13.table.rest_2_, ...), custom_call_target="tpu_custom_call" | custom-call | bytes 4194304 | tf_op jit(solution)/shard_map/reorder/pallas_call | solution.py:668
  44.0 8.4 %all-to-all-done = bf16[16,256,256]{2,1,0:T(8,128)(2,1)S(1)} async-done(((bf16[16,256,256]{2,1,0:T(8,128)(2,1)}), bf16[16,256,256]{2,1,0:T(8,128)(2,1)S(1)}, u32[]{:S(2)}, u32[]{:S(2)}) %all-to-all-start) | async-done | bytes 2097184 | tf_op jit(solution)/shard_map/all_to_all | solution.py:908
  52.4 11.3 %all-to-all-start.2 = ((bf16[16,256,256]{2,1,0:T(8,128)(2,1)}), bf16[16,256,256]{2,1,0:T(8,128)(2,1)}, u32[]{:S(2)}, u32[]{:S(2)}) async-start(bf16[16,256,256]{2,1,0:T(8,128)(2,1)} %reorder.5), calls=%async_computation.2 | async-start | bytes 4194304 | tf_op jit(solution)/shard_map/all_to_all | solution.py:908
  63.7 27.9 %attend_forward.1 = (bf16[4096,256]{1,0:T(8,128)(2,1)}, bf16[4096,256]{1,0:T(8,128)(2,1)}, bf16[4096,256]{1,0:T(8,128)(2,1)}, bf16[256,4096]{1,0:T(8,128)(2,1)},...) custom-call(s32[2]{0:T(128)} %pad_add_fusion.scal.rest_1_, s32[768]{0:T(1024)} %reshape.59.drawn.rest_3_, ...), custom_call_target="tpu_custom_call" | custom-call | flops 16000000000 | bytes 12000000 | tf_op jit(solution)/shard_map/attend_forward/pallas_call | solution.py:265
  91.6 17.5 %ahead.1 = (bf16[4096,256]{1,0:T(8,128)(2,1)}, bf16[4096,256]{1,0:T(8,128)(2,1)}, bf16[4096,256]{1,0:T(8,128)(2,1)}, bf16[4096,1024]{1,0:T(8,128)(2,1)}, bf16[4096,1024]{1,0:T(8,128)(2,1)}) custom-call(s32[2]{0:T(128)} %pad_add_fusion.scal.rest_1_, f32[3,64,128]{2,1,0:T(8,128)} %broadcast_in_dim.13.table.rest_2_, bf16[4096,256]{1,0:T(8,128)(2,1)} %bitcast.18, ...), custom_call_target="tpu_custom_call" | custom-call | flops 5000000000 | bytes 34000000 | tf_op jit(solution)/shard_map/ahead/pallas_call | solution.py:358
  109.2 6.9 %all-to-all-start.1 = ((bf16[16,256,256]{2,1,0:T(8,128)(2,1)}), bf16[16,256,256]{2,1,0:T(8,128)(2,1)S(1)}, u32[]{:S(2)}, u32[]{:S(2)}) async-start(bf16[16,256,256]{2,1,0:T(8,128)(2,1)} %bitcast.20), calls=%async_computation.1 | async-start | bytes 4194304 | tf_op jit(solution)/shard_map/all_to_all | solution.py:926
  116.1 21.7 %behind.1 = (f32[4096,256]{1,0:T(8,128)}, bf16[4096,256]{1,0:T(8,128)(2,1)}, f32[64,256]{1,0:T(8,128)}, bf16[64,2432]{1,0:T(8,128)(2,1)}, bf16[64,2432]{1,0:T(8,...) custom-call(s32[2]{0:T(128)} %pad_add_fusion.scal.rest_1_, f32[3,64,128]{2,1,0:T(8,128)} %broadcast_in_dim.13.table.rest_2_, ...), custom_call_target="tpu_custom_call" | custom-call | flops 10000000000 | bytes 40000000 | tf_op jit(solution)/shard_map/behind/pallas_call | solution.py:471
  138.3 1.5 collective-permute-start.9
  139.8 48.9 %attend_backward.1 = (bf16[4096,256]{1,0:T(8,128)(2,1)}, bf16[64,896]{1,0:T(8,128)(2,1)S(1)}, bf16[64,896]{1,0:T(8,128)(2,1)}, bf16[64,896]{1,0:T(8,128)(2,1)}, bf16[64,896]{1,0:T(8,128)(2,1)}) custom-call(s32[2]{0:T(128)} %pad_add_fusion.scal.rest_1_, s32[768]{0:T(1024)} %reshape.59.drawn.rest_3_, f32[3,64,128]{2,1,0:T(8,128)} %broadcast_in_dim.13.table.rest_2_, ...), custom_call_target="tpu_custom_call" | custom-call | flops 40000000000 | bytes 20000000 | tf_op jit(solution)/shard_map/attend_backward/pallas_call | solution.py:621
  190.0 6.0 %all-to-all-start.3 = ((bf16[16,256,256]{2,1,0:T(8,128)(2,1)}), bf16[16,256,256]{2,1,0:T(8,128)(2,1)S(1)}, u32[]{:S(2)}, u32[]{:S(2)}) async-start(bf16[16,256,256]{2,1,0:T(8,128)(2,1)} %bitcast.16), calls=%async_computation.3 | async-start | bytes 4194304 | tf_op jit(solution)/shard_map/all_to_all | solution.py:926
  196.7 53.0 %conditional.1 = (bf16[8,3200]{1,0:T(8,128)(2,1)S(1)}) conditional(s32[]{:T(128)} %bitcast.5, () %tuple.14, (bf16[64,2432]{1,0:T(8,128)(2,1)}, bf16[64,2432]{1,0:T(8,128)(2,1)S(1)}, bf16[64,2432]{1,0:T(8,128)(2,1)S(1)}, bf16[64,2432]{1,0:T(8,128)(2,1)S(1)}, bf16[64,896]{1,0:T(8,128)(2,1)S(1)}, /*index=5*/bf16[64,896]{1,0:T(8,128)(2,1)}, ...), branch_computations={%region_0.1_spmd, %region_1.2_spmd} | conditional | flops 2292824 | bytes 12428570 | solution.py:943
  196.8 1.6 collective-permute-start.2
  200.2 1.9 collective-permute-done.2
  202.2 2.9 %collective-permute-done.1 = bf16[64,896]{1,0:T(8,128)(2,1)} collective-permute-done((bf16[64,896]{1,0:T(8,128)(2,1)}, bf16[64,896]{1,0:T(8,128)(2,1)}, u32[]{:S(2)}, u32[]{:S(2)}) %collective-permute-start.1) | collective-permute-done | bytes 114720 | tf_op jit(solution)/shard_map/cond/branch_1_fun/ppermute | solution.py:769
  206.3 2.0 collective-permute-start.3
  208.3 11.6 %collective-permute-done.3 = bf16[32,3200]{1,0:T(8,128)(2,1)S(1)} collective-permute-done((bf16[32,3200]{1,0:T(8,128)(2,1)S(1)}, bf16[32,3200]{1,0:T(8,128)(2,1)S(1)}, u32[]{:S(2)}, u32[]{:S(2)}) %collective-permute-start.3) | collective-permute-done | bytes 204832 | tf_op jit(solution)/shard_map/cond/branch_1_fun/ppermute | solution.py:785
  222.1 10.1 %collective-permute-done.6 = bf16[8,3200]{1,0:T(8,128)(2,1)S(1)} collective-permute-done((bf16[8,3200]{1,0:T(8,128)(2,1)S(1)}, bf16[8,3200]{1,0:T(8,128)(2,1)S(1)}, u32[]{:S(2)}, u32[]{:S(2)}) %collective-permute-start.6) | collective-permute-done | bytes 51232 | tf_op jit(solution)/shard_map/cond/branch_1_fun/ppermute | solution.py:794
  232.2 17.3 %collective-permute-done.5 = bf16[8,3200]{1,0:T(8,128)(2,1)S(1)} collective-permute-done((bf16[8,3200]{1,0:T(8,128)(2,1)S(1)}, bf16[8,3200]{1,0:T(8,128)(2,1)S(1)}, u32[]{:S(2)}, u32[]{:S(2)}) %collective-permute-start.5) | collective-permute-done | bytes 51232 | tf_op jit(solution)/shard_map/cond/branch_1_fun/ppermute | solution.py:794
  252.4 1.9 collective-permute-done.13
  254.3 1.5 collective-permute-done.12
  255.8 1.3 collective-permute-done.11
  258.0 1.6 collective-permute-start.14
  259.6 4.2 %collective-permute-done.14.across = bf16[4,8,3200]{2,1,0:T(8,128)(2,1)S(1)} collective-permute-done((bf16[4,8,3200]{2,1,0:T(8,128)(2,1)S(1)}, bf16[4,8,3200]{2,1,0:T(8,128)(2,1)S(1)}, u32[]{:S(2)}, u32[]{:S(2)}) %collective-permute-start.14) | collective-permute-done | bytes 204832 | tf_op jit(solution)/shard_map/ppermute | solution.py:806
  264.5 3.2 %reorder.6.done_out = bf16[16,256,256]{2,1,0:T(8,128)(2,1)} custom-call(s32[1]{0:T(128)} %bitcast.where.shard, s32[32]{0:T(128)} %assign.7, bf16[16,256,256]{2,1,0:T(8,128)(2,1)} %copy-done, bf16[8,3200]{1,0:T(8,128)(2,1)} %copy-done.6), custom_call_target="tpu_custom_call" | custom-call | bytes 4194304 | tf_op jit(solution)/shard_map/reorder/pallas_call | solution.py:668
  269.1 3.2 %reorder.7.done_grad = bf16[16,256,256]{2,1,0:T(8,128)(2,1)} custom-call(s32[1]{0:T(128)} %bitcast.where.shard, s32[32]{0:T(128)} %assign.7, bf16[16,256,256]{2,1,0:T(8,128)(2,1)} %copy-done.1, bf16[4,8,3200]{2,1,0:T(8,128)(2,1)} %copy-done.3), custom_call_target="tpu_custom_call" | custom-call | bytes 4194304 | tf_op jit(solution)/shard_map/reorder/pallas_call | solution.py:668
  273.1 8.4 %update.1 = (f32[128,768]{1,0:T(8,128)}, f32[128,256]{1,0:T(8,128)}, f32[128,1024]{1,0:T(8,128)}, f32[512,256]{1,0:T(8,128)}, f32[4,128]{1,0:T(4,128)}, /*index=...) custom-call(s32[1]{0:T(128)} %bitcast.12.where, bf16[4,8,3200]{2,1,0:T(8,128)(2,1)} %copy-done.3, ...), custom_call_target="tpu_custom_call" | custom-call | flops 10000000 | bytes 14000000 | tf_op jit(solution)/shard_map/update/pallas_call | solution.py:877
  (78 shorter events, 19.6 us)
Async XLA Ops:
  3.9 7.4 %copy-start.15 = (bf16[512]{0:T(512)(128)(2,1)S(1)}, bf16[512]{0:T(512)(128)(2,1)}, u32[]{:S(2)}) copy-start(bf16[512]{0:T(512)(128)(2,1)} %param.30) | copy-start | bytes 3076
  3.9 48.5 %all-to-all-start = ((bf16[16,256,256]{2,1,0:T(8,128)(2,1)}), bf16[16,256,256]{2,1,0:T(8,128)(2,1)S(1)}, u32[]{:S(2)}, u32[]{:S(2)}) async-start(bf16[16,256,256]{2,1,0:T(8,128)(2,1)} %reorder.4.after), calls=%async_computation | async-start | bytes 4194304 | tf_op jit(solution)/shard_map/all_to_all | solution.py:908
  11.3 4.3 %copy-start.11 = (s32[32]{0:T(128)S(1)}, s32[32]{0:T(128)}, u32[]{:S(2)}) copy-start(s32[32]{0:T(128)} %assign.7) | copy-start | bytes 388
  11.3 5.5 %copy-start.13 = (s32[1,4,64,3]{2,1,3,0:T(4,128)S(1)}, s32[1,4,64,3]{2,1,3,0:T(4,128)}, u32[]{:S(2)}) copy-start(s32[1,4,64,3]{2,1,3,0:T(4,128)} %param.25) | copy-start | bytes 9220
  11.3 7.1 %copy-start.14 = (s32[32]{0:T(128)S(1)}, s32[32]{0:T(128)}, u32[]{:S(2)}) copy-start(s32[32]{0:T(128)} %param.23) | copy-start | bytes 388
  14.1 22.2 %collective-permute-start.7 = (bf16[144,3072]{1,0:T(8,128)(2,1)}, bf16[144,3072]{1,0:T(8,128)(2,1)S(1)}, u32[]{:S(2)}, u32[]{:S(2)}) collective-permute-start(bf16[144,3072]{1,0:T(8,128)(2,1)} %pack_weights.1.own), channel_id=1, source_target_pairs={{0,1},{1,0},{2,3},{3,2},{4,5},{5,4},{6,7},{7,6},{8,9},{9,8},{10,11... | collective-permute-start | bytes 2654216 | tf_op jit(solution)/shard_map/ppermute | solution.py:913
  52.4 11.3 %copy-start.2 = (bf16[16,256,256]{2,1,0:T(8,128)(2,1)}, bf16[16,256,256]{2,1,0:T(8,128)(2,1)S(1)}, u32[]{:S(2)}) copy-start(bf16[16,256,256]{2,1,0:T(8,128)(2,1)S(1)} %all-to-all-done) | copy-start | bytes 6291460
  52.4 56.8 %all-to-all-start.2 = ((bf16[16,256,256]{2,1,0:T(8,128)(2,1)}), bf16[16,256,256]{2,1,0:T(8,128)(2,1)}, u32[]{:S(2)}, u32[]{:S(2)}) async-start(bf16[16,256,256]{2,1,0:T(8,128)(2,1)} %reorder.5), calls=%async_computation.2 | async-start | bytes 4194304 | tf_op jit(solution)/shard_map/all_to_all | solution.py:908
  109.2 79.5 %all-to-all-start.1 = ((bf16[16,256,256]{2,1,0:T(8,128)(2,1)}), bf16[16,256,256]{2,1,0:T(8,128)(2,1)S(1)}, u32[]{:S(2)}, u32[]{:S(2)}) async-start(bf16[16,256,256]{2,1,0:T(8,128)(2,1)} %bitcast.20), calls=%async_computation.1 | async-start | bytes 4194304 | tf_op jit(solution)/shard_map/all_to_all | solution.py:926
  137.8 50.8 %collective-permute-start.8 = (bf16[64,2432]{1,0:T(8,128)(2,1)}, bf16[64,2432]{1,0:T(8,128)(2,1)S(1)}, u32[]{:S(2)}, u32[]{:S(2)}) collective-permute-start(bf16[64,2432]{1,0:T(8,128)(2,1)} %get-tuple-element.105), channel_id=1, source_target_pairs={{0,2},{1,3},{2,0},{3,1},{4,6},{5,7},{6,4},{7,5},{8,10},{9,11},{10,... | collective-permute-start | bytes 933896 | tf_op jit(solution)/shard_map/ppermute | solution.py:769
  138.3 50.4 %collective-permute-start.9 = (bf16[64,2432]{1,0:T(8,128)(2,1)}, bf16[64,2432]{1,0:T(8,128)(2,1)S(1)}, u32[]{:S(2)}, u32[]{:S(2)}) collective-permute-start(bf16[64,2432]{1,0:T(8,128)(2,1)} %get-tuple-element.106), channel_id=1, source_target_pairs={{0,1},{1,0},{2,3},{3,2},{4,5},{5,4},{6,7},{7,6},{8,9},{9,8},{10,11... | collective-permute-start | bytes 933896 | tf_op jit(solution)/shard_map/ppermute | solution.py:769
  139.8 48.9 %collective-permute-start.10 = (bf16[64,2432]{1,0:T(8,128)(2,1)}, bf16[64,2432]{1,0:T(8,128)(2,1)S(1)}, u32[]{:S(2)}, u32[]{:S(2)}) collective-permute-start(bf16[64,2432]{1,0:T(8,128)(2,1)} %get-tuple-element.107), channel_id=1, source_target_pairs={{0,3},{1,2},{2,1},{3,0},{4,7},{5,6},{6,5},{7,4},{8,11},{9,10},{10,... | collective-permute-start | bytes 933896 | tf_op jit(solution)/shard_map/ppermute | solution.py:769
  190.0 77.7 %all-to-all-start.3 = ((bf16[16,256,256]{2,1,0:T(8,128)(2,1)}), bf16[16,256,256]{2,1,0:T(8,128)(2,1)S(1)}, u32[]{:S(2)}, u32[]{:S(2)}) async-start(bf16[16,256,256]{2,1,0:T(8,128)(2,1)} %bitcast.16), calls=%async_computation.3 | async-start | bytes 4194304 | tf_op jit(solution)/shard_map/all_to_all | solution.py:926
  196.7 67.1 %copy-start.12 = (f32[3,512]{1,0:T(4,128)S(1)}, f32[3,512]{1,0:T(4,128)}, u32[]{:S(2)}) copy-start(f32[3,512]{1,0:T(4,128)} %param.36) | copy-start | bytes 18436
  196.8 2.2 copy-start.4
  196.8 2.1 copy-start.7
  196.8 5.4 %collective-permute-start.2 = (bf16[64,896]{1,0:T(8,128)(2,1)}, bf16[64,896]{1,0:T(8,128)(2,1)}, u32[]{:S(2)}, u32[]{:S(2)}) collective-permute-start(bf16[64,896]{1,0:T(8,128)(2,1)} %get-tuple-element.28), channel_id=1, source_target_pairs={{0,3},{1,2},{2,1},{3,0},{4,7},{5,6},{6,5},{7,4},{8,11},{9,10},{10,... | collective-permute-start | bytes 344072 | tf_op jit(solution)/shard_map/cond/branch_1_fun/ppermute | solution.py:769
  198.4 6.7 %collective-permute-start.1 = (bf16[64,896]{1,0:T(8,128)(2,1)}, bf16[64,896]{1,0:T(8,128)(2,1)}, u32[]{:S(2)}, u32[]{:S(2)}) collective-permute-start(bf16[64,896]{1,0:T(8,128)(2,1)} %get-tuple-element.27), channel_id=1, source_target_pairs={{0,1},{1,0},{2,3},{3,2},{4,5},{5,4},{6,7},{7,6},{8,9},{9,8},{10,11... | collective-permute-start | bytes 344072 | tf_op jit(solution)/shard_map/cond/branch_1_fun/ppermute | solution.py:769
  198.9 6.2 %collective-permute-start = (bf16[64,896]{1,0:T(8,128)(2,1)}, bf16[64,896]{1,0:T(8,128)(2,1)}, u32[]{:S(2)}, u32[]{:S(2)}) collective-permute-start(bf16[64,896]{1,0:T(8,128)(2,1)} %get-tuple-element.26), channel_id=1, source_target_pairs={{0,2},{1,3},{2,0},{3,1},{4,6},{5,7},{6,4},{7,5},{8,10},{9,11},{10,... | collective-permute-start | bytes 344072 | tf_op jit(solution)/shard_map/cond/branch_1_fun/ppermute | solution.py:769
  206.3 13.6 %collective-permute-start.3 = (bf16[32,3200]{1,0:T(8,128)(2,1)S(1)}, bf16[32,3200]{1,0:T(8,128)(2,1)S(1)}, u32[]{:S(2)}, u32[]{:S(2)}) collective-permute-start(bf16[32,3200]{1,0:T(8,128)(2,1)S(1)} %dynamic-slice_convert_fusion), channel_id=1, source_target_pairs={{0,4},{2,6},{4,0},{6,2},{8,12},{10,14},{12,8},{14,10},{16,20},{18,... | collective-permute-start | bytes 614408 | tf_op jit(solution)/shard_map/cond/branch_1_fun/ppermute | solution.py:785
  220.0 12.2 %collective-permute-start.6 = (bf16[8,3200]{1,0:T(8,128)(2,1)S(1)}, bf16[8,3200]{1,0:T(8,128)(2,1)S(1)}, u32[]{:S(2)}, u32[]{:S(2)}) collective-permute-start(bf16[8,3200]{1,0:T(8,128)(2,1)S(1)} %get-tuple-element.136), channel_id=1, source_target_pairs={{0,24},{2,26},{4,28},{6,30},{8,0},{10,2},{12,4},{14,6},{16,8},{18,... | collective-permute-start | bytes 153608 | tf_op jit(solution)/shard_map/cond/branch_1_fun/ppermute | solution.py:794
  221.3 28.2 %collective-permute-start.5 = (bf16[8,3200]{1,0:T(8,128)(2,1)S(1)}, bf16[8,3200]{1,0:T(8,128)(2,1)S(1)}, u32[]{:S(2)}, u32[]{:S(2)}) collective-permute-start(bf16[8,3200]{1,0:T(8,128)(2,1)S(1)} %get-tuple-element.137), channel_id=1, source_target_pairs={{0,16},{2,18},{4,20},{6,22},{8,24},{10,26},{12,28},{14,30},{16,0},... | collective-permute-start | bytes 153608 | tf_op jit(solution)/shard_map/cond/branch_1_fun/ppermute | solution.py:794
  221.3 28.2 %collective-permute-start.4 = (bf16[8,3200]{1,0:T(8,128)(2,1)S(1)}, bf16[8,3200]{1,0:T(8,128)(2,1)S(1)}, u32[]{:S(2)}, u32[]{:S(2)}) collective-permute-start(bf16[8,3200]{1,0:T(8,128)(2,1)S(1)} %get-tuple-element.135), channel_id=1, source_target_pairs={{0,8},{2,10},{4,12},{6,14},{8,16},{10,18},{12,20},{14,22},{16,24},... | collective-permute-start | bytes 153608 | tf_op jit(solution)/shard_map/cond/branch_1_fun/ppermute | solution.py:794
  249.7 7.4 %copy-start.6 = (bf16[8,3200]{1,0:T(8,128)(2,1)}, bf16[8,3200]{1,0:T(8,128)(2,1)S(1)}, u32[]{:S(2)}) copy-start(bf16[8,3200]{1,0:T(8,128)(2,1)S(1)} %get-tuple-element.140.rest_0_) | copy-start | bytes 153604
  249.8 4.6 %collective-permute-start.13 = (bf16[8,3200]{1,0:T(8,128)(2,1)S(1)}, bf16[8,3200]{1,0:T(8,128)(2,1)S(1)}, u32[]{:S(2)}, u32[]{:S(2)}) collective-permute-start(bf16[8,3200]{1,0:T(8,128)(2,1)S(1)} %get-tuple-element.140.rest_0_), channel_id=1, source_target_pairs={{0,24},{2,26},{4,28},{6,30},{8,0},{10,2},{12,4},{14,6},{16,8},{18,... | collective-permute-start | bytes 153608 | tf_op jit(solution)/shard_map/ppermute | solution.py:804
  250.7 5.1 %collective-permute-start.12 = (bf16[8,3200]{1,0:T(8,128)(2,1)S(1)}, bf16[8,3200]{1,0:T(8,128)(2,1)S(1)}, u32[]{:S(2)}, u32[]{:S(2)}) collective-permute-start(bf16[8,3200]{1,0:T(8,128)(2,1)S(1)} %get-tuple-element.140.rest_0_), channel_id=1, source_target_pairs={{0,16},{2,18},{4,20},{6,22},{8,24},{10,26},{12,28},{14,30},{16,0},... | collective-permute-start | bytes 153608 | tf_op jit(solution)/shard_map/ppermute | solution.py:804
  251.2 5.9 %collective-permute-start.11 = (bf16[8,3200]{1,0:T(8,128)(2,1)S(1)}, bf16[8,3200]{1,0:T(8,128)(2,1)S(1)}, u32[]{:S(2)}, u32[]{:S(2)}) collective-permute-start(bf16[8,3200]{1,0:T(8,128)(2,1)S(1)} %get-tuple-element.140.rest_0_), channel_id=1, source_target_pairs={{0,8},{2,10},{4,12},{6,14},{8,16},{10,18},{12,20},{14,22},{16,24},... | collective-permute-start | bytes 153608 | tf_op jit(solution)/shard_map/ppermute | solution.py:804
  258.0 9.7 %copy-start.3 = (bf16[4,8,3200]{2,1,0:T(8,128)(2,1)}, bf16[4,8,3200]{2,1,0:T(8,128)(2,1)S(1)}, u32[]{:S(2)}) copy-start(bf16[4,8,3200]{2,1,0:T(8,128)(2,1)S(1)} %pad_maximum_fusion.1.rest_0_.near) | copy-start | bytes 614404
  258.0 5.8 %collective-permute-start.14 = (bf16[4,8,3200]{2,1,0:T(8,128)(2,1)S(1)}, bf16[4,8,3200]{2,1,0:T(8,128)(2,1)S(1)}, u32[]{:S(2)}, u32[]{:S(2)}) collective-permute-start(bf16[4,8,3200]{2,1,0:T(8,128)(2,1)S(1)} %pad_maximum_fusion.1.rest_0_.near), channel_id=1, source_target_pairs={{0,4},{2,6},{4,0},{6,2},{8,12},{10,14},{12,8},{14,10},{16,20},{18,... | collective-permute-start | bytes 614408 | tf_op jit(solution)/shard_map/ppermute | solution.py:806
  259.6 12.7 %collective-permute-start.15 = (bf16[4,8,3200]{2,1,0:T(8,128)(2,1)S(1)}, bf16[4,8,3200]{2,1,0:T(8,128)(2,1)S(1)}, u32[]{:S(2)}, u32[]{:S(2)}) collective-permute-start(bf16[4,8,3200]{2,1,0:T(8,128)(2,1)S(1)} %pad_maximum_fusion.1.rest_0_.near), channel_id=1, source_target_pairs={{0,2},{2,0},{4,6},{6,4},{8,10},{10,8},{12,14},{14,12},{16,18},{18,... | collective-permute-start | bytes 614408 | tf_op jit(solution)/shard_map/ppermute | solution.py:807
  263.8 3.9 %copy-start.8 = (bf16[4,8,3200]{2,1,0:T(8,128)(2,1)}, bf16[4,8,3200]{2,1,0:T(8,128)(2,1)S(1)}, u32[]{:S(2)}) copy-start(bf16[4,8,3200]{2,1,0:T(8,128)(2,1)S(1)} %collective-permute-done.14.across) | copy-start | bytes 614404
  263.8 8.5 %collective-permute-start.16 = (bf16[4,8,3200]{2,1,0:T(8,128)(2,1)S(1)}, bf16[4,8,3200]{2,1,0:T(8,128)(2,1)S(1)}, u32[]{:S(2)}, u32[]{:S(2)}) collective-permute-start(bf16[4,8,3200]{2,1,0:T(8,128)(2,1)S(1)} %collective-permute-done.14.across), channel_id=1, source_target_pairs={{0,2},{2,0},{4,6},{6,4},{8,10},{10,8},{12,14},{14,12},{16,18},{18,... | collective-permute-start | bytes 614408 | tf_op jit(solution)/shard_map/ppermute | solution.py:807
  (5 other events, 5.0 us)

commit v5 on v4

--- a/solution.py
+++ b/solution.py
@@ -132,6 +132,10 @@
         return jnp.concatenate(rows, axis=0)
 
 
+def masked(scores, bias):
+    return jnp.concatenate([scores[0:HALF], scores[HALF:] + bias], axis=0)
+
+
 def chunk_bias(table, live, first, count):
     last = live - 1
     rows = []
@@ -201,7 +205,7 @@
         rows = [pl.ds(pl.multiple_of(i * BLOCK, BLOCK), BLOCK) for i in idx]
         bd = [spread_heads(q_v[r, :] * jnp.asarray(QUERY_SCALE, LOW), picks[...]) for r in rows]
         every = range(GROUP)
-        s = [dot_nt(slot_rows(units[u], k_v), bd[u]) + units[u].bias(table, range(8)) for u in every]
+        s = [masked(dot_nt(slot_rows(units[u], k_v), bd[u]), units[u].bias(table, range(2, 8))) for u in every]
         m = [jnp.max(s[u], axis=0, keepdims=True) for u in every]
         e = [jnp.exp(s[u] - m[u]) for u in every]
         total = [jnp.sum(e[u], axis=0, keepdims=True) for u in every]
@@ -531,7 +535,7 @@
                 g[u] = dot_nt(slot_rows(units[u], v), spreads[u][2])
             u = t - 0
             if 0 <= u < count:
-                e = jnp.exp(s[u] + units[u].bias(table, range(8)) - lse[pl.ds(idx[u], 1), :])
+                e = jnp.exp(masked(s[u], units[u].bias(table, range(2, 8))) - lse[pl.ds(idx[u], 1), :])
                 ds[u] = (e * (g[u] - delta[pl.ds(idx[u], 1), :])).astype(LOW)
                 p[u] = e.astype(LOW)
             u = t - 0
@@ -600,7 +604,7 @@
         gw_o[...] += dot_tn(x_v[rows, :], dqkv)
         return shifts + jnp.sum(dqkv.astype(F32), axis=0, keepdims=True)
 
-    shifts = lax.fori_loop(0, length // 512, finish, jnp.zeros((1, 768), F32))
+    shifts = lax.fori_loop(0, length // 512, finish, jnp.zeros((1, 768), F32), unroll=2)
     store = pltpu.make_async_copy(gin_v, gin_o, sems.at[2])
     store.start()
     for r, pack in enumerate((pack0, pack1, pack2, pack3)):
@@ -774,7 +778,7 @@
     return sum(piece.astype(F32) for piece in pieces)
 
 
-def sum_rest(part, data_index):
+def sum_rest(part, data_index, meanwhile):
     count = lax.axis_size("dp")
     groups = count // 4
     half = part.shape[0] // 2
@@ -790,21 +794,23 @@
     def piece(k):
         return lax.dynamic_slice_in_dim(part, lax.rem(at + k, groups) * small, small, 0)
 
-    mine = piece(0)
+    other = meanwhile(part)
+    mine = hold((piece(0),), (other,))[0]
     got = [lax.ppermute(piece(k + 1).astype(LOW), "dp", hop) for k, hop in enumerate(hops)]
     for one in got:
         mine = mine + one.astype(F32)
-    return mine.astype(LOW)
-
-
-def spread_sums(mine):
+    return mine.astype(LOW), other
+
+
+def spread_sums(mine, meanwhile):
     count = lax.axis_size("dp")
     flip = [(d, d ^ 2) for d in range(count)]
     hops = [[(d, (d + 4 * k) % count) for d in range(count)] for k in range(1, count // 4)]
     near = jnp.stack([mine] + [lax.ppermute(mine, "dp", hop) for hop in hops])
     core = [(d, d ^ 1) for d in range(count)]
-    across = lax.ppermute(near, "dp", flip)
-    return near, across, lax.ppermute(near, "dp", core), lax.ppermute(across, "dp", core)
+    other = meanwhile(near)
+    across = hold((lax.ppermute(near, "dp", flip),), (other,))[0]
+    return (near, across, lax.ppermute(near, "dp", core), lax.ppermute(across, "dp", core)), other
 
 
 def adam_update(grad, state, decay):
@@ -818,7 +824,7 @@
 
 
 def update_kernel(
-    where, near, across, near_core, across_core, s_qkv, s_out, s_up, s_down, s_bias, s_vec, done_out, done_grad,
+    where, near, across, near_core, across_core, s_qkv, s_out, s_up, s_down, s_bias, s_vec,
     g_qkv, g_out, g_up, g_down, g_bias, g_vec, o_master, o_first, o_second, grads, flat, sems,
 ):
     groups, small = near.shape[:2]
@@ -830,65 +836,77 @@
             for k in range(groups):
                 at = base + lax.rem(index // 4 + groups - k, groups) * small
                 grads[pl.ds(pl.multiple_of(at, small), small), :] = parts[2 * core + side][k].astype(F32)
-    outs = [flat.at[n] for n in range(3)]
+    copies = []
+
+    def send(here, there):
+        copies.append(pltpu.make_async_copy(here, there, sems.at[len(copies)]))
+        copies[-1].start()
+
+    send(grads.at[:, 2304:3072], g_qkv)
+    send(grads.at[:, 1024:1280], g_out)
+    send(grads.at[:, 0:1024], g_up)
+    for n in range(4):
+        send(grads.at[:, 1280 + 256 * n : 1536 + 256 * n], g_down.at[pl.ds(128 * n, 128), :])
+    outs = (o_master, o_first, o_second)
 
     def place(base, grad, state, decay):
         rows, columns = grad.shape
         wide = columns // HALF
-        for out, value in zip(outs, adam_update(grad, state, decay)):
+        for n, value in enumerate(adam_update(grad, state, decay)):
             for c in range(wide):
                 at = pl.ds(base + c, rows, stride=wide) if wide > 1 else pl.ds(base, rows)
-                out[at, :] = value[:, c * HALF : (c + 1) * HALF]
-
-    qkv, outer, up = grads[:, 2304:3072], grads[:, 1024:1280], grads[:, 0:1024]
-    g_qkv[...] = qkv
-    g_out[...] = outer
-    g_up[...] = up
-    place(0, qkv, s_qkv, WEIGHT_DECAY)
-    place(768, outer, s_out, WEIGHT_DECAY)
-    place(1024, up, s_up, WEIGHT_DECAY)
+                flat[n, at, :] = value[:, c * HALF : (c + 1) * HALF]
+
+    def ship(base, count):
+        for n, there in enumerate(outs):
+            send(flat.at[n, pl.ds(base, count), :], there.reshape(flat.shape[1:]).at[pl.ds(base, count), :])
+
+    place(1024, grads[:, 0:1024], s_up, WEIGHT_DECAY)
+    ship(1024, 1024)
     for n in range(4):
         rows = slice(128 * n, 128 * n + 128)
-        down = grads[:, 1280 + 256 * n : 1536 + 256 * n]
-        g_down[rows, :] = down
-        place(2048 + 256 * n, down, s_down[:, rows, :], WEIGHT_DECAY)
+        place(2048 + 256 * n, grads[:, 1280 + 256 * n : 1536 + 256 * n], s_down[:, rows, :], WEIGHT_DECAY)
+    ship(2048, 1024)
+    place(0, grads[:, 2304:3072], s_qkv, WEIGHT_DECAY)
+    ship(0, 768)
+    place(768, grads[:, 1024:1280], s_out, WEIGHT_DECAY)
+    ship(768, 256)
     extra = grads[0:16, 3072:3200]
     g_bias[...] = extra[0:4]
-    place(3072, extra[0:4], s_bias, 0.0)
+    bias = [
+        jnp.concatenate([s_bias[n : n + 1, c * HALF : (c + 1) * HALF] for c in range(4)], axis=0) for n in range(3)
+    ]
+    place(3072, extra[0:4], bias, 0.0)
     vec = jnp.concatenate(
         [jnp.concatenate([extra[4 + 2 * n : 5 + 2 * n], extra[5 + 2 * n : 6 + 2 * n]], axis=1) for n in range(4)], axis=0
     )
     g_vec[...] = vec
     place(3076, vec, s_vec, 0.0)
-    copies = [
-        pltpu.make_async_copy(flat.at[n], there.reshape(flat.shape[1:]), sems.at[n])
-        for n, there in enumerate((o_master, o_first, o_second))
-    ]
-    for copy in copies:
-        copy.start()
+    ship(3072, 12)
     for copy in copies:
         copy.wait()
 
 
-def update(data_index, parts, states, after):
+def update(data_index, parts, states):
     shape = lambda *dims: jax.ShapeDtypeStruct(dims, F32)
     s_qkv, s_out, s_up, s_down, s_bias, s_vec = states
     flat = shape(1, 3084 * HALF)
+    away = pl.BlockSpec(memory_space=pltpu.HBM)
     *grads, master, first, second = pl.pallas_call(
         update_kernel,
         out_shape=(
             shape(128, 768), shape(128, 256), shape(128, 1024), shape(512, 256), shape(4, HALF), shape(4, 256),
             flat, flat, flat,
         ),
-        in_specs=[smem()] + [vmem()] * 10 + [pl.BlockSpec(memory_space=pltpu.HBM)] * 2,
-        out_specs=[vmem()] * 6 + [pl.BlockSpec(memory_space=pltpu.HBM)] * 3,
+        in_specs=[smem()] + [vmem()] * 10,
+        out_specs=[away] * 4 + [vmem()] * 2 + [away] * 3,
         scratch_shapes=[
-            pltpu.VMEM((128, 3200), F32), pltpu.VMEM((3, 3084, HALF), F32), pltpu.SemaphoreType.DMA((3,)),
+            pltpu.VMEM((128, 3200), F32), pltpu.VMEM((3, 3084, HALF), F32), pltpu.SemaphoreType.DMA((22,)),
         ],
         compiler_params=pltpu.CompilerParams(vmem_limit_bytes=VMEM_LIMIT),
         cost_estimate=pl.CostEstimate(flops=10_000_000, bytes_accessed=14_000_000, transcendentals=400_000),
         name="update",
-    )(data_index.reshape(1), *parts, s_qkv, s_out, s_up, s_down, s_bias.reshape(3, 4, HALF), s_vec, *after)
+    )(data_index.reshape(1), *parts, s_qkv, s_out, s_up, s_down, s_bias, s_vec)
     grads[4] = grads[4].reshape(-1)
     return tuple(grads) + (master, first, second)
 
@@ -934,18 +952,21 @@
     gin, *late = hold((gin, *late), (back_out, *early[1:]))
     back_gin = from_slot(gin)
 
-    def sum_all(early, late):
+    def sum_all(early, late, back_out):
         early, late = total(early), total(trade(late))
         sums = jnp.concatenate([early[:, :2304], late[:, :768], early[:, 2304:] + late[:, 768:]], axis=1)
-        return sum_rest(sums, data_index)
-
-    made = jax.eval_shape(sum_all, early, late)
-    mine = lax.cond(live_blocks[0] > 0, sum_all, lambda *unused: jnp.zeros(made.shape, made.dtype), early, late)
-    parts = spread_sums(mine)
-    layer_out = reorder(shard, assign, back_out, True, (mine,))
-    input_grad = reorder(shard, assign, back_gin, True, (parts[0],))
+        return sum_rest(sums, data_index, lambda part: reorder(shard, assign, back_out, True, (part,)))
+
+    made = jax.eval_shape(sum_all, early, late, back_out)
+    mine, layer_out = lax.cond(
+        live_blocks[0] > 0,
+        sum_all,
+        lambda *unused: jax.tree.map(lambda one: jnp.zeros(one.shape, one.dtype), made),
+        early, late, back_out,
+    )
+    parts, input_grad = spread_sums(mine, lambda near: reorder(shard, assign, back_gin, True, (near,)))
     states = (state_qkv, state_out, state_up, state_down, state_ubias, state_vec)
-    updated = update(data_index, parts, states, (layer_out, input_grad))
+    updated = update(data_index, parts, states)
     return (layer_out, input_grad) + updated
 
 

time: 283 us -> 271 us (0.958)
  waiting for transfers between devices: 77.1 us -> 69.7 us
  Pallas kernels: 142 us -> 138 us
    ppermute x3, waiting for transfers between devices: 27.4 us -> 19.8 us  [sum_rest(): lax.ppermute(piece(k + 1).astype(LOW), 'dp', hop)]
    pallas_call x1, Pallas kernels: 48.9 us -> 44.5 us  [backward_attention(): pl.pallas_call(backward_kernel, out_shape=(shape((length, 256), LOW),) +...]
    ppermute x1, waiting for transfers between devices: 4.2 us -> 1.21 us  [spread_sums(): across = hold((lax.ppermute(near, 'dp', flip),), (other,))[0]]
  transfers between devices with their start and end apart: 21 -> 21, of which waited for: 11 -> 11; matrix products, arithmetic and copies ran while one was open for 3% -> 4% of each run, Pallas kernels for 46% -> 47%
where the time goes in v5:
time: 271 us
  Pallas kernels  138 us (51%)
  waiting for transfers between devices  69.7 us (26%)
  starting transfers between devices  46.4 us (17%)
  local copies, waits for them, and re-layouts  7.28 us (3%)
  other arithmetic  6.82 us (3%)
    pallas_call x1, Pallas kernels, backward_attention(): pl.pallas_call(backward_kernel, out_shape=(shape((length, 256), LOW),) +...  44.5 us
    pallas_call x1, Pallas kernels, forward_attention(): pl.pallas_call(forward_kernel, out_shape=(rows, rows, rows, jax.ShapeDtyp...  28.1 us
    pallas_call x1, Pallas kernels, behind(): pl.pallas_call(behind_kernel, grid_spec=pltpu.PrefetchScalarGridSpec(num_...  21.8 us
    ppermute x3, waiting for transfers between devices, sum_rest(): lax.ppermute(piece(k + 1).astype(LOW), 'dp', hop)  19.8 us
    all_to_all x2, starting transfers between devices, to_slot(): lax.all_to_all(rows, 'dp', split_axis=0, concat_axis=0, tiled=True)  18.7 us
    pallas_call x1, Pallas kernels, ahead(): pl.pallas_call(ahead_kernel, grid_spec=pltpu.PrefetchScalarGridSpec(num_s...  17.5 us
    ppermute x1, waiting for transfers between devices, on_device(): got = lax.ppermute(pack, 'shard', [(0, 1), (1, 0)])  15.9 us
    pallas_call x4, Pallas kernels, reorder(): pl.pallas_call(functools.partial(reorder_kernel, scatter), out_shape=jax....  14.3 us
  transfers between devices with their start and end apart: 21, of which 11 were waited for; matrix products, arithmetic and copies ran while one was open for 4% of the time, Pallas kernels for 47%

profile of v5, /device:TPU:0, one launch (start us, length us, event | category | flops | bytes accessed | tf_op | source)
XLA Modules:
  0.0 270.6 jit_solution(14579192159556768809)
XLA Ops:
  0.6 3.2 %reorder.5.after = bf16[16,256,256]{2,1,0:T(8,128)(2,1)} custom-call(s32[1]{0:T(128)} %bitcast.4.where.shard, s32[32]{0:T(128)} %assign.5, bf16[16,256,256]{2,1,0:T(8,128)(2,1)} %src.2), custom_call_target="tpu_custom_call" | custom-call | bytes 4194304 | tf_op jit(solution)/shard_map/reorder/pallas_call | solution.py:672
  3.9 7.4 %all-to-all-start.1 = ((bf16[16,256,256]{2,1,0:T(8,128)(2,1)}), bf16[16,256,256]{2,1,0:T(8,128)(2,1)S(1)}, u32[]{:S(2)}, u32[]{:S(2)}) async-start(bf16[16,256,256]{2,1,0:T(8,128)(2,1)} %reorder.5.after), calls=%async_computation.1 | async-start | bytes 4194304 | tf_op jit(solution)/shard_map/all_to_all | solution.py:926
  11.9 2.2 pack_weights.1.own
  14.1 1.5 collective-permute-start.7
  20.4 15.9 %collective-permute-done.7.got = bf16[144,3072]{1,0:T(8,128)(2,1)S(1)} collective-permute-done((bf16[144,3072]{1,0:T(8,128)(2,1)}, bf16[144,3072]{1,0:T(8,128)(2,1)S(1)}, u32[]{:S(2)}, u32[]{:S(2)}) %collective-permute-start.7) | collective-permute-done | bytes 884768 | tf_op jit(solution)/shard_map/ppermute | solution.py:931
  37.2 2.8 %unpack_weights.1 = (bf16[256,768]{1,0:T(8,128)(2,1)}, bf16[256,256]{1,0:T(8,128)(2,1)}, bf16[256,1024]{1,0:T(8,128)(2,1)}, bf16[1024,256]{1,0:T(8,128)(2,1)}, b...) custom-call(s32[1]{0:T(128)} %bitcast.4.where.shard, ...), custom_call_target="tpu_custom_call" | custom-call | tf_op jit(solution)/shard_map/unpack_weights/pallas_call | solution.py:754
  40.8 3.1 %reorder.6 = bf16[16,256,256]{2,1,0:T(8,128)(2,1)} custom-call(s32[1]{0:T(128)} %bitcast.4.where.shard, s32[32]{0:T(128)S(1)} %copy-done.10, bf16[16,256,256]{2,1,0:T(8,128)(2,1)} %src.3, bf16[256,768]{1,0:T(8,128)(2,1)} %get-tuple-element.98.rest_0_.w, s32[2]{0:T(128)} %pad_add_fusion.rest_1_.scal, f32[3,64,128]{2,1,0:T(8,128)} %broadcast_in_dim.13.rest_2_.table, ...), custom_call_target="tpu_custom_call" | custom-call | bytes 4194304 | tf_op jit(solution)/shard_map/reorder/pallas_call | solution.py:672
  43.9 8.5 %all-to-all-done.1 = bf16[16,256,256]{2,1,0:T(8,128)(2,1)S(1)} async-done(((bf16[16,256,256]{2,1,0:T(8,128)(2,1)}), bf16[16,256,256]{2,1,0:T(8,128)(2,1)S(1)}, u32[]{:S(2)}, u32[]{:S(2)}) %all-to-all-start.1) | async-done | bytes 2097184 | tf_op jit(solution)/shard_map/all_to_all | solution.py:926
  52.4 11.3 %all-to-all-start = ((bf16[16,256,256]{2,1,0:T(8,128)(2,1)}), bf16[16,256,256]{2,1,0:T(8,128)(2,1)}, u32[]{:S(2)}, u32[]{:S(2)}) async-start(bf16[16,256,256]{2,1,0:T(8,128)(2,1)} %reorder.6), calls=%async_computation | async-start | bytes 4194304 | tf_op jit(solution)/shard_map/all_to_all | solution.py:926
  63.7 28.1 %attend_forward.1 = (bf16[4096,256]{1,0:T(8,128)(2,1)}, bf16[4096,256]{1,0:T(8,128)(2,1)}, bf16[4096,256]{1,0:T(8,128)(2,1)}, bf16[256,4096]{1,0:T(8,128)(2,1)},...) custom-call(s32[2]{0:T(128)} %pad_add_fusion.rest_1_.scal, s32[768]{0:T(1024)} %reshape.56.rest_3_.drawn, ...), custom_call_target="tpu_custom_call" | custom-call | flops 16000000000 | bytes 12000000 | tf_op jit(solution)/shard_map/attend_forward/pallas_call | solution.py:269
  91.8 17.5 %ahead.1 = (bf16[4096,256]{1,0:T(8,128)(2,1)}, bf16[4096,256]{1,0:T(8,128)(2,1)}, bf16[4096,256]{1,0:T(8,128)(2,1)}, bf16[4096,1024]{1,0:T(8,128)(2,1)}, bf16[4096,1024]{1,0:T(8,128)(2,1)}) custom-call(s32[2]{0:T(128)} %pad_add_fusion.rest_1_.scal, f32[3,64,128]{2,1,0:T(8,128)} %broadcast_in_dim.13.rest_2_.table, bf16[4096,256]{1,0:T(8,128)(2,1)} %bitcast.18, ...), custom_call_target="tpu_custom_call" | custom-call | flops 5000000000 | bytes 34000000 | tf_op jit(solution)/shard_map/ahead/pallas_call | solution.py:362
  109.3 6.7 %all-to-all-start.2 = ((bf16[16,256,256]{2,1,0:T(8,128)(2,1)}), bf16[16,256,256]{2,1,0:T(8,128)(2,1)S(1)}, u32[]{:S(2)}, u32[]{:S(2)}) async-start(bf16[16,256,256]{2,1,0:T(8,128)(2,1)} %bitcast.20), calls=%async_computation.2 | async-start | bytes 4194304 | tf_op jit(solution)/shard_map/all_to_all | solution.py:944
  116.1 21.8 %behind.1 = (f32[4096,256]{1,0:T(8,128)}, bf16[4096,256]{1,0:T(8,128)(2,1)}, f32[64,256]{1,0:T(8,128)}, bf16[64,2432]{1,0:T(8,128)(2,1)}, bf16[64,2432]{1,0:T(8,...) custom-call(s32[2]{0:T(128)} %pad_add_fusion.rest_1_.scal, f32[3,64,128]{2,1,0:T(8,128)} %broadcast_in_dim.13.rest_2_.table, ...), custom_call_target="tpu_custom_call" | custom-call | flops 10000000000 | bytes 40000000 | tf_op jit(solution)/shard_map/behind/pallas_call | solution.py:475
  138.3 1.5 collective-permute-start.9
  139.8 44.5 %attend_backward.1 = (bf16[4096,256]{1,0:T(8,128)(2,1)}, bf16[64,896]{1,0:T(8,128)(2,1)S(1)}, bf16[64,896]{1,0:T(8,128)(2,1)}, bf16[64,896]{1,0:T(8,128)(2,1)}, bf16[64,896]{1,0:T(8,128)(2,1)}) custom-call(s32[2]{0:T(128)} %pad_add_fusion.rest_1_.scal, s32[768]{0:T(1024)} %reshape.56.rest_3_.drawn, f32[3,64,128]{2,1,0:T(8,128)} %broadcast_in_dim.13.rest_2_.table, ...), custom_call_target="tpu_custom_call" | custom-call | flops 40000000000 | bytes 20000000 | tf_op jit(solution)/shard_map/attend_backward/pallas_call | solution.py:625
  184.3 6.1 %all-to-all-start.3 = ((bf16[16,256,256]{2,1,0:T(8,128)(2,1)}), bf16[16,256,256]{2,1,0:T(8,128)(2,1)}, u32[]{:S(2)}, u32[]{:S(2)}) async-start(bf16[16,256,256]{2,1,0:T(8,128)(2,1)} %bitcast.16), calls=%async_computation.3 | async-start | bytes 4194304 | tf_op jit(solution)/shard_map/all_to_all | solution.py:944
  191.0 55.1 %conditional.1 = (bf16[8,3200]{1,0:T(8,128)(2,1)}, bf16[16,256,256]{2,1,0:T(8,128)(2,1)}, bf16[1,8,3200]{2,1,0:T(8,128)(2,1)S(1)}) conditional(s32[]{:T(128)} %bitcast.1, () %tuple.18, (bf16[64,2432]{1,0:T(8,128)(2,1)}, bf16[64,2432]{1,0:T(8,128)(2,1)S(1)}, bf16[64,2432]{1,0:T(8,128)(2,1)S(1)}, bf16[64,2432]{1,0:T(8,128)(2,1)S(1)}, ...), branch_computations={%region_0.1_spmd, %region_1.2_spmd} | conditional | flops 2292824 | bytes 18568518 | solution.py:961
  191.5 1.5 collective-permute-start.1
  194.4 3.3 %collective-permute-done.1 = bf16[64,896]{1,0:T(8,128)(2,1)} collective-permute-done((bf16[64,896]{1,0:T(8,128)(2,1)}, bf16[64,896]{1,0:T(8,128)(2,1)}, u32[]{:S(2)}, u32[]{:S(2)}) %collective-permute-start.1) | collective-permute-done | bytes 114720 | tf_op jit(solution)/shard_map/cond/branch_1_fun/ppermute | solution.py:773
  200.1 2.1 collective-permute-start.3
  202.1 12.4 %collective-permute-done.3 = bf16[32,3200]{1,0:T(8,128)(2,1)S(1)} collective-permute-done((bf16[32,3200]{1,0:T(8,128)(2,1)S(1)}, bf16[32,3200]{1,0:T(8,128)(2,1)S(1)}, u32[]{:S(2)}, u32[]{:S(2)}) %collective-permute-start.3) | collective-permute-done | bytes 204832 | tf_op jit(solution)/shard_map/cond/branch_1_fun/ppermute | solution.py:789
  214.6 3.8 %collective-permute-start.6 = (bf16[8,3200]{1,0:T(8,128)(2,1)S(1)}, bf16[8,3200]{1,0:T(8,128)(2,1)S(1)}, u32[]{:S(2)}, u32[]{:S(2)}) collective-permute-start(bf16[8,3200]{1,0:T(8,128)(2,1)S(1)} %get-tuple-element.149), channel_id=1, source_target_pairs={{0,24},{2,26},{4,28},{6,30},{8,0},{10,2},{12,4},{14,6},{16,8},{18,... | collective-permute-start | bytes 153608 | tf_op jit(solution)/shard_map/cond/branch_1_fun/ppermute | solution.py:799
  219.1 4.9 %reorder.4.refs_1_ = bf16[16,256,256]{2,1,0:T(8,128)(2,1)} custom-call(s32[1]{0:T(128)} %get-tuple-element.34.where, s32[32]{0:T(128)S(1)} %get-tuple-element.35.assign, bf16[16,256,256]{2,1,0:T(8,128)(2,1)S(1)} %get-tuple-element.36.src, f32[32,3200]{1,0:T(8,128)} %copy-done), custom_call_target="tpu_custom_call" | custom-call | bytes 4194304 | tf_op jit(solution)/shard_map/cond/branch_1_fun/reorder/pallas_call | solution.py:672
  224.0 6.8 %collective-permute-done.4 = bf16[8,3200]{1,0:T(8,128)(2,1)S(1)} collective-permute-done((bf16[8,3200]{1,0:T(8,128)(2,1)S(1)}, bf16[8,3200]{1,0:T(8,128)(2,1)S(1)}, u32[]{:S(2)}, u32[]{:S(2)}) %collective-permute-start.4) | collective-permute-done | bytes 51232 | tf_op jit(solution)/shard_map/cond/branch_1_fun/ppermute | solution.py:799
  230.8 13.1 %collective-permute-done.5 = bf16[8,3200]{1,0:T(8,128)(2,1)S(1)} collective-permute-done((bf16[8,3200]{1,0:T(8,128)(2,1)S(1)}, bf16[8,3200]{1,0:T(8,128)(2,1)S(1)}, u32[]{:S(2)}, u32[]{:S(2)}) %collective-permute-start.5) | collective-permute-done | bytes 51232 | tf_op jit(solution)/shard_map/cond/branch_1_fun/ppermute | solution.py:799
  243.8 1.5 add_convert_fusion
  246.2 1.5 collective-permute-start.13
  248.2 2.3 collective-permute-done.13
  250.5 3.5 %collective-permute-done.12 = bf16[8,3200]{1,0:T(8,128)(2,1)S(1)} collective-permute-done((bf16[8,3200]{1,0:T(8,128)(2,1)}, bf16[8,3200]{1,0:T(8,128)(2,1)S(1)}, u32[]{:S(2)}, u32[]{:S(2)}) %collective-permute-start.12) | collective-permute-done | bytes 51232 | tf_op jit(solution)/shard_map/ppermute | solution.py:809
  256.3 3.1 %reorder.7.refs_1_ = bf16[16,256,256]{2,1,0:T(8,128)(2,1)} custom-call(s32[1]{0:T(128)} %bitcast.4.where.shard, s32[32]{0:T(128)S(1)} %copy-done.10, bf16[16,256,256]{2,1,0:T(8,128)(2,1)} %all-to-all-done.3.src, bf16[4,8,3200]{2,1,0:T(8,128)(2,1)} %copy-done.2), custom_call_target="tpu_custom_call" | custom-call | bytes 4194304 | tf_op jit(solution)/shard_map/reorder/pallas_call | solution.py:672
  261.3 1.7 collective-permute-done.16.across_core
  263.7 6.7 %update.1 = (f32[128,768]{1,0:T(8,128)}, f32[128,256]{1,0:T(8,128)}, f32[128,1024]{1,0:T(8,128)}, f32[512,256]{1,0:T(8,128)}, f32[4,128]{1,0:T(4,128)}, /*index=...) custom-call(s32[1]{0:T(128)} %bitcast.12.where, bf16[4,8,3200]{2,1,0:T(8,128)(2,1)} %copy-done.2, ...), custom_call_target="tpu_custom_call" | custom-call | flops 10000000 | bytes 14000000 | tf_op jit(solution)/shard_map/update/pallas_call | solution.py:895
  (77 shorter events, 17.9 us)
Async XLA Ops:
  3.9 7.4 %copy-start.13 = (bf16[512]{0:T(512)(128)(2,1)S(1)}, bf16[512]{0:T(512)(128)(2,1)}, u32[]{:S(2)}) copy-start(bf16[512]{0:T(512)(128)(2,1)} %param.30) | copy-start | bytes 3076
  3.9 48.5 %all-to-all-start.1 = ((bf16[16,256,256]{2,1,0:T(8,128)(2,1)}), bf16[16,256,256]{2,1,0:T(8,128)(2,1)S(1)}, u32[]{:S(2)}, u32[]{:S(2)}) async-start(bf16[16,256,256]{2,1,0:T(8,128)(2,1)} %reorder.5.after), calls=%async_computation.1 | async-start | bytes 4194304 | tf_op jit(solution)/shard_map/all_to_all | solution.py:926
  11.3 4.3 %copy-start.10 = (s32[32]{0:T(128)S(1)}, s32[32]{0:T(128)}, u32[]{:S(2)}) copy-start(s32[32]{0:T(128)} %assign.5) | copy-start | bytes 388
  11.3 5.5 %copy-start.11 = (s32[1,4,64,3]{2,1,3,0:T(4,128)S(1)}, s32[1,4,64,3]{2,1,3,0:T(4,128)}, u32[]{:S(2)}) copy-start(s32[1,4,64,3]{2,1,3,0:T(4,128)} %param.25) | copy-start | bytes 9220
  11.3 7.1 %copy-start.12 = (s32[32]{0:T(128)S(1)}, s32[32]{0:T(128)}, u32[]{:S(2)}) copy-start(s32[32]{0:T(128)} %param.23) | copy-start | bytes 388
  14.1 22.2 %collective-permute-start.7 = (bf16[144,3072]{1,0:T(8,128)(2,1)}, bf16[144,3072]{1,0:T(8,128)(2,1)S(1)}, u32[]{:S(2)}, u32[]{:S(2)}) collective-permute-start(bf16[144,3072]{1,0:T(8,128)(2,1)} %pack_weights.1.own), channel_id=1, source_target_pairs={{0,1},{1,0},{2,3},{3,2},{4,5},{5,4},{6,7},{7,6},{8,9},{9,8},{10,11... | collective-permute-start | bytes 2654216 | tf_op jit(solution)/shard_map/ppermute | solution.py:931
  52.4 11.3 %copy-start.1 = (bf16[16,256,256]{2,1,0:T(8,128)(2,1)}, bf16[16,256,256]{2,1,0:T(8,128)(2,1)S(1)}, u32[]{:S(2)}) copy-start(bf16[16,256,256]{2,1,0:T(8,128)(2,1)S(1)} %all-to-all-done.1) | copy-start | bytes 6291460
  52.4 56.9 %all-to-all-start = ((bf16[16,256,256]{2,1,0:T(8,128)(2,1)}), bf16[16,256,256]{2,1,0:T(8,128)(2,1)}, u32[]{:S(2)}, u32[]{:S(2)}) async-start(bf16[16,256,256]{2,1,0:T(8,128)(2,1)} %reorder.6), calls=%async_computation | async-start | bytes 4194304 | tf_op jit(solution)/shard_map/all_to_all | solution.py:926
  109.3 75.0 %all-to-all-start.2 = ((bf16[16,256,256]{2,1,0:T(8,128)(2,1)}), bf16[16,256,256]{2,1,0:T(8,128)(2,1)S(1)}, u32[]{:S(2)}, u32[]{:S(2)}) async-start(bf16[16,256,256]{2,1,0:T(8,128)(2,1)} %bitcast.20), calls=%async_computation.2 | async-start | bytes 4194304 | tf_op jit(solution)/shard_map/all_to_all | solution.py:944
  137.8 46.5 %collective-permute-start.8 = (bf16[64,2432]{1,0:T(8,128)(2,1)}, bf16[64,2432]{1,0:T(8,128)(2,1)S(1)}, u32[]{:S(2)}, u32[]{:S(2)}) collective-permute-start(bf16[64,2432]{1,0:T(8,128)(2,1)} %get-tuple-element.114), channel_id=1, source_target_pairs={{0,2},{1,3},{2,0},{3,1},{4,6},{5,7},{6,4},{7,5},{8,10},{9,11},{10,... | collective-permute-start | bytes 933896 | tf_op jit(solution)/shard_map/ppermute | solution.py:773
  138.3 46.0 %collective-permute-start.9 = (bf16[64,2432]{1,0:T(8,128)(2,1)}, bf16[64,2432]{1,0:T(8,128)(2,1)S(1)}, u32[]{:S(2)}, u32[]{:S(2)}) collective-permute-start(bf16[64,2432]{1,0:T(8,128)(2,1)} %get-tuple-element.115), channel_id=1, source_target_pairs={{0,1},{1,0},{2,3},{3,2},{4,5},{5,4},{6,7},{7,6},{8,9},{9,8},{10,11... | collective-permute-start | bytes 933896 | tf_op jit(solution)/shard_map/ppermute | solution.py:773
  139.8 44.5 %collective-permute-start.10 = (bf16[64,2432]{1,0:T(8,128)(2,1)}, bf16[64,2432]{1,0:T(8,128)(2,1)S(1)}, u32[]{:S(2)}, u32[]{:S(2)}) collective-permute-start(bf16[64,2432]{1,0:T(8,128)(2,1)} %get-tuple-element.116), channel_id=1, source_target_pairs={{0,3},{1,2},{2,1},{3,0},{4,7},{5,6},{6,5},{7,4},{8,11},{9,10},{10,... | collective-permute-start | bytes 933896 | tf_op jit(solution)/shard_map/ppermute | solution.py:773
  184.3 72.0 %all-to-all-start.3 = ((bf16[16,256,256]{2,1,0:T(8,128)(2,1)}), bf16[16,256,256]{2,1,0:T(8,128)(2,1)}, u32[]{:S(2)}, u32[]{:S(2)}) async-start(bf16[16,256,256]{2,1,0:T(8,128)(2,1)} %bitcast.16), calls=%async_computation.3 | async-start | bytes 4194304 | tf_op jit(solution)/shard_map/all_to_all | solution.py:944
  191.1 2.0 copy-start.3
  191.1 2.0 copy-start.6
  191.1 3.3 %collective-permute-start = (bf16[64,896]{1,0:T(8,128)(2,1)}, bf16[64,896]{1,0:T(8,128)(2,1)}, u32[]{:S(2)}, u32[]{:S(2)}) collective-permute-start(bf16[64,896]{1,0:T(8,128)(2,1)} %get-tuple-element.30), channel_id=1, source_target_pairs={{0,2},{1,3},{2,0},{3,1},{4,6},{5,7},{6,4},{7,5},{8,10},{9,11},{10,... | collective-permute-start | bytes 344072 | tf_op jit(solution)/shard_map/cond/branch_1_fun/ppermute | solution.py:773
  191.5 6.2 %collective-permute-start.1 = (bf16[64,896]{1,0:T(8,128)(2,1)}, bf16[64,896]{1,0:T(8,128)(2,1)}, u32[]{:S(2)}, u32[]{:S(2)}) collective-permute-start(bf16[64,896]{1,0:T(8,128)(2,1)} %get-tuple-element.31), channel_id=1, source_target_pairs={{0,1},{1,0},{2,3},{3,2},{4,5},{5,4},{6,7},{7,6},{8,9},{9,8},{10,11... | collective-permute-start | bytes 344072 | tf_op jit(solution)/shard_map/cond/branch_1_fun/ppermute | solution.py:773
  193.1 5.7 %collective-permute-start.2 = (bf16[64,896]{1,0:T(8,128)(2,1)}, bf16[64,896]{1,0:T(8,128)(2,1)}, u32[]{:S(2)}, u32[]{:S(2)}) collective-permute-start(bf16[64,896]{1,0:T(8,128)(2,1)} %get-tuple-element.32), channel_id=1, source_target_pairs={{0,3},{1,2},{2,1},{3,0},{4,7},{5,6},{6,5},{7,4},{8,11},{9,10},{10,... | collective-permute-start | bytes 344072 | tf_op jit(solution)/shard_map/cond/branch_1_fun/ppermute | solution.py:773
  200.1 14.4 %collective-permute-start.3 = (bf16[32,3200]{1,0:T(8,128)(2,1)S(1)}, bf16[32,3200]{1,0:T(8,128)(2,1)S(1)}, u32[]{:S(2)}, u32[]{:S(2)}) collective-permute-start(bf16[32,3200]{1,0:T(8,128)(2,1)S(1)} %dynamic-slice_convert_fusion), channel_id=1, source_target_pairs={{0,4},{2,6},{4,0},{6,2},{8,12},{10,14},{12,8},{14,10},{16,20},{18,... | collective-permute-start | bytes 614408 | tf_op jit(solution)/shard_map/cond/branch_1_fun/ppermute | solution.py:789
  214.5 4.6 %copy-start = (f32[32,3200]{1,0:T(8,128)}, f32[32,3200]{1,0:T(8,128)S(1)}, u32[]{:S(2)}) copy-start(f32[32,3200]{1,0:T(8,128)S(1)} %convert_add_fusion.1.rest_0_) | copy-start | bytes 1228804 | tf_op jit(solution)/shard_map/cond
  214.6 16.2 %collective-permute-start.4 = (bf16[8,3200]{1,0:T(8,128)(2,1)S(1)}, bf16[8,3200]{1,0:T(8,128)(2,1)S(1)}, u32[]{:S(2)}, u32[]{:S(2)}) collective-permute-start(bf16[8,3200]{1,0:T(8,128)(2,1)S(1)} %get-tuple-element.148), channel_id=1, source_target_pairs={{0,8},{2,10},{4,12},{6,14},{8,16},{10,18},{12,20},{14,22},{16,24},... | collective-permute-start | bytes 153608 | tf_op jit(solution)/shard_map/cond/branch_1_fun/ppermute | solution.py:799
  214.6 16.1 %collective-permute-start.6 = (bf16[8,3200]{1,0:T(8,128)(2,1)S(1)}, bf16[8,3200]{1,0:T(8,128)(2,1)S(1)}, u32[]{:S(2)}, u32[]{:S(2)}) collective-permute-start(bf16[8,3200]{1,0:T(8,128)(2,1)S(1)} %get-tuple-element.149), channel_id=1, source_target_pairs={{0,24},{2,26},{4,28},{6,30},{8,0},{10,2},{12,4},{14,6},{16,8},{18,... | collective-permute-start | bytes 153608 | tf_op jit(solution)/shard_map/cond/branch_1_fun/ppermute | solution.py:799
  218.5 25.4 %collective-permute-start.5 = (bf16[8,3200]{1,0:T(8,128)(2,1)S(1)}, bf16[8,3200]{1,0:T(8,128)(2,1)S(1)}, u32[]{:S(2)}, u32[]{:S(2)}) collective-permute-start(bf16[8,3200]{1,0:T(8,128)(2,1)S(1)} %get-tuple-element.150), channel_id=1, source_target_pairs={{0,16},{2,18},{4,20},{6,22},{8,24},{10,26},{12,28},{14,30},{16,0},... | collective-permute-start | bytes 153608 | tf_op jit(solution)/shard_map/cond/branch_1_fun/ppermute | solution.py:799
  246.2 7.8 %copy-start.7 = (bf16[1,8,3200]{2,1,0:T(8,128)(2,1)}, bf16[1,8,3200]{2,1,0:T(8,128)(2,1)S(1)}, u32[]{:S(2)}) copy-start(bf16[1,8,3200]{2,1,0:T(8,128)(2,1)S(1)} %get-tuple-element.137) | copy-start | bytes 153604
  246.2 4.3 %collective-permute-start.13 = (bf16[8,3200]{1,0:T(8,128)(2,1)}, bf16[8,3200]{1,0:T(8,128)(2,1)S(1)}, u32[]{:S(2)}, u32[]{:S(2)}) collective-permute-start(bf16[8,3200]{1,0:T(8,128)(2,1)} %get-tuple-element.138), channel_id=1, source_target_pairs={{0,24},{2,26},{4,28},{6,30},{8,0},{10,2},{12,4},{14,6},{16,8},{18,... | collective-permute-start | bytes 153608 | tf_op jit(solution)/shard_map/ppermute | solution.py:809
  247.7 6.3 %collective-permute-start.12 = (bf16[8,3200]{1,0:T(8,128)(2,1)}, bf16[8,3200]{1,0:T(8,128)(2,1)S(1)}, u32[]{:S(2)}, u32[]{:S(2)}) collective-permute-start(bf16[8,3200]{1,0:T(8,128)(2,1)} %get-tuple-element.138), channel_id=1, source_target_pairs={{0,16},{2,18},{4,20},{6,22},{8,24},{10,26},{12,28},{14,30},{16,0},... | collective-permute-start | bytes 153608 | tf_op jit(solution)/shard_map/ppermute | solution.py:809
  247.7 6.3 %collective-permute-start.11 = (bf16[8,3200]{1,0:T(8,128)(2,1)}, bf16[8,3200]{1,0:T(8,128)(2,1)S(1)}, u32[]{:S(2)}, u32[]{:S(2)}) collective-permute-start(bf16[8,3200]{1,0:T(8,128)(2,1)} %get-tuple-element.138), channel_id=1, source_target_pairs={{0,8},{2,10},{4,12},{6,14},{8,16},{10,18},{12,20},{14,22},{16,24},... | collective-permute-start | bytes 153608 | tf_op jit(solution)/shard_map/ppermute | solution.py:809
  254.8 1.5 copy-start.2
  254.8 5.8 %collective-permute-start.14 = (bf16[4,8,3200]{2,1,0:T(8,128)(2,1)S(1)}, bf16[4,8,3200]{2,1,0:T(8,128)(2,1)S(1)}, u32[]{:S(2)}, u32[]{:S(2)}) collective-permute-start(bf16[4,8,3200]{2,1,0:T(8,128)(2,1)S(1)} %pad_maximum_fusion.1.rest_0_.near), channel_id=1, source_target_pairs={{0,4},{2,6},{4,0},{6,2},{8,12},{10,14},{12,8},{14,10},{16,20},{18,... | collective-permute-start | bytes 614408 | tf_op jit(solution)/shard_map/ppermute | solution.py:812
  256.3 5.0 %collective-permute-start.15 = (bf16[4,8,3200]{2,1,0:T(8,128)(2,1)S(1)}, bf16[4,8,3200]{2,1,0:T(8,128)(2,1)S(1)}, u32[]{:S(2)}, u32[]{:S(2)}) collective-permute-start(bf16[4,8,3200]{2,1,0:T(8,128)(2,1)S(1)} %pad_maximum_fusion.1.rest_0_.near), channel_id=1, source_target_pairs={{0,2},{2,0},{4,6},{6,4},{8,10},{10,8},{12,14},{14,12},{16,18},{18,... | collective-permute-start | bytes 614408 | tf_op jit(solution)/shard_map/ppermute | solution.py:813
  261.3 1.7 collective-permute-start.16
  261.3 1.7 copy-start.8
  (3 other events, 2.3 us)

commit v6 on v5

--- a/solution.py
+++ b/solution.py
@@ -27,7 +27,7 @@
 GROUP = 31
 AHEAD_ROWS = 1024
 BEHIND_ROWS = 512
-BACK = 10
+BACK = 20
 
 
 def dot_nn(a, b):
@@ -410,8 +410,8 @@
     grad_first = grad_z2 + dot_nt(back[...], w_up[...])
     gup_o[...] += dot_tn(first_low, back[...])
     grad_z1 = normalize_back(grad_first * row(3), normed_one, factor_one)
-    gz1_o[...] = grad_z1
     grad_attended = grad_z1.astype(LOW)
+    gz1_o[...] = grad_attended
     ctx_v = ctx[...]
     gout_o[...] += dot_tn(ctx_v, grad_attended)
     grad_context = dot_nt(grad_attended, w_out[...]).astype(LOW)
@@ -491,7 +491,7 @@
             ],
         ),
         out_shape=(
-            shape((length, 256), F32), shape((length, 256), LOW), shape((length // BLOCK, 256), F32),
+            shape((length, 256), LOW), shape((length, 256), LOW), shape((length // BLOCK, 256), F32),
         ) + (shape((64, 2432), LOW),) * 4,
         compiler_params=pltpu.CompilerParams(vmem_limit_bytes=VMEM_LIMIT),
         cost_estimate=pl.CostEstimate(flops=10_000_000_000, bytes_accessed=40_000_000, transcendentals=0),
@@ -600,7 +600,7 @@
     def finish(c, shifts):
         rows = pl.ds(pl.multiple_of(c * 512, 512), 512)
         dqkv = jnp.concatenate([dq[rows, :], dk[rows, :].astype(LOW), dv[rows, :].astype(LOW)], axis=1)
-        gin_v[rows, :] = (gz1_v[rows, :] + dot_nt(dqkv, w[...])).astype(LOW)
+        gin_v[rows, :] = (gz1_v[rows, :].astype(F32) + dot_nt(dqkv, w[...])).astype(LOW)
         gw_o[...] += dot_tn(x_v[rows, :], dqkv)
         return shifts + jnp.sum(dqkv.astype(F32), axis=0, keepdims=True)
 
@@ -635,7 +635,7 @@
             pltpu.VMEM((length, 256), F32),
             pltpu.VMEM((length, 256), F32),
             pltpu.VMEM((256, 768), F32),
-            pltpu.VMEM((length, 256), F32),
+            pltpu.VMEM((length, 256), LOW),
             pltpu.VMEM((length, 256), LOW),
             pltpu.VMEM((length, 256), LOW),
             pltpu.SemaphoreType.DMA((3,)),

time: 271 us -> 284 us (1.048); the launches traced: 271 us -> 280 us
  Pallas kernels: 138 us -> 147 us
    pallas_call x1, Pallas kernels: 17.5 us -> 27.9 us  [ahead(): pl.pallas_call(ahead_kernel, grid_spec=pltpu.PrefetchScalarGridSpec(num_s...]
  transfers between devices with their start and end apart: 21 -> 21, of which waited for: 11 -> 11; matrix products, arithmetic and copies ran while one was open for 4% -> 4% of each run, Pallas kernels for 47% -> 49%
where the time goes in v6:
time: 284 us; the launch traced here: 280 us
  Pallas kernels  147 us (52%)
  waiting for transfers between devices  69.7 us (25%)
  starting transfers between devices  45.7 us (16%)
  local copies, waits for them, and re-layouts  7.3 us (3%)
  other arithmetic  6.77 us (2%)
    pallas_call x1, Pallas kernels, backward_attention(): pl.pallas_call(backward_kernel, out_shape=(shape((length, 256), LOW),) +...  43.6 us
    pallas_call x1, Pallas kernels, forward_attention(): pl.pallas_call(forward_kernel, out_shape=(rows, rows, rows, jax.ShapeDtyp...  28.1 us
    pallas_call x1, Pallas kernels, ahead(): pl.pallas_call(ahead_kernel, grid_spec=pltpu.PrefetchScalarGridSpec(num_s...  27.9 us
    pallas_call x1, Pallas kernels, behind(): pl.pallas_call(behind_kernel, grid_spec=pltpu.PrefetchScalarGridSpec(num_...  21.7 us
    ppermute x3, waiting for transfers between devices, sum_rest(): lax.ppermute(piece(k + 1).astype(LOW), 'dp', hop)  19.8 us
    all_to_all x2, starting transfers between devices, to_slot(): lax.all_to_all(rows, 'dp', split_axis=0, concat_axis=0, tiled=True)  18.7 us
    ppermute x1, waiting for transfers between devices, on_device(): got = lax.ppermute(pack, 'shard', [(0, 1), (1, 0)])  16 us
    pallas_call x4, Pallas kernels, reorder(): pl.pallas_call(functools.partial(reorder_kernel, scatter), out_shape=jax....  14.3 us
  transfers between devices with their start and end apart: 21, of which 11 were waited for; matrix products, arithmetic and copies ran while one was open for 4% of the time, Pallas kernels for 49%

profile of v6, /device:TPU:0, one launch (start us, length us, event | category | flops | bytes accessed | tf_op | source)
XLA Modules:
  0.0 279.6 jit_solution(8770861699837151375)
XLA Ops:
  0.6 3.2 %reorder.5.after = bf16[16,256,256]{2,1,0:T(8,128)(2,1)} custom-call(s32[1]{0:T(128)} %bitcast.4.where.shard, s32[32]{0:T(128)} %assign.5, bf16[16,256,256]{2,1,0:T(8,128)(2,1)} %src.2), custom_call_target="tpu_custom_call" | custom-call | bytes 4194304 | tf_op jit(solution)/shard_map/reorder/pallas_call | solution.py:672
  3.9 7.4 %all-to-all-start.1 = ((bf16[16,256,256]{2,1,0:T(8,128)(2,1)}), bf16[16,256,256]{2,1,0:T(8,128)(2,1)S(1)}, u32[]{:S(2)}, u32[]{:S(2)}) async-start(bf16[16,256,256]{2,1,0:T(8,128)(2,1)} %reorder.5.after), calls=%async_computation.1 | async-start | bytes 4194304 | tf_op jit(solution)/shard_map/all_to_all | solution.py:926
  11.9 2.2 pack_weights.1.own
  14.1 1.5 collective-permute-start.7
  20.3 16.0 %collective-permute-done.7.got = bf16[144,3072]{1,0:T(8,128)(2,1)S(1)} collective-permute-done((bf16[144,3072]{1,0:T(8,128)(2,1)}, bf16[144,3072]{1,0:T(8,128)(2,1)S(1)}, u32[]{:S(2)}, u32[]{:S(2)}) %collective-permute-start.7) | collective-permute-done | bytes 884768 | tf_op jit(solution)/shard_map/ppermute | solution.py:931
  37.2 2.8 %unpack_weights.1 = (bf16[256,768]{1,0:T(8,128)(2,1)}, bf16[256,256]{1,0:T(8,128)(2,1)}, bf16[256,1024]{1,0:T(8,128)(2,1)}, bf16[1024,256]{1,0:T(8,128)(2,1)}, b...) custom-call(s32[1]{0:T(128)} %bitcast.4.where.shard, ...), custom_call_target="tpu_custom_call" | custom-call | tf_op jit(solution)/shard_map/unpack_weights/pallas_call | solution.py:754
  40.8 3.1 %reorder.6 = bf16[16,256,256]{2,1,0:T(8,128)(2,1)} custom-call(s32[1]{0:T(128)} %bitcast.4.where.shard, s32[32]{0:T(128)S(1)} %copy-done.10, bf16[16,256,256]{2,1,0:T(8,128)(2,1)} %src.3, bf16[256,768]{1,0:T(8,128)(2,1)} %get-tuple-element.98.rest_0_.w, s32[2]{0:T(128)} %pad_add_fusion.rest_1_.scal, f32[3,64,128]{2,1,0:T(8,128)} %broadcast_in_dim.13.rest_2_.table, ...), custom_call_target="tpu_custom_call" | custom-call | bytes 4194304 | tf_op jit(solution)/shard_map/reorder/pallas_call | solution.py:672
  43.9 8.5 %all-to-all-done.1 = bf16[16,256,256]{2,1,0:T(8,128)(2,1)S(1)} async-done(((bf16[16,256,256]{2,1,0:T(8,128)(2,1)}), bf16[16,256,256]{2,1,0:T(8,128)(2,1)S(1)}, u32[]{:S(2)}, u32[]{:S(2)}) %all-to-all-start.1) | async-done | bytes 2097184 | tf_op jit(solution)/shard_map/all_to_all | solution.py:926
  52.4 11.3 %all-to-all-start = ((bf16[16,256,256]{2,1,0:T(8,128)(2,1)}), bf16[16,256,256]{2,1,0:T(8,128)(2,1)}, u32[]{:S(2)}, u32[]{:S(2)}) async-start(bf16[16,256,256]{2,1,0:T(8,128)(2,1)} %reorder.6), calls=%async_computation | async-start | bytes 4194304 | tf_op jit(solution)/shard_map/all_to_all | solution.py:926
  63.7 28.1 %attend_forward.1 = (bf16[4096,256]{1,0:T(8,128)(2,1)}, bf16[4096,256]{1,0:T(8,128)(2,1)}, bf16[4096,256]{1,0:T(8,128)(2,1)}, bf16[256,4096]{1,0:T(8,128)(2,1)},...) custom-call(s32[2]{0:T(128)} %pad_add_fusion.rest_1_.scal, s32[768]{0:T(1024)} %reshape.56.rest_3_.drawn, ...), custom_call_target="tpu_custom_call" | custom-call | flops 16000000000 | bytes 12000000 | tf_op jit(solution)/shard_map/attend_forward/pallas_call | solution.py:269
  91.8 27.9 %ahead.1 = (bf16[4096,256]{1,0:T(8,128)(2,1)}, bf16[4096,256]{1,0:T(8,128)(2,1)}, bf16[4096,256]{1,0:T(8,128)(2,1)}, bf16[4096,1024]{1,0:T(8,128)(2,1)}, bf16[4096,1024]{1,0:T(8,128)(2,1)}) custom-call(s32[2]{0:T(128)} %pad_add_fusion.rest_1_.scal, f32[3,64,128]{2,1,0:T(8,128)} %broadcast_in_dim.13.rest_2_.table, bf16[4096,256]{1,0:T(8,128)(2,1)} %bitcast.18, ...), custom_call_target="tpu_custom_call" | custom-call | flops 5000000000 | bytes 34000000 | tf_op jit(solution)/shard_map/ahead/pallas_call | solution.py:362
  119.7 6.0 %all-to-all-start.2 = ((bf16[16,256,256]{2,1,0:T(8,128)(2,1)}), bf16[16,256,256]{2,1,0:T(8,128)(2,1)S(1)}, u32[]{:S(2)}, u32[]{:S(2)}) async-start(bf16[16,256,256]{2,1,0:T(8,128)(2,1)} %bitcast.20), calls=%async_computation.2 | async-start | bytes 4194304 | tf_op jit(solution)/shard_map/all_to_all | solution.py:944
  125.7 21.7 %behind.1 = (bf16[4096,256]{1,0:T(8,128)(2,1)}, bf16[4096,256]{1,0:T(8,128)(2,1)}, f32[64,256]{1,0:T(8,128)}, bf16[64,2432]{1,0:T(8,128)(2,1)}, bf16[64,2432]{1,...) custom-call(s32[2]{0:T(128)} %pad_add_fusion.rest_1_.scal, ...), custom_call_target="tpu_custom_call" | custom-call | flops 10000000000 | bytes 40000000 | tf_op jit(solution)/shard_map/behind/pallas_call | solution.py:475
  147.8 1.5 collective-permute-start.9
  149.3 43.6 %attend_backward.1 = (bf16[4096,256]{1,0:T(8,128)(2,1)}, bf16[64,896]{1,0:T(8,128)(2,1)S(1)}, bf16[64,896]{1,0:T(8,128)(2,1)}, bf16[64,896]{1,0:T(8,128)(2,1)}, bf16[64,896]{1,0:T(8,128)(2,1)}) custom-call(s32[2]{0:T(128)} %pad_add_fusion.rest_1_.scal, s32[768]{0:T(1024)} %reshape.56.rest_3_.drawn, f32[3,64,128]{2,1,0:T(8,128)} %broadcast_in_dim.13.rest_2_.table, ...), custom_call_target="tpu_custom_call" | custom-call | flops 40000000000 | bytes 20000000 | tf_op jit(solution)/shard_map/attend_backward/pallas_call | solution.py:625
  193.1 6.1 %all-to-all-start.3 = ((bf16[16,256,256]{2,1,0:T(8,128)(2,1)}), bf16[16,256,256]{2,1,0:T(8,128)(2,1)}, u32[]{:S(2)}, u32[]{:S(2)}) async-start(bf16[16,256,256]{2,1,0:T(8,128)(2,1)} %bitcast.16), calls=%async_computation.3 | async-start | bytes 4194304 | tf_op jit(solution)/shard_map/all_to_all | solution.py:944
  199.8 55.1 %conditional.1 = (bf16[8,3200]{1,0:T(8,128)(2,1)}, bf16[16,256,256]{2,1,0:T(8,128)(2,1)}, bf16[1,8,3200]{2,1,0:T(8,128)(2,1)S(1)}) conditional(s32[]{:T(128)} %bitcast.1, () %tuple.18, (bf16[64,2432]{1,0:T(8,128)(2,1)}, bf16[64,2432]{1,0:T(8,128)(2,1)S(1)}, bf16[64,2432]{1,0:T(8,128)(2,1)S(1)}, bf16[64,2432]{1,0:T(8,128)(2,1)S(1)}, ...), branch_computations={%region_0.1_spmd, %region_1.2_spmd} | conditional | flops 2292824 | bytes 18568518 | solution.py:961
  203.1 3.5 %collective-permute-done.1 = bf16[64,896]{1,0:T(8,128)(2,1)} collective-permute-done((bf16[64,896]{1,0:T(8,128)(2,1)}, bf16[64,896]{1,0:T(8,128)(2,1)}, u32[]{:S(2)}, u32[]{:S(2)}) %collective-permute-start.1) | collective-permute-done | bytes 114720 | tf_op jit(solution)/shard_map/cond/branch_1_fun/ppermute | solution.py:773
  208.7 2.1 collective-permute-start.3
  210.8 12.4 %collective-permute-done.3 = bf16[32,3200]{1,0:T(8,128)(2,1)S(1)} collective-permute-done((bf16[32,3200]{1,0:T(8,128)(2,1)S(1)}, bf16[32,3200]{1,0:T(8,128)(2,1)S(1)}, u32[]{:S(2)}, u32[]{:S(2)}) %collective-permute-start.3) | collective-permute-done | bytes 204832 | tf_op jit(solution)/shard_map/cond/branch_1_fun/ppermute | solution.py:789
  223.4 3.8 %collective-permute-start.6 = (bf16[8,3200]{1,0:T(8,128)(2,1)S(1)}, bf16[8,3200]{1,0:T(8,128)(2,1)S(1)}, u32[]{:S(2)}, u32[]{:S(2)}) collective-permute-start(bf16[8,3200]{1,0:T(8,128)(2,1)S(1)} %get-tuple-element.149), channel_id=1, source_target_pairs={{0,24},{2,26},{4,28},{6,30},{8,0},{10,2},{12,4},{14,6},{16,8},{18,... | collective-permute-start | bytes 153608 | tf_op jit(solution)/shard_map/cond/branch_1_fun/ppermute | solution.py:799
  227.8 4.9 %reorder.4.refs_1_ = bf16[16,256,256]{2,1,0:T(8,128)(2,1)} custom-call(s32[1]{0:T(128)} %get-tuple-element.34.where, s32[32]{0:T(128)S(1)} %get-tuple-element.35.assign, bf16[16,256,256]{2,1,0:T(8,128)(2,1)S(1)} %get-tuple-element.36.src, f32[32,3200]{1,0:T(8,128)} %copy-done), custom_call_target="tpu_custom_call" | custom-call | bytes 4194304 | tf_op jit(solution)/shard_map/cond/branch_1_fun/reorder/pallas_call | solution.py:672
  232.7 6.8 %collective-permute-done.4 = bf16[8,3200]{1,0:T(8,128)(2,1)S(1)} collective-permute-done((bf16[8,3200]{1,0:T(8,128)(2,1)S(1)}, bf16[8,3200]{1,0:T(8,128)(2,1)S(1)}, u32[]{:S(2)}, u32[]{:S(2)}) %collective-permute-start.4) | collective-permute-done | bytes 51232 | tf_op jit(solution)/shard_map/cond/branch_1_fun/ppermute | solution.py:799
  239.5 13.1 %collective-permute-done.5 = bf16[8,3200]{1,0:T(8,128)(2,1)S(1)} collective-permute-done((bf16[8,3200]{1,0:T(8,128)(2,1)S(1)}, bf16[8,3200]{1,0:T(8,128)(2,1)S(1)}, u32[]{:S(2)}, u32[]{:S(2)}) %collective-permute-start.5) | collective-permute-done | bytes 51232 | tf_op jit(solution)/shard_map/cond/branch_1_fun/ppermute | solution.py:799
  252.5 1.5 add_convert_fusion
  254.9 1.5 collective-permute-start.13
  257.0 2.3 collective-permute-done.13
  259.2 3.5 %collective-permute-done.12 = bf16[8,3200]{1,0:T(8,128)(2,1)S(1)} collective-permute-done((bf16[8,3200]{1,0:T(8,128)(2,1)}, bf16[8,3200]{1,0:T(8,128)(2,1)S(1)}, u32[]{:S(2)}, u32[]{:S(2)}) %collective-permute-start.12) | collective-permute-done | bytes 51232 | tf_op jit(solution)/shard_map/ppermute | solution.py:809
  263.6 1.5 collective-permute-start.14
  265.1 3.1 %reorder.7.refs_1_ = bf16[16,256,256]{2,1,0:T(8,128)(2,1)} custom-call(s32[1]{0:T(128)} %bitcast.4.where.shard, s32[32]{0:T(128)S(1)} %copy-done.10, bf16[16,256,256]{2,1,0:T(8,128)(2,1)} %all-to-all-done.3.src, bf16[4,8,3200]{2,1,0:T(8,128)(2,1)} %copy-done.2), custom_call_target="tpu_custom_call" | custom-call | bytes 4194304 | tf_op jit(solution)/shard_map/reorder/pallas_call | solution.py:672
  270.1 1.7 collective-permute-done.16.across_core
  272.4 6.7 %update.1 = (f32[128,768]{1,0:T(8,128)}, f32[128,256]{1,0:T(8,128)}, f32[128,1024]{1,0:T(8,128)}, f32[512,256]{1,0:T(8,128)}, f32[4,128]{1,0:T(4,128)}, /*index=...) custom-call(s32[1]{0:T(128)} %bitcast.12.where, bf16[4,8,3200]{2,1,0:T(8,128)(2,1)} %copy-done.2, ...), custom_call_target="tpu_custom_call" | custom-call | flops 10000000 | bytes 14000000 | tf_op jit(solution)/shard_map/update/pallas_call | solution.py:895
  (77 shorter events, 17.7 us)
Async XLA Ops:
  3.9 7.4 %copy-start.13 = (bf16[512]{0:T(512)(128)(2,1)S(1)}, bf16[512]{0:T(512)(128)(2,1)}, u32[]{:S(2)}) copy-start(bf16[512]{0:T(512)(128)(2,1)} %param.30) | copy-start | bytes 3076
  3.9 48.5 %all-to-all-start.1 = ((bf16[16,256,256]{2,1,0:T(8,128)(2,1)}), bf16[16,256,256]{2,1,0:T(8,128)(2,1)S(1)}, u32[]{:S(2)}, u32[]{:S(2)}) async-start(bf16[16,256,256]{2,1,0:T(8,128)(2,1)} %reorder.5.after), calls=%async_computation.1 | async-start | bytes 4194304 | tf_op jit(solution)/shard_map/all_to_all | solution.py:926
  11.3 4.3 %copy-start.10 = (s32[32]{0:T(128)S(1)}, s32[32]{0:T(128)}, u32[]{:S(2)}) copy-start(s32[32]{0:T(128)} %assign.5) | copy-start | bytes 388
  11.3 5.5 %copy-start.11 = (s32[1,4,64,3]{2,1,3,0:T(4,128)S(1)}, s32[1,4,64,3]{2,1,3,0:T(4,128)}, u32[]{:S(2)}) copy-start(s32[1,4,64,3]{2,1,3,0:T(4,128)} %param.25) | copy-start | bytes 9220
  11.3 7.1 %copy-start.12 = (s32[32]{0:T(128)S(1)}, s32[32]{0:T(128)}, u32[]{:S(2)}) copy-start(s32[32]{0:T(128)} %param.23) | copy-start | bytes 388
  14.1 22.2 %collective-permute-start.7 = (bf16[144,3072]{1,0:T(8,128)(2,1)}, bf16[144,3072]{1,0:T(8,128)(2,1)S(1)}, u32[]{:S(2)}, u32[]{:S(2)}) collective-permute-start(bf16[144,3072]{1,0:T(8,128)(2,1)} %pack_weights.1.own), channel_id=1, source_target_pairs={{0,1},{1,0},{2,3},{3,2},{4,5},{5,4},{6,7},{7,6},{8,9},{9,8},{10,11... | collective-permute-start | bytes 2654216 | tf_op jit(solution)/shard_map/ppermute | solution.py:931
  52.4 11.3 %copy-start.1 = (bf16[16,256,256]{2,1,0:T(8,128)(2,1)}, bf16[16,256,256]{2,1,0:T(8,128)(2,1)S(1)}, u32[]{:S(2)}) copy-start(bf16[16,256,256]{2,1,0:T(8,128)(2,1)S(1)} %all-to-all-done.1) | copy-start | bytes 6291460
  52.4 67.2 %all-to-all-start = ((bf16[16,256,256]{2,1,0:T(8,128)(2,1)}), bf16[16,256,256]{2,1,0:T(8,128)(2,1)}, u32[]{:S(2)}, u32[]{:S(2)}) async-start(bf16[16,256,256]{2,1,0:T(8,128)(2,1)} %reorder.6), calls=%async_computation | async-start | bytes 4194304 | tf_op jit(solution)/shard_map/all_to_all | solution.py:926
  119.7 73.4 %all-to-all-start.2 = ((bf16[16,256,256]{2,1,0:T(8,128)(2,1)}), bf16[16,256,256]{2,1,0:T(8,128)(2,1)S(1)}, u32[]{:S(2)}, u32[]{:S(2)}) async-start(bf16[16,256,256]{2,1,0:T(8,128)(2,1)} %bitcast.20), calls=%async_computation.2 | async-start | bytes 4194304 | tf_op jit(solution)/shard_map/all_to_all | solution.py:944
  147.4 45.6 %collective-permute-start.8 = (bf16[64,2432]{1,0:T(8,128)(2,1)}, bf16[64,2432]{1,0:T(8,128)(2,1)S(1)}, u32[]{:S(2)}, u32[]{:S(2)}) collective-permute-start(bf16[64,2432]{1,0:T(8,128)(2,1)} %get-tuple-element.114), channel_id=1, source_target_pairs={{0,2},{1,3},{2,0},{3,1},{4,6},{5,7},{6,4},{7,5},{8,10},{9,11},{10,... | collective-permute-start | bytes 933896 | tf_op jit(solution)/shard_map/ppermute | solution.py:773
  147.8 45.2 %collective-permute-start.9 = (bf16[64,2432]{1,0:T(8,128)(2,1)}, bf16[64,2432]{1,0:T(8,128)(2,1)S(1)}, u32[]{:S(2)}, u32[]{:S(2)}) collective-permute-start(bf16[64,2432]{1,0:T(8,128)(2,1)} %get-tuple-element.115), channel_id=1, source_target_pairs={{0,1},{1,0},{2,3},{3,2},{4,5},{5,4},{6,7},{7,6},{8,9},{9,8},{10,11... | collective-permute-start | bytes 933896 | tf_op jit(solution)/shard_map/ppermute | solution.py:773
  149.3 43.7 %collective-permute-start.10 = (bf16[64,2432]{1,0:T(8,128)(2,1)}, bf16[64,2432]{1,0:T(8,128)(2,1)S(1)}, u32[]{:S(2)}, u32[]{:S(2)}) collective-permute-start(bf16[64,2432]{1,0:T(8,128)(2,1)} %get-tuple-element.116), channel_id=1, source_target_pairs={{0,3},{1,2},{2,1},{3,0},{4,7},{5,6},{6,5},{7,4},{8,11},{9,10},{10,... | collective-permute-start | bytes 933896 | tf_op jit(solution)/shard_map/ppermute | solution.py:773
  193.1 72.0 %all-to-all-start.3 = ((bf16[16,256,256]{2,1,0:T(8,128)(2,1)}), bf16[16,256,256]{2,1,0:T(8,128)(2,1)}, u32[]{:S(2)}, u32[]{:S(2)}) async-start(bf16[16,256,256]{2,1,0:T(8,128)(2,1)} %bitcast.16), calls=%async_computation.3 | async-start | bytes 4194304 | tf_op jit(solution)/shard_map/all_to_all | solution.py:944
  199.8 2.0 copy-start.3
  199.8 2.0 copy-start.6
  199.8 3.2 %collective-permute-start = (bf16[64,896]{1,0:T(8,128)(2,1)}, bf16[64,896]{1,0:T(8,128)(2,1)}, u32[]{:S(2)}, u32[]{:S(2)}) collective-permute-start(bf16[64,896]{1,0:T(8,128)(2,1)} %get-tuple-element.30), channel_id=1, source_target_pairs={{0,2},{1,3},{2,0},{3,1},{4,6},{5,7},{6,4},{7,5},{8,10},{9,11},{10,... | collective-permute-start | bytes 344072 | tf_op jit(solution)/shard_map/cond/branch_1_fun/ppermute | solution.py:773
  200.2 6.3 %collective-permute-start.1 = (bf16[64,896]{1,0:T(8,128)(2,1)}, bf16[64,896]{1,0:T(8,128)(2,1)}, u32[]{:S(2)}, u32[]{:S(2)}) collective-permute-start(bf16[64,896]{1,0:T(8,128)(2,1)} %get-tuple-element.31), channel_id=1, source_target_pairs={{0,1},{1,0},{2,3},{3,2},{4,5},{5,4},{6,7},{7,6},{8,9},{9,8},{10,11... | collective-permute-start | bytes 344072 | tf_op jit(solution)/shard_map/cond/branch_1_fun/ppermute | solution.py:773
  201.7 5.7 %collective-permute-start.2 = (bf16[64,896]{1,0:T(8,128)(2,1)}, bf16[64,896]{1,0:T(8,128)(2,1)}, u32[]{:S(2)}, u32[]{:S(2)}) collective-permute-start(bf16[64,896]{1,0:T(8,128)(2,1)} %get-tuple-element.32), channel_id=1, source_target_pairs={{0,3},{1,2},{2,1},{3,0},{4,7},{5,6},{6,5},{7,4},{8,11},{9,10},{10,... | collective-permute-start | bytes 344072 | tf_op jit(solution)/shard_map/cond/branch_1_fun/ppermute | solution.py:773
  208.7 14.5 %collective-permute-start.3 = (bf16[32,3200]{1,0:T(8,128)(2,1)S(1)}, bf16[32,3200]{1,0:T(8,128)(2,1)S(1)}, u32[]{:S(2)}, u32[]{:S(2)}) collective-permute-start(bf16[32,3200]{1,0:T(8,128)(2,1)S(1)} %dynamic-slice_convert_fusion), channel_id=1, source_target_pairs={{0,4},{2,6},{4,0},{6,2},{8,12},{10,14},{12,8},{14,10},{16,20},{18,... | collective-permute-start | bytes 614408 | tf_op jit(solution)/shard_map/cond/branch_1_fun/ppermute | solution.py:789
  223.3 4.6 %copy-start = (f32[32,3200]{1,0:T(8,128)}, f32[32,3200]{1,0:T(8,128)S(1)}, u32[]{:S(2)}) copy-start(f32[32,3200]{1,0:T(8,128)S(1)} %convert_add_fusion.1.rest_0_) | copy-start | bytes 1228804 | tf_op jit(solution)/shard_map/cond
  223.3 16.2 %collective-permute-start.4 = (bf16[8,3200]{1,0:T(8,128)(2,1)S(1)}, bf16[8,3200]{1,0:T(8,128)(2,1)S(1)}, u32[]{:S(2)}, u32[]{:S(2)}) collective-permute-start(bf16[8,3200]{1,0:T(8,128)(2,1)S(1)} %get-tuple-element.148), channel_id=1, source_target_pairs={{0,8},{2,10},{4,12},{6,14},{8,16},{10,18},{12,20},{14,22},{16,24},... | collective-permute-start | bytes 153608 | tf_op jit(solution)/shard_map/cond/branch_1_fun/ppermute | solution.py:799
  223.4 16.1 %collective-permute-start.6 = (bf16[8,3200]{1,0:T(8,128)(2,1)S(1)}, bf16[8,3200]{1,0:T(8,128)(2,1)S(1)}, u32[]{:S(2)}, u32[]{:S(2)}) collective-permute-start(bf16[8,3200]{1,0:T(8,128)(2,1)S(1)} %get-tuple-element.149), channel_id=1, source_target_pairs={{0,24},{2,26},{4,28},{6,30},{8,0},{10,2},{12,4},{14,6},{16,8},{18,... | collective-permute-start | bytes 153608 | tf_op jit(solution)/shard_map/cond/branch_1_fun/ppermute | solution.py:799
  227.2 25.4 %collective-permute-start.5 = (bf16[8,3200]{1,0:T(8,128)(2,1)S(1)}, bf16[8,3200]{1,0:T(8,128)(2,1)S(1)}, u32[]{:S(2)}, u32[]{:S(2)}) collective-permute-start(bf16[8,3200]{1,0:T(8,128)(2,1)S(1)} %get-tuple-element.150), channel_id=1, source_target_pairs={{0,16},{2,18},{4,20},{6,22},{8,24},{10,26},{12,28},{14,30},{16,0},... | collective-permute-start | bytes 153608 | tf_op jit(solution)/shard_map/cond/branch_1_fun/ppermute | solution.py:799
  254.9 7.8 %copy-start.7 = (bf16[1,8,3200]{2,1,0:T(8,128)(2,1)}, bf16[1,8,3200]{2,1,0:T(8,128)(2,1)S(1)}, u32[]{:S(2)}) copy-start(bf16[1,8,3200]{2,1,0:T(8,128)(2,1)S(1)} %get-tuple-element.137) | copy-start | bytes 153604
  254.9 4.3 %collective-permute-start.13 = (bf16[8,3200]{1,0:T(8,128)(2,1)}, bf16[8,3200]{1,0:T(8,128)(2,1)S(1)}, u32[]{:S(2)}, u32[]{:S(2)}) collective-permute-start(bf16[8,3200]{1,0:T(8,128)(2,1)} %get-tuple-element.138), channel_id=1, source_target_pairs={{0,24},{2,26},{4,28},{6,30},{8,0},{10,2},{12,4},{14,6},{16,8},{18,... | collective-permute-start | bytes 153608 | tf_op jit(solution)/shard_map/ppermute | solution.py:809
  256.4 6.3 %collective-permute-start.12 = (bf16[8,3200]{1,0:T(8,128)(2,1)}, bf16[8,3200]{1,0:T(8,128)(2,1)S(1)}, u32[]{:S(2)}, u32[]{:S(2)}) collective-permute-start(bf16[8,3200]{1,0:T(8,128)(2,1)} %get-tuple-element.138), channel_id=1, source_target_pairs={{0,16},{2,18},{4,20},{6,22},{8,24},{10,26},{12,28},{14,30},{16,0},... | collective-permute-start | bytes 153608 | tf_op jit(solution)/shard_map/ppermute | solution.py:809
  256.4 6.3 %collective-permute-start.11 = (bf16[8,3200]{1,0:T(8,128)(2,1)}, bf16[8,3200]{1,0:T(8,128)(2,1)S(1)}, u32[]{:S(2)}, u32[]{:S(2)}) collective-permute-start(bf16[8,3200]{1,0:T(8,128)(2,1)} %get-tuple-element.138), channel_id=1, source_target_pairs={{0,8},{2,10},{4,12},{6,14},{8,16},{10,18},{12,20},{14,22},{16,24},... | collective-permute-start | bytes 153608 | tf_op jit(solution)/shard_map/ppermute | solution.py:809
  263.6 1.5 copy-start.2
  263.6 5.8 %collective-permute-start.14 = (bf16[4,8,3200]{2,1,0:T(8,128)(2,1)S(1)}, bf16[4,8,3200]{2,1,0:T(8,128)(2,1)S(1)}, u32[]{:S(2)}, u32[]{:S(2)}) collective-permute-start(bf16[4,8,3200]{2,1,0:T(8,128)(2,1)S(1)} %pad_maximum_fusion.1.rest_0_.near), channel_id=1, source_target_pairs={{0,4},{2,6},{4,0},{6,2},{8,12},{10,14},{12,8},{14,10},{16,20},{18,... | collective-permute-start | bytes 614408 | tf_op jit(solution)/shard_map/ppermute | solution.py:812
  265.1 5.0 %collective-permute-start.15 = (bf16[4,8,3200]{2,1,0:T(8,128)(2,1)S(1)}, bf16[4,8,3200]{2,1,0:T(8,128)(2,1)S(1)}, u32[]{:S(2)}, u32[]{:S(2)}) collective-permute-start(bf16[4,8,3200]{2,1,0:T(8,128)(2,1)S(1)} %pad_maximum_fusion.1.rest_0_.near), channel_id=1, source_target_pairs={{0,2},{2,0},{4,6},{6,4},{8,10},{10,8},{12,14},{14,12},{16,18},{18,... | collective-permute-start | bytes 614408 | tf_op jit(solution)/shard_map/ppermute | solution.py:813
  270.1 1.7 collective-permute-start.16
  270.1 1.7 copy-start.8
  (3 other events, 2.3 us)
